TPU v7x, 128 devices: a whole 4x4x4 slice. The times are simulated.
128 devices in a mesh: gx: 16 (over z, x), gy: 8 (over y, core).
Axes of the slice: x: 4, y: 4, z: 4, core: 2. Of those that a mesh axis runs over, the one named last changes fastest.
Arguments:
- state: float32 [40, 72, 16384], P(None, None, ('gx', 'gy')), may hold values from -6 to 6
- prev_tendency: bfloat16 [40, 72, 16384], P(None, None, ('gx', 'gy')), may hold values from -6 to 6
- wind: float32 [2, 72, 16384], P(None, None, ('gx', 'gy')), may hold values from -3 to 3
- edge_links: int32 [2, 4, 1024], P(None, None, ('gx', 'gy')), may hold values from 0 to 1023, as said below
- swap_slot: int32 [16384], P(('gx', 'gy')), may hold values from 0 to 16383, as said below
- inverse: float32 [1024, 72, 72], P(('gx', 'gy'))
Outputs:
- state_out: float32 [40, 72, 16384], P(None, None, ('gx', 'gy'))
- tendency: bfloat16 [40, 72, 16384], P(None, None, ('gx', 'gy'))
Inputs may be any that keep to these rules, and one draw needn't show every extreme that they name: `edge_links`: every neighbour lies within 2 elements of its element along the element order, taken cyclically, and that distance is reached; the second row holds edge numbers 0 to 3. `swap_slot`: A permutation of the columns. A column either keeps a slot of its own device (slots 128 d to 128 d + 127 for device d along gx+gy) or takes a slot of the device half of all devices away along gx+gy; two such partners hand each other equally many columns, at most 64, and some pair hands exactly 64.
All inputs are finite; a program needn't handle non-finite values.
Results may differ from a plain program's by a relative error of at most 0.0045.
Values may be sent and summed in bfloat16 or wider, within the bound.
No kernel may reach another device: no remote copies, remote signals or barrier semaphores. Data moves between devices by JAX's collectives and lax.ppermute only.
A program may use at most 128 MiB of HBM per device.

v0:
```python
import math

import jax
import jax.numpy as jnp
import numpy as np
from jax import lax
from jax.experimental import pallas as pl
from jax.experimental.pallas import tpu as pltpu
from jax.sharding import PartitionSpec as P

SUBSTEPS = 4
AXES = ("gx", "gy")
LANES = 128
PARTS = 4
VMEM = 16 * 1024 * 1024

time_step = 0.2
edge_points = ((0, 1, 2, 3), (3, 7, 11, 15), (15, 14, 13, 12), (12, 8, 4, 0))


def point_tables():
    edge_of = np.zeros((2, 16), np.int32)
    spot_of = np.zeros((2, 16), np.int32)
    weight_of = np.zeros((2, 16), np.float32)
    filled = np.zeros(16, np.int32)
    for k in range(4):
        for m in range(4):
            p = edge_points[k][m]
            s = filled[p]
            edge_of[s, p] = k
            spot_of[s, p] = m
            weight_of[s, p] = 1.0
            filled[p] = s + 1
    return (edge_of, spot_of, weight_of)


def gll_derivative():
    gll_nodes = np.array([-1.0, -1.0 / np.sqrt(5.0), 1.0 / np.sqrt(5.0), 1.0])
    factors = np.array(
        [np.prod([gll_nodes[i] - gll_nodes[k] for k in range(4) if k != i]) for i in range(4)]
    )
    derivative = np.zeros((4, 4))
    for i in range(4):
        for k in range(4):
            if i != k:
                derivative[i, k] = factors[i] / (factors[k] * (gll_nodes[i] - gll_nodes[k]))
            else:
                derivative[i, k] = sum(
                    (1.0 / (gll_nodes[i] - gll_nodes[j]) for j in range(4) if j != i)
                )
    return derivative


def derivative_matrix():
    derivative = gll_derivative()
    eye_block = np.eye(8)
    both = np.concatenate(
        [
            np.kron(eye_block, np.kron(derivative, np.eye(4)).T),
            np.kron(eye_block, np.kron(np.eye(4), derivative).T),
        ],
        axis=1,
    )
    high = both.astype(jnp.bfloat16)
    low = (both - high.astype(np.float64)).astype(jnp.bfloat16)
    return np.concatenate([high, low], axis=0)


def hermite(substep):
    instant = (substep + 1.0) / SUBSTEPS
    square = instant * instant
    cube = square * instant
    h00 = 2.0 * cube - 3.0 * square + 1.0
    h01 = -2.0 * cube + 3.0 * square
    slope = cube - 2.0 * square + instant + (cube - square)
    return (h00 - slope, h01 + slope)


def lane_ids(rows=1):
    return lax.broadcasted_iota(jnp.int32, (rows, LANES), 1)


def point_sets():
    point = lane_ids() % 16
    across = (point // 4 == 0) | (point // 4 == 3)
    along = (point % 4 == 0) | (point % 4 == 3)
    slots = (across | along, across & along)
    share = jnp.where(slots[1], 1.0 / 3.0, jnp.where(slots[0], 0.5, 1.0)).astype(jnp.float32)
    return slots, share


def edge_targets(links_ref, first_elem, element_count):
    edge_of, spot_of, _ = point_tables()
    elements = links_ref.shape[2]
    own = first_elem + lax.broadcasted_iota(jnp.int32, (4, elements), 1)
    apart = links_ref[0] - own
    half = element_count // 2
    apart = jnp.where(apart > half, apart - element_count, apart)
    apart = jnp.where(apart < -half, apart + element_count, apart) + 2
    both = jnp.concatenate([apart, links_ref[1]], axis=0).astype(jnp.float32)
    spread = lax.broadcasted_iota(jnp.int32, (elements, LANES), 0)
    spread = (spread == lax.broadcasted_iota(jnp.int32, (elements, LANES), 1) // 16).astype(jnp.float32)
    both = jnp.dot(both, spread, preferred_element_type=jnp.float32)
    both = (both + 0.5).astype(jnp.int32)
    lane = lane_ids()
    point = lane % 16
    rows = []
    for s in range(2):
        edge = jnp.zeros((1, LANES), jnp.int32)
        spot = edge
        for p in range(16):
            edge = jnp.where(point == p, int(edge_of[s, p]), edge)
            spot = jnp.where(point == p, int(spot_of[s, p]), spot)
        away, far = both[0:1], both[4:5]
        for k in range(1, 4):
            away = jnp.where(edge == k, both[k : k + 1], away)
            far = jnp.where(edge == k, both[4 + k : 5 + k], far)
        place = jnp.where(far == 2, 12 + spot, 4 * spot)
        place = jnp.where(far == 1, 15 - 4 * spot, place)
        place = jnp.where(far == 0, 3 - spot, place)
        rows.append(lane - point + 16 * away + place)
    rows = jnp.concatenate(rows + [jnp.zeros((6, LANES), jnp.int32)], axis=0)
    return rows.astype(jnp.float32)


def packed_halves(value, low):
    away = [pltpu.roll(value[k + 2], 64, 1) for k in range(2)]
    upper = [jnp.where(low, away[k], value[k]) for k in range(2)]
    lower = [jnp.where(low, value[k], away[k]) for k in range(2)]
    return upper, lower


def whole_halves(left, right, low):
    count, rows = left.shape[0], left.shape[1]
    direct = jnp.where(low, right, left).reshape(count * rows, LANES)
    turned = jnp.where(low, left, right).reshape(count * rows, LANES)
    return jnp.concatenate([direct, pltpu.roll(turned, 64, 1)], axis=0)


def pack_kernel(state_ref, prev_ref, wind_ref, links_ref, right_ref, left_ref, target_ref):
    step = pl.program_id(0)
    rows = state_ref.shape[1]
    at = pl.ds(pl.multiple_of(step * rows, 16), rows)
    low = lane_ids() < 64
    upper, lower = packed_halves([state_ref[k] for k in range(PARTS)], low)
    for k in range(2):
        right_ref[k, at] = upper[k].astype(jnp.bfloat16)
        left_ref[k, at] = lower[k].astype(jnp.bfloat16)
    quarter = lane_ids() // 32
    to_right = jnp.zeros((rows, LANES), jnp.float32)
    to_left = to_right
    for k in range(PARTS):
        turned = prev_ref[k].astype(jnp.float32)
        turned = pltpu.roll(turned, 32 * k, 1) if k else turned
        to_right = jnp.where(quarter == (3 + k) % 4, turned, to_right)
        to_left = jnp.where(quarter == k, turned, to_left)
    right_ref[2, at] = to_right.astype(jnp.bfloat16)
    left_ref[2, at] = to_left.astype(jnp.bfloat16)

    @pl.when(step == 0)
    def _():
        devices = lax.axis_size(AXES)
        elements = links_ref.shape[2]
        targets = edge_targets(links_ref, lax.axis_index(AXES) * elements, elements * devices)
        target_ref[...] = targets
        end = right_ref.shape[1]
        blank = jnp.zeros((24, LANES), jnp.float32)
        for k in range(3):
            piece = wind_ref[pl.ds(48 * k, 48), :]
            piece = jnp.concatenate([piece, targets, blank], axis=0).astype(jnp.bfloat16)
            right_ref[k, end - 80 : end] = piece
            left_ref[k, end - 80 : end] = piece


def chosen_products(matrices, state_ref, group, first, emit):
    lev = 72
    group = jnp.concatenate([group, group], axis=1)
    picks = [jnp.broadcast_to(group == first + c, (lev, 2 * LANES)) for c in range(8)]
    matrices = jnp.concatenate([matrices, matrices], axis=1)
    blank = jnp.zeros((LANES - lev, 2 * LANES), jnp.float32)
    for k in range(PARTS):
        pair = state_ref[k]
        pair = jnp.concatenate([pair[:lev], pair[lev:]], axis=1)
        high = pair.astype(jnp.bfloat16).astype(jnp.float32)
        column = jnp.concatenate([high, blank, pair - high, blank], axis=0).astype(jnp.bfloat16)
        product = jnp.dot(matrices, column, preferred_element_type=jnp.float32)
        chosen = jnp.zeros((lev, 2 * LANES), jnp.float32)
        for c in range(8):
            chosen = jnp.where(picks[c], product[c * lev : (c + 1) * lev], chosen)
        emit(k, jnp.concatenate([chosen[:, :LANES], chosen[:, LANES:]], axis=0))


def column_group(slot_ref):
    slot = slot_ref[...]
    return jnp.where(slot // LANES == lax.axis_index(AXES), 0, 8) + slot % LANES // 16


def moved(value, slope, blow_x, blow_y):
    rows, lev = value.shape[0], blow_x.shape[0]
    value = value.astype(jnp.bfloat16)
    both = jnp.dot(jnp.concatenate([value, value], axis=1), slope, preferred_element_type=jnp.float32)
    both = both.reshape(rows // lev, lev, 2 * LANES)
    motion = both[..., :LANES] * blow_x + both[..., LANES:] * blow_y
    return motion.reshape(rows, LANES).astype(jnp.bfloat16)


def sum_block(source, targets, slots, own):
    row = lax.broadcasted_iota(jnp.int32, (LANES, LANES), 0)
    total = jnp.zeros((LANES, LANES), jnp.float32)
    if own:
        total = (row == lax.broadcasted_iota(jnp.int32, (LANES, LANES), 1)).astype(jnp.float32)
    place = {
        "own": row,
        "near": jnp.where(row < 64, row + LANES, row - LANES),
        "outer": jnp.where(row < 64, row - LANES, row + LANES),
    }[source]
    for s in range(2):
        total = total + ((place == targets[s : s + 1]) & slots[s]).astype(jnp.float32)
    return total.astype(jnp.bfloat16)


def own_kernel(
    state_ref, prev_ref, wind_ref, target_ref, slope_ref, slot_ref, own_ref, part_ref, next_ref, sum_ref
):
    slots, share = point_sets()

    @pl.when(pl.program_id(0) == 0)
    def _():
        targets = target_ref[...].astype(jnp.int32) - 32
        sum_ref[...] = sum_block("own", targets, slots, True)

    def emit(k, chosen):
        part_ref[k] = chosen

    chosen_products(own_ref[...], state_ref, column_group(slot_ref), 0, emit)
    early = time_step * hermite(0)[0]
    pairs, rows = state_ref.shape[0], state_ref.shape[1]
    state = state_ref[...].reshape(pairs * rows, LANES)
    motion = moved(state, slope_ref[...], -time_step * wind_ref[0], -time_step * wind_ref[1])
    total = jnp.dot(motion, sum_ref[...], preferred_element_type=jnp.float32)
    ahead = state + total * share + early * prev_ref[...].astype(jnp.float32).reshape(state.shape)
    next_ref[...] = ahead.reshape(pairs, rows, LANES)


def far_kernel(
    state_ref, prev_ref, slot_ref, far_ref, part_ref, next_ref, tend_ref, ahead_ref, right_ref, left_ref
):
    group = column_group(slot_ref)
    here = group < 8
    quarter = lane_ids() // 32
    inner = (quarter == 1) | (quarter == 2)
    low = lane_ids() < 64
    late = time_step * hermite(0)[1]
    early_1, late_1 = (time_step * w for w in hermite(1))
    ahead, force = [], []

    def emit(k, chosen):
        tend = jnp.where(here, part_ref[k], chosen).astype(jnp.bfloat16)
        tend_ref[k] = tend
        tend = tend.astype(jnp.float32)
        ahead.append(next_ref[k] + late * tend)
        ahead_ref[k] = ahead[k]
        forced = early_1 * prev_ref[k].astype(jnp.float32) + late_1 * tend
        force.append(jnp.where(inner, forced, tend))

    chosen_products(far_ref[...], state_ref, group, 8, emit)
    upper, lower = packed_halves(force, low)
    for k in range(2):
        middle = jnp.where(inner, ahead[k], pltpu.roll(ahead[k + 2], 64, 1)).astype(jnp.bfloat16)
        right_ref[k] = middle
        left_ref[k] = middle
        right_ref[2 + k] = upper[k].astype(jnp.bfloat16)
        left_ref[2 + k] = lower[k].astype(jnp.bfloat16)


def near_kernel(
    state_ref,
    wind_ref,
    target_ref,
    slope_ref,
    left_ref,
    right_ref,
    left_extra_ref,
    right_extra_ref,
    add_ref,
    near_ref,
    force_ref,
    sum_ref,
    outer_sum_ref,
    blow_ref,
):
    lev = wind_ref.shape[1]
    slots, share = point_sets()
    low = lane_ids() < 64

    @pl.when(pl.program_id(0) == 0)
    def _():
        def winds(ref):
            whole = jnp.concatenate([ref[k].astype(jnp.float32)[:48] for k in range(3)], axis=0)
            return whole[:lev], whole[lev:]

        def targets(ref):
            return ref[0].astype(jnp.float32)[48:56].astype(jnp.int32) - 32

        own_t = target_ref[...].astype(jnp.int32) - 32
        left_t, right_t = targets(left_extra_ref) - LANES, targets(right_extra_ref) + LANES
        near_t = jnp.where(low, right_t, left_t)
        sum_ref[:LANES, :LANES] = sum_block("own", own_t, slots, True)
        sum_ref[LANES:, :LANES] = sum_block("near", own_t, slots, False)
        sum_ref[:LANES, LANES:] = sum_block("own", near_t, slots, False)
        sum_ref[LANES:, LANES:] = sum_block("near", near_t, slots, True)
        outer_sum_ref[...] = sum_block("outer", near_t, slots, False)
        left_w, right_w = winds(left_extra_ref), winds(right_extra_ref)
        for d in range(2):
            blow_ref[0, d] = -time_step * wind_ref[d]
            blow_ref[1, d] = -time_step * jnp.where(low, right_w[d], left_w[d])
            blow_ref[2, d] = -time_step * jnp.where(low, left_w[d], right_w[d])

    pairs, rows = state_ref.shape[0], state_ref.shape[1]
    slope = slope_ref[...]
    own = state_ref[...].reshape(pairs * rows, LANES)
    left, right = left_ref[...].astype(jnp.float32), right_ref[...].astype(jnp.float32)
    near = whole_halves(left[:2], right[:2], low)
    own_move = moved(own, slope, blow_ref[0, 0], blow_ref[0, 1])
    near_move = moved(near, slope, blow_ref[1, 0], blow_ref[1, 1])
    total = jnp.dot(near_move, sum_ref[LANES:], preferred_element_type=jnp.float32)
    near_total = total[:, LANES:] + jnp.dot(
        own_move, sum_ref[:LANES, LANES:], preferred_element_type=jnp.float32
    )
    add_ref[...] = (total[:, :LANES] * share).reshape(pairs, rows, LANES)
    prev = jnp.concatenate(
        [
            jnp.where(low, right[2], left[2])
            if k == 0
            else jnp.where(
                low, pltpu.roll(right[2], LANES - 32 * k, 1), pltpu.roll(left[2], LANES - 32 * k, 1)
            )
            for k in range(PARTS)
        ],
        axis=0,
    )
    early = time_step * hermite(0)[0]
    near_ref[...] = (near + near_total * share + early * prev).reshape(pairs, rows, LANES)
    force_ref[...] = prev.astype(jnp.bfloat16).reshape(pairs, rows, LANES)


def advance_kernel(
    ahead_ref,
    add_ref,
    near_ref,
    near_prev_ref,
    prev_ref,
    tend_ref,
    left_ref,
    right_ref,
    slope_ref,
    sum_ref,
    outer_sum_ref,
    blow_ref,
    out_ref,
):
    pairs, pair = ahead_ref.shape[0], ahead_ref.shape[1]
    rows = pairs * pair
    _, share = point_sets()
    quarter = lane_ids() // 32
    inner = (quarter == 1) | (quarter == 2)
    low = lane_ids() < 64
    slope, sums = slope_ref[...], sum_ref[...]
    weights = [tuple(time_step * w for w in hermite(s)) for s in range(SUBSTEPS)]

    def flat(ref):
        return ref[...].astype(jnp.float32).reshape(rows, LANES)

    def advect(value, unit):
        return moved(value, slope, blow_ref[unit, 0], blow_ref[unit, 1])

    def gather(pieces, matrix):
        return jnp.dot(jnp.concatenate(pieces, axis=1), matrix, preferred_element_type=jnp.float32)

    left, right = left_ref[...].astype(jnp.float32), right_ref[...].astype(jnp.float32)

    def middle(value):
        value = value.reshape(2 * pair, LANES)
        return jnp.concatenate([value, pltpu.roll(value, 64, 1)], axis=0)

    left_mid, right_mid = middle(left[:2]), middle(right[:2])
    received = whole_halves(left[2:], right[2:], low)
    own_prev, own_tend, near_prev = flat(prev_ref), flat(tend_ref), flat(near_prev_ref)
    own = flat(ahead_ref) + flat(add_ref)
    near = flat(near_ref) + weights[0][1] * received
    near = jnp.where(inner, jnp.where(low, right_mid, left_mid), near)
    outer = jnp.where(low, left_mid, right_mid)
    for s in range(1, SUBSTEPS):
        early, late = weights[s]
        own_force = early * own_prev + late * own_tend
        own_move, near_move = advect(own, 0), advect(near, 1)
        if s == SUBSTEPS - 1:
            total = gather([own_move, near_move], sums[:, :LANES])
            out_ref[...] = (own + total * share + own_force).reshape(pairs, pair, LANES)
            break
        near_force = early * near_prev + late * received
        total = gather([own_move, near_move], sums)
        own = own + total[:, :LANES] * share + own_force
        near_total = total[:, LANES:]
        if s == 1:
            near_force = jnp.where(inner, received, near_force)
            near_total = near_total + jnp.dot(
                advect(outer, 2), outer_sum_ref[...], preferred_element_type=jnp.float32
            )
        near = near + near_total * share + near_force


def shifted(value, by):
    count = lax.axis_size(AXES)
    return lax.ppermute(value, AXES, [(i, (i + by) % count) for i in range(count)])


def per_device(state, prev_tendency, wind, edge_links, swap_slot, inverse):
    devices = lax.axis_size(AXES)
    shape = state.shape
    lev = shape[1]
    pair = 2 * lev
    rows = shape[0] * lev // PARTS
    steps = rows // pair
    params = pltpu.CompilerParams(vmem_limit_bytes=VMEM)
    bf16, f32 = jnp.bfloat16, jnp.float32

    def like(count, kind, length=rows):
        return jax.ShapeDtypeStruct((count, length, LANES), kind)

    def chunk(count):
        return pl.BlockSpec((count, pair, LANES), lambda j: (0, j, 0))

    def whole(array):
        return pl.BlockSpec(array.shape, lambda j, n=len(array.shape): (0,) * n)

    def call(body, ins, outs, name, passes):
        size = sum(math.prod(array.shape) * array.dtype.itemsize for array, _ in ins)
        cost = pl.CostEstimate(
            flops=passes * 2 * PARTS * rows * 256 * 256, bytes_accessed=2 * size, transcendentals=0
        )
        return pl.pallas_call(
            body,
            grid=(steps,),
            in_specs=[spec for _, spec in ins],
            out_specs=tuple(spec for _, spec in outs),
            out_shape=tuple(kind for kind, _ in outs),
            compiler_params=params,
            cost_estimate=cost,
            name=name,
        )(*[array for array, _ in ins])

    matrices = (inverse - jnp.eye(lev, dtype=f32)).astype(bf16)
    matrices = jnp.pad(matrices, ((0, 0), (0, 0), (0, LANES - lev))).reshape(-1, LANES)
    far_matrices = lax.ppermute(matrices, AXES, [(i, i ^ (devices // 2)) for i in range(devices)])

    state4 = state.reshape(PARTS, rows, LANES)
    prev4 = prev_tendency.reshape(PARTS, rows, LANES)
    slot = swap_slot.reshape(1, LANES)
    flat_wind = wind.reshape(pair, LANES)
    slope = jnp.asarray(derivative_matrix())
    message = like(3, bf16, rows + 80)
    target_kind = jax.ShapeDtypeStruct((8, LANES), f32)
    to_right, to_left, targets = call(
        pack_kernel,
        [(state4, chunk(4)), (prev4, chunk(4)), (flat_wind, whole(flat_wind)), (edge_links, whole(edge_links))],
        [(message, whole(message)), (message, whole(message)), (target_kind, whole(target_kind))],
        "pack",
        2,
    )
    from_left, from_right = shifted(to_right, 1), shifted(to_left, -1)

    sum_kind = jax.ShapeDtypeStruct((LANES, LANES), bf16)
    part, ahead, _ = call(
        own_kernel,
        [
            (state4, chunk(4)),
            (prev4, chunk(4)),
            (wind, whole(wind)),
            (targets, whole(targets)),
            (slope, whole(slope)),
            (slot, whole(slot)),
            (matrices, whole(matrices)),
        ],
        [(like(4, f32), chunk(4)), (like(4, f32), chunk(4)), (sum_kind, whole(sum_kind))],
        "own",
        10,
    )
    tend4, ahead, mid_right, mid_left = call(
        far_kernel,
        [
            (state4, chunk(4)),
            (prev4, chunk(4)),
            (slot, whole(slot)),
            (far_matrices, whole(far_matrices)),
            (part, chunk(4)),
            (ahead, chunk(4)),
        ],
        [(like(4, bf16), chunk(4)), (like(4, f32), chunk(4)), (like(4, bf16), chunk(4)), (like(4, bf16), chunk(4))],
        "far",
        10,
    )
    mid_from_left, mid_from_right = shifted(mid_right, 1), shifted(mid_left, -1)

    extra = pl.BlockSpec((3, 80, LANES), lambda j: (0, rows // 80, 0))
    both_kind = jax.ShapeDtypeStruct((2 * LANES, 2 * LANES), bf16)
    blow_kind = jax.ShapeDtypeStruct((3, 2, lev, LANES), f32)
    add, near, near_prev, sums, outer_sums, blow = call(
        near_kernel,
        [
            (state4, chunk(4)),
            (wind, whole(wind)),
            (targets, whole(targets)),
            (slope, whole(slope)),
            (from_left, chunk(3)),
            (from_right, chunk(3)),
            (from_left, extra),
            (from_right, extra),
        ],
        [
            (like(4, f32), chunk(4)),
            (like(4, f32), chunk(4)),
            (like(4, bf16), chunk(4)),
            (both_kind, whole(both_kind)),
            (sum_kind, whole(sum_kind)),
            (blow_kind, whole(blow_kind)),
        ],
        "near",
        8,
    )
    (out4,) = call(
        advance_kernel,
        [
            (ahead, chunk(4)),
            (add, chunk(4)),
            (near, chunk(4)),
            (near_prev, chunk(4)),
            (prev4, chunk(4)),
            (tend4, chunk(4)),
            (mid_from_left, chunk(4)),
            (mid_from_right, chunk(4)),
            (slope, whole(slope)),
            (sums, whole(sums)),
            (outer_sums, whole(outer_sums)),
            (blow, whole(blow)),
        ],
        [(like(4, f32), chunk(4))],
        "advance",
        24,
    )
    return (out4.reshape(shape), tend4.reshape(shape))


def solution(mesh):
    columns = P(None, None, AXES)
    return jax.shard_map(
        per_device,
        mesh=mesh,
        in_specs=(columns, columns, columns, columns, P(AXES), P(AXES, None, None)),
        out_specs=(columns, columns),
        check_vma=False,
    )
```

profile of v0, /device:TPU:0, one launch (start us, length us, event | category | flops | bytes accessed | tf_op | source)
XLA Modules:
  0.0 50.9 jit_solution(7850236516745701942)
XLA Ops:
  0.6 1.0 %subtract_convert_fusion = bf16[8,72,72]{2,1,0:T(8,128)(2,1)S(1)} fusion(f32[8,72,72]{2,1,0:T(8,128)} %param.12, f32[72,72]{1,0:T(8,128)S(1)} %fusion), kind=kLoop, calls=%fused_computation | loop fusion | flops 82944 | bytes 269568 | tf_op jit(solution)/shard_map/convert_element_type | solution.py:453
  1.6 0.0 copy-start.8
  1.7 0.0 copy-start.6
  1.7 4.0 %collective-permute-start = (bf16[576,128]{1,0:T(8,128)(2,1)S(1)}, bf16[576,128]{1,0:T(8,128)(2,1)S(1)}, u32[]{:S(2)}, u32[]{:S(2)}) collective-permute-start(bf16[576,128]{1,0:T(8,128)(2,1)S(1)} %bitcast.7), channel_id=1, source_target_pairs={{0,64},{1,65},{2,66},{3,67},{4,68},{5,69},{6,70},{7,71},{8,72},{9,... | collective-permute-start | bytes 442376 | tf_op jit(solution)/shard_map/ppermute | solution.py:455
  5.7 0.0 copy-start
  5.7 1.4 %copy-done = f32[40,72,128]{2,1,0:T(8,128)S(1)} copy-done((f32[40,72,128]{2,1,0:T(8,128)S(1)}, f32[40,72,128]{2,1,0:T(8,128)}, u32[]{:S(2)}) %copy-start) | copy-done | bytes 1474584
  7.1 0.0 copy-start.1
  7.1 1.1 %copy-done.1 = bf16[40,72,128]{2,1,0:T(8,128)(2,1)S(1)} copy-done((bf16[40,72,128]{2,1,0:T(8,128)(2,1)S(1)}, bf16[40,72,128]{2,1,0:T(8,128)(2,1)}, u32[]{:S(2)}) %copy-start.1) | copy-done | bytes 737304
  8.2 0.0 copy-start.3
  8.2 0.9 %copy-done.3 = f32[2,72,128]{2,1,0:T(8,128)S(1)} copy-done((f32[2,72,128]{2,1,0:T(8,128)S(1)}, f32[2,72,128]{2,1,0:T(8,128)}, u32[]{:S(2)}) %copy-start.3) | copy-done | bytes 73752
  9.1 0.0 copy-start.5
  9.1 0.7 %copy-done.5 = s32[2,4,8]{2,1,0:T(4,128)S(1)} copy-done((s32[2,4,8]{2,1,0:T(4,128)S(1)}, s32[2,4,8]{2,1,0:T(4,128)}, u32[]{:S(2)}) %copy-start.5) | copy-done | bytes 280
  9.8 1.0 %pack.1 = (bf16[3,800,128]{2,1,0:T(8,128)(2,1)S(1)}, bf16[3,800,128]{2,1,0:T(8,128)(2,1)S(1)}, f32[8,128]{1,0:T(8,128)S(1)}) custom-call(f32[4,720,128]{2,1,0:T(8,128)S(1)} %bitcast.9, bf16[4,720,128]{2,1,0:T(8,128)(2,1)S(1)} %bitcast.13, f32[144,128]{1,0:T(8,128)S(1)} %bitcast.17, s32[2,4,8]{2,1,0:T(4,128)S(1)} %copy-done.5), custom_call_target="tpu_custom_call" | custom-call | flops 754974720 | bytes 4571648 | tf_op jit(solution)/shard_map/pack/pallas_call | solution.py:442
  10.8 0.1 collective-permute-start.1
  10.9 7.2 %collective-permute-start.2 = (bf16[3,800,128]{2,1,0:T(8,128)(2,1)S(1)}, bf16[3,800,128]{2,1,0:T(8,128)(2,1)S(1)}, u32[]{:S(2)}, u32[]{:S(2)}) collective-permute-start(bf16[3,800,128]{2,1,0:T(8,128)(2,1)S(1)} %get-tuple-element.22), channel_id=1, source_target_pairs={{0,127},{1,0},{2,1},{3,2},{4,3},{5,4},{6,5},{7,6},{8,7},{9,8},{10,... | collective-permute-start | bytes 1843208 | tf_op jit(solution)/shard_map/ppermute | solution.py:415
  18.0 0.0 copy-done.8
  18.0 0.0 copy-done.6
  18.0 4.5 %own.1 = (f32[4,720,128]{2,1,0:T(8,128)S(1)}, f32[4,720,128]{2,1,0:T(8,128)S(1)}, bf16[128,128]{1,0:T(8,128)(2,1)}) custom-call(f32[4,720,128]{2,1,0:T(8,128)S(1)} %bitcast.10, bf16[4,720,128]{2,1,0:T(8,128)(2,1)S(1)} %bitcast.14, f32[2,72,128]{2,1,0:T(8,128)S(1)} %copy-done.3, f32[8,128]{1,0:T(8,128)S(1)} %get-tuple-element.17.target_ref, ...), custom_call_target="tpu_custom_call" | custom-call | flops 3774873600 | bytes 5137408 | tf_op jit(solution)/shard_map/own/pallas_call | solution.py:442
  22.6 0.0 collective-permute-done.far_ref
  22.6 0.0 copy-start.4
  22.6 4.3 %far.1 = (bf16[4,720,128]{2,1,0:T(8,128)(2,1)}, f32[4,720,128]{2,1,0:T(8,128)S(1)}, bf16[4,720,128]{2,1,0:T(8,128)(2,1)S(1)}, bf16[4,720,128]{2,1,0:T(8,128)(2,1)S(1)}) custom-call(f32[4,720,128]{2,1,0:T(8,128)S(1)} %bitcast.11, bf16[4,720,128]{2,1,0:T(8,128)(2,1)S(1)} %bitcast.15, s32[1,128]{1,0:T(1,128)S(1)} %bitcast.19, ...), custom_call_target="tpu_custom_call" | custom-call | flops 3774873600 | bytes 10617856 | tf_op jit(solution)/shard_map/far/pallas_call | solution.py:442
  26.9 0.0 collective-permute-start.3
  26.9 0.0 copy-start.2
  26.9 0.0 copy-start.7
  26.9 7.2 %collective-permute-start.4 = (bf16[4,720,128]{2,1,0:T(8,128)(2,1)S(1)}, bf16[4,720,128]{2,1,0:T(8,128)(2,1)S(1)}, u32[]{:S(2)}, u32[]{:S(2)}) collective-permute-start(bf16[4,720,128]{2,1,0:T(8,128)(2,1)S(1)} %get-tuple-element.28), channel_id=1, source_target_pairs={{0,127},{1,0},{2,1},{3,2},{4,3},{5,4},{6,5},{7,6},{8,7},{9,8},{10,... | collective-permute-start | bytes 2211848 | tf_op jit(solution)/shard_map/ppermute | solution.py:415
  34.1 0.0 collective-permute-done.1.left_ref.left_extra_ref
  34.1 0.0 collective-permute-done.2.right_ref.right_extra_ref
  34.1 0.0 copy-done.4
  34.1 3.5 %near.1 = (f32[4,720,128]{2,1,0:T(8,128)S(1)}, f32[4,720,128]{2,1,0:T(8,128)S(1)}, bf16[4,720,128]{2,1,0:T(8,128)(2,1)S(1)}, bf16[256,256]{1,0:T(8,128)(2,1)S(1)...) custom-call(f32[4,720,128]{2,1,0:T(8,128)S(1)} %bitcast.12, f32[2,72,128]{2,1,0:T(8,128)S(1)} %copy-done.4, ...), custom_call_target="tpu_custom_call" | custom-call | flops 3019898880 | bytes 8282112 | tf_op jit(solution)/shard_map/near/pallas_call | solution.py:442
  37.6 5.6 %collective-permute-done.3.left_ref = bf16[4,720,128]{2,1,0:T(8,128)(2,1)S(1)} collective-permute-done((bf16[4,720,128]{2,1,0:T(8,128)(2,1)S(1)}, bf16[4,720,128]{2,1,0:T(8,128)(2,1)S(1)}, u32[]{:S(2)}, u32[]{:S(2)}) %collective-permute-start.3) | collective-permute-done | bytes 737312 | tf_op jit(solution)/shard_map/ppermute | solution.py:415
  43.2 0.0 collective-permute-done.4.right_ref
  43.2 0.0 copy-done.2
  43.2 0.0 copy-done.7
  43.2 7.6 %advance.1 = f32[4,720,128]{2,1,0:T(8,128)} custom-call(f32[4,720,128]{2,1,0:T(8,128)S(1)} %get-tuple-element.20.ahead_ref, f32[4,720,128]{2,1,0:T(8,128)S(1)} %get-tuple-element.23.add_ref, f32[4,720,128]{2,1,0:T(8,128)S(1)} %get-tuple-element.24.near_ref, bf16[4,720,128]{2,1,0:T(8,128)(2,1)S(1)} %get-tuple-element.25.near_prev_ref, ...), custom_call_target="tpu_custom_call" | custom-call | flops 9059696640 | bytes 17252352 | tf_op jit(solution)/shard_map/advance/pallas_call | solution.py:442
  (2 shorter events, 0.0 us)
Async XLA Ops:
  1.6 16.4 %copy-start.8 = (bf16[256,256]{1,0:T(8,128)(2,1)S(1)}, bf16[256,256]{1,0:T(8,128)(2,1)}, u32[]{:S(2)}) copy-start(bf16[256,256]{1,0:T(8,128)(2,1)} %constant.5.clone.slope_ref) | copy-start | bytes 393220
  1.7 16.3 %copy-start.6 = (s32[128]{0:T(128)S(1)}, s32[128]{0:T(128)}, u32[]{:S(2)}) copy-start(s32[128]{0:T(128)} %param.11) | copy-start | bytes 1540
  1.7 20.9 %collective-permute-start = (bf16[576,128]{1,0:T(8,128)(2,1)S(1)}, bf16[576,128]{1,0:T(8,128)(2,1)S(1)}, u32[]{:S(2)}, u32[]{:S(2)}) collective-permute-start(bf16[576,128]{1,0:T(8,128)(2,1)S(1)} %bitcast.7), channel_id=1, source_target_pairs={{0,64},{1,65},{2,66},{3,67},{4,68},{5,69},{6,70},{7,71},{8,72},{9,... | collective-permute-start | bytes 442376 | tf_op jit(solution)/shard_map/ppermute | solution.py:455
  5.7 1.4 %copy-start = (f32[40,72,128]{2,1,0:T(8,128)S(1)}, f32[40,72,128]{2,1,0:T(8,128)}, u32[]{:S(2)}) copy-start(f32[40,72,128]{2,1,0:T(8,128)} %param.7) | copy-start | bytes 4423684
  7.1 1.1 %copy-start.1 = (bf16[40,72,128]{2,1,0:T(8,128)(2,1)S(1)}, bf16[40,72,128]{2,1,0:T(8,128)(2,1)}, u32[]{:S(2)}) copy-start(bf16[40,72,128]{2,1,0:T(8,128)(2,1)} %param.8) | copy-start | bytes 2211844
  8.2 0.9 %copy-start.3 = (f32[2,72,128]{2,1,0:T(8,128)S(1)}, f32[2,72,128]{2,1,0:T(8,128)}, u32[]{:S(2)}) copy-start(f32[2,72,128]{2,1,0:T(8,128)} %wind_ref.3) | copy-start | bytes 221188
  9.1 0.7 %copy-start.5 = (s32[2,4,8]{2,1,0:T(4,128)S(1)}, s32[2,4,8]{2,1,0:T(4,128)}, u32[]{:S(2)}) copy-start(s32[2,4,8]{2,1,0:T(4,128)} %links_ref.1) | copy-start | bytes 772
  10.8 23.3 %collective-permute-start.1 = (bf16[3,800,128]{2,1,0:T(8,128)(2,1)S(1)}, bf16[3,800,128]{2,1,0:T(8,128)(2,1)S(1)}, u32[]{:S(2)}, u32[]{:S(2)}) collective-permute-start(bf16[3,800,128]{2,1,0:T(8,128)(2,1)S(1)} %get-tuple-element.21), channel_id=1, source_target_pairs={{0,1},{1,2},{2,3},{3,4},{4,5},{5,6},{6,7},{7,8},{8,9},{9,10},{10,1... | collective-permute-start | bytes 1843208 | tf_op jit(solution)/shard_map/ppermute | solution.py:415
  10.9 23.2 %collective-permute-start.2 = (bf16[3,800,128]{2,1,0:T(8,128)(2,1)S(1)}, bf16[3,800,128]{2,1,0:T(8,128)(2,1)S(1)}, u32[]{:S(2)}, u32[]{:S(2)}) collective-permute-start(bf16[3,800,128]{2,1,0:T(8,128)(2,1)S(1)} %get-tuple-element.22), channel_id=1, source_target_pairs={{0,127},{1,0},{2,1},{3,2},{4,3},{5,4},{6,5},{7,6},{8,7},{9,8},{10,... | collective-permute-start | bytes 1843208 | tf_op jit(solution)/shard_map/ppermute | solution.py:415
  22.6 11.5 %copy-start.4 = (f32[2,72,128]{2,1,0:T(8,128)S(1)}, f32[2,72,128]{2,1,0:T(8,128)}, u32[]{:S(2)}) copy-start(f32[2,72,128]{2,1,0:T(8,128)} %wind_ref.3) | copy-start | bytes 221188
  26.9 16.3 %collective-permute-start.3 = (bf16[4,720,128]{2,1,0:T(8,128)(2,1)S(1)}, bf16[4,720,128]{2,1,0:T(8,128)(2,1)S(1)}, u32[]{:S(2)}, u32[]{:S(2)}) collective-permute-start(bf16[4,720,128]{2,1,0:T(8,128)(2,1)S(1)} %get-tuple-element.27), channel_id=1, source_target_pairs={{0,1},{1,2},{2,3},{3,4},{4,5},{5,6},{6,7},{7,8},{8,9},{9,10},{10,1... | collective-permute-start | bytes 2211848 | tf_op jit(solution)/shard_map/ppermute | solution.py:415
  26.9 16.3 %copy-start.2 = (bf16[40,72,128]{2,1,0:T(8,128)(2,1)S(1)}, bf16[40,72,128]{2,1,0:T(8,128)(2,1)}, u32[]{:S(2)}) copy-start(bf16[40,72,128]{2,1,0:T(8,128)(2,1)} %param.8) | copy-start | bytes 2211844
  26.9 16.3 %copy-start.7 = (bf16[4,720,128]{2,1,0:T(8,128)(2,1)S(1)}, bf16[4,720,128]{2,1,0:T(8,128)(2,1)}, u32[]{:S(2)}) copy-start(bf16[4,720,128]{2,1,0:T(8,128)(2,1)} %get-tuple-element.26.tend_ref) | copy-start | bytes 2211844
  26.9 16.3 %collective-permute-start.4 = (bf16[4,720,128]{2,1,0:T(8,128)(2,1)S(1)}, bf16[4,720,128]{2,1,0:T(8,128)(2,1)S(1)}, u32[]{:S(2)}, u32[]{:S(2)}) collective-permute-start(bf16[4,720,128]{2,1,0:T(8,128)(2,1)S(1)} %get-tuple-element.28), channel_id=1, source_target_pairs={{0,127},{1,0},{2,1},{3,2},{4,3},{5,4},{6,5},{7,6},{8,7},{9,8},{10,... | collective-permute-start | bytes 2211848 | tf_op jit(solution)/shard_map/ppermute | solution.py:415
where the time goes:
time: 51.1 us; the launch traced here: 50.9 us
  Pallas kernels  21 us (41%)
  starting transfers between devices  18.5 us (36%)
  waiting for transfers between devices  5.61 us (11%)
  local copies, waits for them, and re-layouts  4.12 us (8%)
  other arithmetic  1 us (2%)
  between operations  0.71 us (1%)
    pallas_call x5, Pallas kernels, call(): pl.pallas_call(body, grid=(steps,), in_specs=[spec for _, spec in ins], o...  21 us
    ppermute x4, starting transfers between devices, shifted(): lax.ppermute(value, AXES, [(i, (i + by) % count) for i in range(count)])  14.4 us
    ppermute x4, waiting for transfers between devices, shifted(): lax.ppermute(value, AXES, [(i, (i + by) % count) for i in range(count)])  5.61 us
    unnamed x18, local copies, waits for them, and re-layouts  4.08 us
    ppermute x1, starting transfers between devices, per_device(): lax.ppermute(matrices, AXES, [(i, i ^ devices // 2) for i in range(device...  4.04 us
  transfers between devices with their start and end apart: 5, of which 1 were waited for; matrix products, arithmetic and copies ran while one was open for 0% of the time, Pallas kernels for 26%

commit v1 on v0

v1 whole, which is shorter than its diff:
```python
import math

import jax
import jax.numpy as jnp
import numpy as np
from jax import lax
from jax.experimental import pallas as pl
from jax.experimental.pallas import tpu as pltpu
from jax.sharding import PartitionSpec as P

SUBSTEPS = 4
AXES = ("gx", "gy")
LANES = 128
CHUNK = 144
PARTS = 4
VMEM = 16 * 1024 * 1024

time_step = 0.2
edge_points = ((0, 1, 2, 3), (3, 7, 11, 15), (15, 14, 13, 12), (12, 8, 4, 0))


def point_tables():
    edge_of = np.zeros((2, 16), np.int32)
    spot_of = np.zeros((2, 16), np.int32)
    weight_of = np.zeros((2, 16), np.float32)
    filled = np.zeros(16, np.int32)
    for k in range(4):
        for m in range(4):
            p = edge_points[k][m]
            s = filled[p]
            edge_of[s, p] = k
            spot_of[s, p] = m
            weight_of[s, p] = 1.0
            filled[p] = s + 1
    return (edge_of, spot_of, weight_of)


def gll_derivative():
    gll_nodes = np.array([-1.0, -1.0 / np.sqrt(5.0), 1.0 / np.sqrt(5.0), 1.0])
    factors = np.array(
        [np.prod([gll_nodes[i] - gll_nodes[k] for k in range(4) if k != i]) for i in range(4)]
    )
    derivative = np.zeros((4, 4))
    for i in range(4):
        for k in range(4):
            if i != k:
                derivative[i, k] = factors[i] / (factors[k] * (gll_nodes[i] - gll_nodes[k]))
            else:
                derivative[i, k] = sum(
                    (1.0 / (gll_nodes[i] - gll_nodes[j]) for j in range(4) if j != i)
                )
    return derivative


def derivative_matrix():
    derivative = gll_derivative()
    eye_block = np.eye(8)
    both = np.concatenate(
        [
            np.kron(eye_block, np.kron(derivative, np.eye(4)).T),
            np.kron(eye_block, np.kron(np.eye(4), derivative).T),
        ],
        axis=1,
    )
    high = both.astype(jnp.bfloat16)
    low = (both - high.astype(np.float64)).astype(jnp.bfloat16)
    return np.concatenate([high, low], axis=0)


def hermite(substep):
    instant = (substep + 1.0) / SUBSTEPS
    square = instant * instant
    cube = square * instant
    h00 = 2.0 * cube - 3.0 * square + 1.0
    h01 = -2.0 * cube + 3.0 * square
    slope = cube - 2.0 * square + instant + (cube - square)
    return (h00 - slope, h01 + slope)


def lane_ids(rows=1):
    return lax.broadcasted_iota(jnp.int32, (rows, LANES), 1)


def point_sets():
    point = lane_ids() % 16
    across = (point // 4 == 0) | (point // 4 == 3)
    along = (point % 4 == 0) | (point % 4 == 3)
    slots = (across | along, across & along)
    share = jnp.where(slots[1], 1.0 / 3.0, jnp.where(slots[0], 0.5, 1.0)).astype(jnp.float32)
    return slots, share


def edge_targets(links_ref, first_elem, element_count):
    edge_of, spot_of, _ = point_tables()
    elements = links_ref.shape[2]
    own = first_elem + lax.broadcasted_iota(jnp.int32, (4, elements), 1)
    apart = links_ref[0] - own
    half = element_count // 2
    apart = jnp.where(apart > half, apart - element_count, apart)
    apart = jnp.where(apart < -half, apart + element_count, apart) + 2
    both = jnp.concatenate([apart, links_ref[1]], axis=0).astype(jnp.float32)
    spread = lax.broadcasted_iota(jnp.int32, (elements, LANES), 0)
    spread = (spread == lax.broadcasted_iota(jnp.int32, (elements, LANES), 1) // 16).astype(jnp.float32)
    both = jnp.dot(both, spread, preferred_element_type=jnp.float32)
    both = (both + 0.5).astype(jnp.int32)
    lane = lane_ids()
    point = lane % 16
    rows = []
    for s in range(2):
        edge = jnp.zeros((1, LANES), jnp.int32)
        spot = edge
        for p in range(16):
            edge = jnp.where(point == p, int(edge_of[s, p]), edge)
            spot = jnp.where(point == p, int(spot_of[s, p]), spot)
        away, far = both[0:1], both[4:5]
        for k in range(1, 4):
            away = jnp.where(edge == k, both[k : k + 1], away)
            far = jnp.where(edge == k, both[4 + k : 5 + k], far)
        place = jnp.where(far == 2, 12 + spot, 4 * spot)
        place = jnp.where(far == 1, 15 - 4 * spot, place)
        place = jnp.where(far == 0, 3 - spot, place)
        rows.append(lane - point + 16 * away + place)
    rows = jnp.concatenate(rows + [jnp.zeros((6, LANES), jnp.int32)], axis=0)
    return rows.astype(jnp.float32)


def on_odd():
    return lax.axis_index(AXES) % 2 == 1


def sides():
    return (lane_ids() < 64) == on_odd()


def packed_halves(value, chosen):
    away = [pltpu.roll(value[k + 2], 64, 1) for k in range(2)]
    off = [jnp.where(chosen, away[k], value[k]) for k in range(2)]
    on = [jnp.where(chosen, value[k], away[k]) for k in range(2)]
    return off, on


def whole_halves(off, on, chosen):
    count, rows = off.shape[0], off.shape[1]
    direct = jnp.where(chosen, off, on).reshape(count * rows, LANES)
    turned = jnp.where(chosen, on, off).reshape(count * rows, LANES)
    return jnp.concatenate([direct, pltpu.roll(turned, 64, 1)], axis=0)


def pack_kernel(
    inverse_hbm,
    wind_hbm,
    links_hbm,
    state_hbm,
    prev_hbm,
    matrix_ref,
    off_ref,
    on_ref,
    target_ref,
    wind_ref,
    state_ref,
    prev_ref,
    inverse_ref,
    links_ref,
    sems,
):
    pairs = [(inverse_hbm, inverse_ref), (wind_hbm, wind_ref), (links_hbm, links_ref)]
    for k in range(PARTS):
        pairs += [(state_hbm.at[k], state_ref.at[k]), (prev_hbm.at[k], prev_ref.at[k])]
    copies = [pltpu.make_async_copy(a, b, sems.at[i]) for i, (a, b) in enumerate(pairs)]
    for copy in copies:
        copy.start()
    groups, lev = inverse_ref.shape[0], inverse_ref.shape[1]
    copies[0].wait()
    eye = lax.broadcasted_iota(jnp.int32, (lev, lev), 0) == lax.broadcasted_iota(jnp.int32, (lev, lev), 1)
    eye = eye.astype(jnp.float32)
    blank = jnp.zeros((lev, LANES - lev), jnp.float32)
    matrix = [jnp.concatenate([inverse_ref[c] - eye, blank], axis=1) for c in range(groups)]
    matrix_ref[...] = jnp.concatenate(matrix, axis=0).astype(jnp.bfloat16)
    copies[1].wait()
    copies[2].wait()
    devices = lax.axis_size(AXES)
    elements = links_ref.shape[2]
    targets = edge_targets(links_ref, lax.axis_index(AXES) * elements, elements * devices)
    target_ref[...] = targets
    end = off_ref.shape[1]
    filler = jnp.zeros((24, LANES), jnp.float32)
    flat_wind = wind_ref[...].reshape(2 * lev, LANES)
    for k in range(3):
        piece = jnp.concatenate([flat_wind[48 * k : 48 * k + 48], targets, filler], axis=0)
        piece = piece.astype(jnp.bfloat16)
        off_ref[k, end - 80 : end] = piece
        on_ref[k, end - 80 : end] = piece
    chosen = sides()
    odd = jnp.where(on_odd(), 3, 0)
    quarter = lane_ids() // 32
    for copy in copies[3:]:
        copy.wait()
    for at in chunks(state_ref):
        off, on = packed_halves([state_ref[k, at] for k in range(PARTS)], chosen)
        for k in range(2):
            off_ref[k, at] = off[k].astype(jnp.bfloat16)
            on_ref[k, at] = on[k].astype(jnp.bfloat16)
        to_off = jnp.zeros((CHUNK, LANES), jnp.float32)
        to_on = to_off
        for k in range(PARTS):
            turned = prev_ref[k, at].astype(jnp.float32)
            turned = pltpu.roll(turned, 32 * k, 1) if k else turned
            to_off = jnp.where(quarter == (odd + k) % 4, turned, to_off)
            to_on = jnp.where(quarter == (3 - odd + k) % 4, turned, to_on)
        off_ref[2, at] = to_off.astype(jnp.bfloat16)
        on_ref[2, at] = to_on.astype(jnp.bfloat16)


def chunks(ref):
    return [pl.ds(start, CHUNK) for start in range(0, ref.shape[1], CHUNK)]


def each_chunk(ref, body):
    def step(j, carry):
        body(pl.ds(pl.multiple_of(j * CHUNK, CHUNK), CHUNK))
        return carry

    lax.fori_loop(0, ref.shape[1] // CHUNK, step, 0)


def product_tables(matrices, group, first):
    lev = 72
    group = jnp.concatenate([group, group], axis=1)
    picks = [jnp.broadcast_to(group == first + c, (lev, 2 * LANES)) for c in range(8)]
    return jnp.concatenate([matrices, matrices], axis=1), picks


def chosen_product(tables, pair):
    matrices, picks = tables
    lev = pair.shape[0] // 2
    blank = jnp.zeros((LANES - lev, 2 * LANES), jnp.float32)
    pair = jnp.concatenate([pair[:lev], pair[lev:]], axis=1)
    high = pair.astype(jnp.bfloat16).astype(jnp.float32)
    column = jnp.concatenate([high, blank, pair - high, blank], axis=0).astype(jnp.bfloat16)
    product = jnp.dot(matrices, column, preferred_element_type=jnp.float32)
    chosen = jnp.zeros((lev, 2 * LANES), jnp.float32)
    for c in range(8):
        chosen = jnp.where(picks[c], product[c * lev : (c + 1) * lev], chosen)
    return jnp.concatenate([chosen[:, :LANES], chosen[:, LANES:]], axis=0)


def column_group(slot_ref):
    slot = slot_ref[...]
    return jnp.where(slot // LANES == lax.axis_index(AXES), 0, 8) + slot % LANES // 16


def flat(value):
    return value.astype(jnp.float32).reshape(-1, LANES)


def moved(value, slope, blow_x, blow_y):
    rows, lev = value.shape[0], blow_x.shape[0]
    value = value.astype(jnp.bfloat16)
    both = jnp.dot(jnp.concatenate([value, value], axis=1), slope, preferred_element_type=jnp.float32)
    both = both.reshape(rows // lev, lev, 2 * LANES)
    motion = both[..., :LANES] * blow_x + both[..., LANES:] * blow_y
    return motion.reshape(rows, LANES).astype(jnp.bfloat16)


def sum_block(source, targets, slots, own):
    row = lax.broadcasted_iota(jnp.int32, (LANES, LANES), 0)
    total = jnp.zeros((LANES, LANES), jnp.float32)
    if own:
        total = (row == lax.broadcasted_iota(jnp.int32, (LANES, LANES), 1)).astype(jnp.float32)
    place = {
        "own": row,
        "near": jnp.where(row < 64, row + LANES, row - LANES),
        "outer": jnp.where(row < 64, row - LANES, row + LANES),
    }[source]
    for s in range(2):
        total = total + ((place == targets[s : s + 1]) & slots[s]).astype(jnp.float32)
    return total.astype(jnp.bfloat16)


def own_kernel(state_ref, prev_ref, wind_ref, target_ref, slope_ref, slot_ref, own_ref, part_ref, next_ref):
    slots, share = point_sets()
    sums = sum_block("own", target_ref[...].astype(jnp.int32) - 32, slots, True)
    tables = product_tables(own_ref[...], column_group(slot_ref), 0)
    early = time_step * hermite(0)[0]
    blow = [-time_step * wind_ref[d] for d in range(2)]
    slope = slope_ref[...]

    def body(at):
        for k in range(PARTS):
            part_ref[k, at] = chosen_product(tables, state_ref[k, at])
        state = flat(state_ref[:, at])
        motion = moved(state, slope, *blow)
        total = jnp.dot(motion, sums, preferred_element_type=jnp.float32)
        ahead = state + total * share + early * flat(prev_ref[:, at])
        next_ref[:, at] = ahead.reshape(PARTS, CHUNK, LANES)

    each_chunk(state_ref, body)


def far_kernel(
    state_ref, prev_ref, slot_ref, far_ref, part_ref, next_ref, tend_ref, ahead_ref, off_ref, on_ref
):
    group = column_group(slot_ref)
    here = group < 8
    tables = product_tables(far_ref[...], group, 8)
    quarter = lane_ids() // 32
    inner = (quarter == 1) | (quarter == 2)
    chosen = sides()
    late = time_step * hermite(0)[1]
    early_1, late_1 = (time_step * w for w in hermite(1))

    def body(at):
        ahead, force = [], []
        for k in range(PARTS):
            tend = jnp.where(here, part_ref[k, at], chosen_product(tables, state_ref[k, at]))
            tend = tend.astype(jnp.bfloat16)
            tend_ref[k, at] = tend
            tend = tend.astype(jnp.float32)
            ahead.append(next_ref[k, at] + late * tend)
            ahead_ref[k, at] = ahead[k]
            forced = early_1 * prev_ref[k, at].astype(jnp.float32) + late_1 * tend
            force.append(jnp.where(inner, forced, tend))
        off, on = packed_halves(force, chosen)
        for k in range(2):
            middle = jnp.where(inner, ahead[k], pltpu.roll(ahead[k + 2], 64, 1)).astype(jnp.bfloat16)
            off_ref[k, at] = middle
            on_ref[k, at] = middle
            off_ref[2 + k, at] = off[k].astype(jnp.bfloat16)
            on_ref[2 + k, at] = on[k].astype(jnp.bfloat16)

    each_chunk(state_ref, body)


def near_kernel(
    state_ref,
    wind_ref,
    target_ref,
    slope_ref,
    off_ref,
    on_ref,
    add_ref,
    near_ref,
    force_ref,
    sum_ref,
    outer_sum_ref,
    blow_ref,
):
    lev = wind_ref.shape[1]
    slots, share = point_sets()
    chosen = sides()
    end = off_ref.shape[1]

    def extra(ref, k):
        return ref[k, end - 80 : end].astype(jnp.float32)

    def winds(ref):
        whole = jnp.concatenate([extra(ref, k)[:48] for k in range(3)], axis=0)
        return whole[:lev], whole[lev:]

    def targets(ref):
        return extra(ref, 0)[48:56].astype(jnp.int32) - 32

    own_t = target_ref[...].astype(jnp.int32) - 32
    near_t = jnp.where(chosen, targets(off_ref), targets(on_ref))
    near_t = near_t + jnp.where(lane_ids() < 64, LANES, -LANES)
    sum_ref[:LANES, :LANES] = sum_block("own", own_t, slots, True)
    sum_ref[LANES:, :LANES] = sum_block("near", own_t, slots, False)
    sum_ref[:LANES, LANES:] = sum_block("own", near_t, slots, False)
    sum_ref[LANES:, LANES:] = sum_block("near", near_t, slots, True)
    outer_sum_ref[...] = sum_block("outer", near_t, slots, False)
    off_w, on_w = winds(off_ref), winds(on_ref)
    for d in range(2):
        blow_ref[0, d] = -time_step * wind_ref[d]
        blow_ref[1, d] = -time_step * jnp.where(chosen, off_w[d], on_w[d])
        blow_ref[2, d] = -time_step * jnp.where(chosen, on_w[d], off_w[d])

    slope = slope_ref[...]
    early = time_step * hermite(0)[0]

    def body(at):
        off, on = off_ref[:, at].astype(jnp.float32), on_ref[:, at].astype(jnp.float32)
        near = whole_halves(off[:2], on[:2], chosen)
        own_move = moved(flat(state_ref[:, at]), slope, blow_ref[0, 0], blow_ref[0, 1])
        near_move = moved(near, slope, blow_ref[1, 0], blow_ref[1, 1])
        total = jnp.dot(near_move, sum_ref[LANES:], preferred_element_type=jnp.float32)
        near_total = total[:, LANES:] + jnp.dot(
            own_move, sum_ref[:LANES, LANES:], preferred_element_type=jnp.float32
        )
        add_ref[:, at] = (total[:, :LANES] * share).reshape(PARTS, CHUNK, LANES)
        prev = [jnp.where(chosen, off[2], on[2])]
        for k in range(1, PARTS):
            turned = [pltpu.roll(side[2], LANES - 32 * k, 1) for side in (off, on)]
            prev.append(jnp.where(chosen, *turned))
        prev = jnp.concatenate(prev, axis=0)
        near = near + near_total * share + early * prev
        near_ref[:, at] = near.reshape(PARTS, CHUNK, LANES)
        force_ref[:, at] = prev.astype(jnp.bfloat16).reshape(PARTS, CHUNK, LANES)

    each_chunk(state_ref, body)


def advance_kernel(
    ahead_ref,
    add_ref,
    near_ref,
    near_prev_ref,
    prev_ref,
    tend_ref,
    off_ref,
    on_ref,
    slope_ref,
    sum_ref,
    outer_sum_ref,
    blow_ref,
    out_hbm,
    tend_hbm,
    out_ref,
    sems,
):
    tend_copy = pltpu.make_async_copy(tend_ref, tend_hbm, sems.at[0])
    tend_copy.start()
    _, share = point_sets()
    quarter = lane_ids() // 32
    inner = (quarter == 1) | (quarter == 2)
    chosen = sides()
    slope, sums = slope_ref[...], sum_ref[...]
    weights = [tuple(time_step * w for w in hermite(s)) for s in range(SUBSTEPS)]

    def advect(value, unit):
        return moved(value, slope, blow_ref[unit, 0], blow_ref[unit, 1])

    def gather(pieces, matrix):
        return jnp.dot(jnp.concatenate(pieces, axis=1), matrix, preferred_element_type=jnp.float32)

    def middle(value):
        value = value.reshape(2 * CHUNK, LANES)
        return jnp.concatenate([value, pltpu.roll(value, 64, 1)], axis=0)

    def body(at):
        off, on = off_ref[:, at].astype(jnp.float32), on_ref[:, at].astype(jnp.float32)
        off_mid, on_mid = middle(off[:2]), middle(on[:2])
        received = whole_halves(off[2:], on[2:], chosen)
        own_prev, own_tend = flat(prev_ref[:, at]), flat(tend_ref[:, at])
        near_prev = flat(near_prev_ref[:, at])
        own = flat(ahead_ref[:, at]) + flat(add_ref[:, at])
        near = flat(near_ref[:, at]) + weights[0][1] * received
        near = jnp.where(inner, jnp.where(chosen, off_mid, on_mid), near)
        outer = jnp.where(chosen, on_mid, off_mid)
        for s in range(1, SUBSTEPS):
            early, late = weights[s]
            own_force = early * own_prev + late * own_tend
            own_move, near_move = advect(own, 0), advect(near, 1)
            if s == SUBSTEPS - 1:
                total = gather([own_move, near_move], sums[:, :LANES])
                out = own + total * share + own_force
                out_ref[:, at] = out.reshape(PARTS, CHUNK, LANES)
                break
            near_force = early * near_prev + late * received
            total = gather([own_move, near_move], sums)
            own = own + total[:, :LANES] * share + own_force
            near_total = total[:, LANES:]
            if s == 1:
                near_force = jnp.where(inner, received, near_force)
                near_total = near_total + jnp.dot(
                    advect(outer, 2), outer_sum_ref[...], preferred_element_type=jnp.float32
                )
            near = near + near_total * share + near_force

    copies = []
    for j, at in enumerate(chunks(out_ref)):
        body(at)
        copies.append(pltpu.make_async_copy(out_ref.at[:, at], out_hbm.at[:, at], sems.at[1 + j]))
        copies[j].start()
    for copy in copies:
        copy.wait()
    tend_copy.wait()


def exchanged(off, on):
    count = lax.axis_size(AXES)
    across = [(i, (i + 1) % count if i % 2 else (i - 1) % count) for i in range(count)]
    inside = [(i, i ^ 1) for i in range(count)]
    return lax.ppermute(off, AXES, across), lax.ppermute(on, AXES, inside)


def per_device(state, prev_tendency, wind, edge_links, swap_slot, inverse):
    devices = lax.axis_size(AXES)
    shape = state.shape
    lev = shape[1]
    rows = shape[0] * lev // PARTS
    params = pltpu.CompilerParams(vmem_limit_bytes=VMEM)
    bf16, f32 = jnp.bfloat16, jnp.float32
    inner = pl.BlockSpec(memory_space=pltpu.VMEM)
    outer = pl.BlockSpec(memory_space=pltpu.HBM)

    def like(count, kind, length=rows):
        return pltpu.VMEM((count, length, LANES), kind)

    def table(kind, *size):
        return pltpu.VMEM(size, kind)

    def call(body, ins, outs, name, passes, **more):
        size = sum(math.prod(array.shape) * array.dtype.itemsize for array in ins)
        cost = pl.CostEstimate(
            flops=passes * 2 * PARTS * rows * 256 * 256, bytes_accessed=2 * size, transcendentals=0
        )
        more = {"in_specs": [inner] * len(ins), "out_specs": (inner,) * len(outs)} | more
        return pl.pallas_call(
            body, out_shape=outs, compiler_params=params, cost_estimate=cost, name=name, **more
        )(*ins)

    slot = swap_slot.reshape(1, LANES)
    slope = jnp.asarray(derivative_matrix())
    message = like(3, bf16, rows + 80)
    inputs = (
        inverse,
        wind,
        edge_links,
        state.reshape(PARTS, rows, LANES),
        prev_tendency.reshape(PARTS, rows, LANES),
    )
    inputs = tuple(pltpu.with_memory_space_constraint(array, pltpu.HBM) for array in inputs)
    matrices, to_off, to_on, targets, wind, state, prev = call(
        pack_kernel,
        inputs,
        (
            table(bf16, inverse.shape[0] * lev, LANES),
            message,
            message,
            table(f32, 8, LANES),
            table(f32, *wind.shape),
            like(4, f32),
            like(4, bf16),
        ),
        "pack",
        2,
        in_specs=[outer] * len(inputs),
        scratch_shapes=[
            pltpu.VMEM(inverse.shape, f32),
            pltpu.VMEM(edge_links.shape, jnp.int32),
            pltpu.SemaphoreType.DMA((3 + 2 * PARTS,)),
        ],
    )
    far_matrices = lax.ppermute(matrices, AXES, [(i, i ^ (devices // 2)) for i in range(devices)])
    off, on = exchanged(to_off, to_on)
    part, ahead = call(
        own_kernel,
        (state, prev, wind, targets, slope, slot, matrices),
        (like(4, f32), like(4, f32)),
        "own",
        10,
    )
    tend, ahead, mid_off, mid_on = call(
        far_kernel,
        (state, prev, slot, far_matrices, part, ahead),
        (like(4, bf16), like(4, f32), like(4, bf16), like(4, bf16)),
        "far",
        10,
    )
    mid_off, mid_on = exchanged(mid_off, mid_on)
    add, near, near_prev, sums, outer_sums, blow = call(
        near_kernel,
        (state, wind, targets, slope, off, on),
        (
            like(4, f32),
            like(4, f32),
            like(4, bf16),
            table(bf16, 2 * LANES, 2 * LANES),
            table(bf16, LANES, LANES),
            table(f32, 3, 2, lev, LANES),
        ),
        "near",
        8,
    )
    out, tend = call(
        advance_kernel,
        (ahead, add, near, near_prev, prev, tend, mid_off, mid_on, slope, sums, outer_sums, blow),
        (
            jax.ShapeDtypeStruct((PARTS, rows, LANES), f32),
            jax.ShapeDtypeStruct((PARTS, rows, LANES), bf16),
        ),
        "advance",
        24,
        out_specs=(outer, outer),
        scratch_shapes=[
            pltpu.VMEM((PARTS, rows, LANES), f32),
            pltpu.SemaphoreType.DMA((1 + rows // CHUNK,)),
        ],
    )
    return (out.reshape(shape), tend.reshape(shape))


def solution(mesh):
    columns = P(None, None, AXES)
    return jax.shard_map(
        per_device,
        mesh=mesh,
        in_specs=(columns, columns, columns, columns, P(AXES), P(AXES, None, None)),
        out_specs=(columns, columns),
        check_vma=False,
    )
```

time: 51.1 us -> 40.8 us (0.80)
  starting transfers between devices: 18.5 us -> 11.3 us
  waiting for transfers between devices: 5.61 us -> 11.1 us
  local copies, waits for them, and re-layouts: 4.12 us -> 0.01 us
  Pallas kernels: 21 us -> 17.6 us
  other arithmetic: 1 us -> 0 us
    ppermute x4, starting transfers between devices: 14.4 us -> 7.25 us  [exchanged(): return (lax.ppermute(off, AXES, across), lax.ppermute(on, AXES, inside))]
    ppermute x4, waiting for transfers between devices: 5.61 us -> 11.1 us  [exchanged(): return (lax.ppermute(off, AXES, across), lax.ppermute(on, AXES, inside))]
    unnamed x18 -> x4, local copies, waits for them, and re-layouts: 4.08 us -> 0.01 us
    pallas_call x5, Pallas kernels: 21 us -> 17.6 us  [call(): pl.pallas_call(body, out_shape=outs, compiler_params=params, cost_estimat...]
    convert_element_type x2 -> x0, other arithmetic: 1 us -> none  [per_device(): matrices = (inverse - jnp.eye(lev, dtype=f32)).astype(bf16)]
  transfers between devices with their start and end apart: 5 -> 5, of which waited for: 1 -> 2; matrix products, arithmetic and copies ran while one was open for 0% -> 0% of each run, Pallas kernels for 26% -> 22%
where the time goes in v1:
time: 40.8 us; the launch traced here: 40.7 us
  Pallas kernels  17.6 us (43%)
  starting transfers between devices  11.3 us (28%)
  waiting for transfers between devices  11.1 us (27%)
  between operations  0.69 us (2%)
    pallas_call x5, Pallas kernels, call(): pl.pallas_call(body, out_shape=outs, compiler_params=params, cost_estimat...  17.6 us
    ppermute x4, waiting for transfers between devices, exchanged(): return (lax.ppermute(off, AXES, across), lax.ppermute(on, AXES, inside))  11.1 us
    ppermute x4, starting transfers between devices, exchanged(): return (lax.ppermute(off, AXES, across), lax.ppermute(on, AXES, inside))  7.25 us
    ppermute x1, starting transfers between devices, per_device(): lax.ppermute(matrices, AXES, [(i, i ^ devices // 2) for i in range(device...  4.04 us
  transfers between devices with their start and end apart: 5, of which 2 were waited for; matrix products, arithmetic and copies ran while one was open for 0% of the time, Pallas kernels for 22%

profile of v1, /device:TPU:0, one launch (start us, length us, event | category | flops | bytes accessed | tf_op | source)
XLA Modules:
  0.0 40.7 jit_solution(11590277209355230437)
XLA Ops:
  0.6 0.0 copy-start.1
  0.6 0.0 copy-start
  0.7 2.2 %pack.1 = (bf16[576,128]{1,0:T(8,128)(2,1)S(1)}, bf16[3,800,128]{2,1,0:T(8,128)(2,1)S(1)}, bf16[3,800,128]{2,1,0:T(8,128)(2,1)S(1)}, f32[8,128]{1,0:T(8,128)S(1)...) custom-call(f32[8,72,72]{2,1,0:T(8,128)} %inverse_hbm.1, ...), custom_call_target="tpu_custom_call" | custom-call | flops 754974720 | bytes 4903424 | tf_op jit(solution)/shard_map/pack/pallas_call | solution.py:508
  2.8 4.0 %collective-permute-start = (bf16[576,128]{1,0:T(8,128)(2,1)S(1)}, bf16[576,128]{1,0:T(8,128)(2,1)S(1)}, u32[]{:S(2)}, u32[]{:S(2)}) collective-permute-start(bf16[576,128]{1,0:T(8,128)(2,1)S(1)} %get-tuple-element.25.own_ref), channel_id=1, source_target_pairs={{0,64},{1,65},{2,66},{3,67},{4,68},{5,69},{6,70},{7,71},{8,72},{9,... | collective-permute-start | bytes 442376 | tf_op jit(solution)/shard_map/ppermute | solution.py:544
  6.9 4.5 %collective-permute-start.1 = (bf16[3,800,128]{2,1,0:T(8,128)(2,1)S(1)}, bf16[3,800,128]{2,1,0:T(8,128)(2,1)S(1)}, u32[]{:S(2)}, u32[]{:S(2)}) collective-permute-start(bf16[3,800,128]{2,1,0:T(8,128)(2,1)S(1)} %get-tuple-element.31), channel_id=1, source_target_pairs={{0,127},{1,2},{2,1},{3,4},{4,3},{5,6},{6,5},{7,8},{8,7},{9,10},{10... | collective-permute-start | bytes 1843208 | tf_op jit(solution)/shard_map/ppermute | solution.py:483
  11.4 0.0 collective-permute-start.2
  11.4 0.0 copy-done.1
  11.4 0.0 copy-done
  11.4 3.6 %own.1 = (f32[4,720,128]{2,1,0:T(8,128)S(1)}, f32[4,720,128]{2,1,0:T(8,128)S(1)}) custom-call(f32[4,720,128]{2,1,0:T(8,128)S(1)} %get-tuple-element.23.state_ref, bf16[4,720,128]{2,1,0:T(8,128)(2,1)S(1)} %get-tuple-element.24.prev_ref, f32[2,72,128]{2,1,0:T(8,128)S(1)} %get-tuple-element.26.wind_ref, f32[8,128]{1,0:T(8,128)S(1)} %get-tuple-element.27.target_ref, ...), custom_call_target="tpu_custom_call" | custom-call | flops 3774873600 | bytes 5137408 | tf_op jit(solution)/shard_map/own/pallas_call | solution.py:508
  15.0 0.0 collective-permute-done.far_ref
  15.0 3.0 %far.1 = (bf16[4,720,128]{2,1,0:T(8,128)(2,1)S(1)}, f32[4,720,128]{2,1,0:T(8,128)S(1)}, bf16[4,720,128]{2,1,0:T(8,128)(2,1)S(1)}, bf16[4,720,128]{2,1,0:T(8,128)(2,1)S(1)}) custom-call(f32[4,720,128]{2,1,0:T(8,128)S(1)} %get-tuple-element.23.state_ref, bf16[4,720,128]{2,1,0:T(8,128)(2,1)S(1)} %get-tuple-element.24.prev_ref, s32[1,128]{1,0:T(1,128)S(1)} %bitcast.6, ...), custom_call_target="tpu_custom_call" | custom-call | flops 3774873600 | bytes 10617856 | tf_op jit(solution)/shard_map/far/pallas_call | solution.py:508
  18.0 2.7 %collective-permute-start.3 = (bf16[4,720,128]{2,1,0:T(8,128)(2,1)S(1)}, bf16[4,720,128]{2,1,0:T(8,128)(2,1)S(1)}, u32[]{:S(2)}, u32[]{:S(2)}) collective-permute-start(bf16[4,720,128]{2,1,0:T(8,128)(2,1)S(1)} %get-tuple-element.37), channel_id=1, source_target_pairs={{0,127},{1,2},{2,1},{3,4},{4,3},{5,6},{6,5},{7,8},{8,7},{9,10},{10... | collective-permute-start | bytes 2211848 | tf_op jit(solution)/shard_map/ppermute | solution.py:483
  20.7 0.0 collective-permute-start.4
  20.7 1.1 %collective-permute-done.1.off_ref = bf16[3,800,128]{2,1,0:T(8,128)(2,1)S(1)} collective-permute-done((bf16[3,800,128]{2,1,0:T(8,128)(2,1)S(1)}, bf16[3,800,128]{2,1,0:T(8,128)(2,1)S(1)}, u32[]{:S(2)}, u32[]{:S(2)}) %collective-permute-start.1) | collective-permute-done | bytes 614432 | tf_op jit(solution)/shard_map/ppermute | solution.py:483
  21.9 0.0 collective-permute-done.2.on_ref
  21.9 2.6 %near.1 = (f32[4,720,128]{2,1,0:T(8,128)S(1)}, f32[4,720,128]{2,1,0:T(8,128)S(1)}, bf16[4,720,128]{2,1,0:T(8,128)(2,1)S(1)}, bf16[256,256]{1,0:T(8,128)(2,1)S(1)...) custom-call(f32[4,720,128]{2,1,0:T(8,128)S(1)} %get-tuple-element.23.state_ref, ...), custom_call_target="tpu_custom_call" | custom-call | flops 3019898880 | bytes 5824512 | tf_op jit(solution)/shard_map/near/pallas_call | solution.py:508
  24.4 10.0 %collective-permute-done.3.off_ref = bf16[4,720,128]{2,1,0:T(8,128)(2,1)S(1)} collective-permute-done((bf16[4,720,128]{2,1,0:T(8,128)(2,1)S(1)}, bf16[4,720,128]{2,1,0:T(8,128)(2,1)S(1)}, u32[]{:S(2)}, u32[]{:S(2)}) %collective-permute-start.3) | collective-permute-done | bytes 737312 | tf_op jit(solution)/shard_map/ppermute | solution.py:483
  34.4 0.0 collective-permute-done.4.on_ref
  34.4 6.3 %advance.1 = (f32[4,720,128]{2,1,0:T(8,128)}, bf16[4,720,128]{2,1,0:T(8,128)(2,1)}) custom-call(f32[4,720,128]{2,1,0:T(8,128)S(1)} %get-tuple-element.30.ahead_ref, f32[4,720,128]{2,1,0:T(8,128)S(1)} %get-tuple-element.33.add_ref, f32[4,720,128]{2,1,0:T(8,128)S(1)} %get-tuple-element.34.near_ref, bf16[4,720,128]{2,1,0:T(8,128)(2,1)S(1)} %get-tuple-element.35.near_prev_ref, ...), custom_call_target="tpu_custom_call" | custom-call | flops 9059696640 | bytes 17252352 | tf_op jit(solution)/shard_map/advance/pallas_call | solution.py:508
Async XLA Ops:
  0.6 10.8 %copy-start.1 = (bf16[256,256]{1,0:T(8,128)(2,1)S(1)}, bf16[256,256]{1,0:T(8,128)(2,1)}, u32[]{:S(2)}) copy-start(bf16[256,256]{1,0:T(8,128)(2,1)} %constant.2.clone.slope_ref) | copy-start | bytes 393220
  0.6 10.7 %copy-start = (s32[128]{0:T(128)S(1)}, s32[128]{0:T(128)}, u32[]{:S(2)}) copy-start(s32[128]{0:T(128)} %param.11) | copy-start | bytes 1540
  2.8 12.2 %collective-permute-start = (bf16[576,128]{1,0:T(8,128)(2,1)S(1)}, bf16[576,128]{1,0:T(8,128)(2,1)S(1)}, u32[]{:S(2)}, u32[]{:S(2)}) collective-permute-start(bf16[576,128]{1,0:T(8,128)(2,1)S(1)} %get-tuple-element.25.own_ref), channel_id=1, source_target_pairs={{0,64},{1,65},{2,66},{3,67},{4,68},{5,69},{6,70},{7,71},{8,72},{9,... | collective-permute-start | bytes 442376 | tf_op jit(solution)/shard_map/ppermute | solution.py:544
  6.9 15.0 %collective-permute-start.1 = (bf16[3,800,128]{2,1,0:T(8,128)(2,1)S(1)}, bf16[3,800,128]{2,1,0:T(8,128)(2,1)S(1)}, u32[]{:S(2)}, u32[]{:S(2)}) collective-permute-start(bf16[3,800,128]{2,1,0:T(8,128)(2,1)S(1)} %get-tuple-element.31), channel_id=1, source_target_pairs={{0,127},{1,2},{2,1},{3,4},{4,3},{5,6},{6,5},{7,8},{8,7},{9,10},{10... | collective-permute-start | bytes 1843208 | tf_op jit(solution)/shard_map/ppermute | solution.py:483
  11.4 10.5 %collective-permute-start.2 = (bf16[3,800,128]{2,1,0:T(8,128)(2,1)S(1)}, bf16[3,800,128]{2,1,0:T(8,128)(2,1)S(1)}, u32[]{:S(2)}, u32[]{:S(2)}) collective-permute-start(bf16[3,800,128]{2,1,0:T(8,128)(2,1)S(1)} %get-tuple-element.32), channel_id=1, source_target_pairs={{0,1},{1,0},{2,3},{3,2},{4,5},{5,4},{6,7},{7,6},{8,9},{9,8},{10,11... | collective-permute-start | bytes 1843208 | tf_op jit(solution)/shard_map/ppermute | solution.py:483
  18.0 16.4 %collective-permute-start.3 = (bf16[4,720,128]{2,1,0:T(8,128)(2,1)S(1)}, bf16[4,720,128]{2,1,0:T(8,128)(2,1)S(1)}, u32[]{:S(2)}, u32[]{:S(2)}) collective-permute-start(bf16[4,720,128]{2,1,0:T(8,128)(2,1)S(1)} %get-tuple-element.37), channel_id=1, source_target_pairs={{0,127},{1,2},{2,1},{3,4},{4,3},{5,6},{6,5},{7,8},{8,7},{9,10},{10... | collective-permute-start | bytes 2211848 | tf_op jit(solution)/shard_map/ppermute | solution.py:483
  20.7 13.7 %collective-permute-start.4 = (bf16[4,720,128]{2,1,0:T(8,128)(2,1)S(1)}, bf16[4,720,128]{2,1,0:T(8,128)(2,1)S(1)}, u32[]{:S(2)}, u32[]{:S(2)}) collective-permute-start(bf16[4,720,128]{2,1,0:T(8,128)(2,1)S(1)} %get-tuple-element.38), channel_id=1, source_target_pairs={{0,1},{1,0},{2,3},{3,2},{4,5},{5,4},{6,7},{7,6},{8,9},{9,8},{10,11... | collective-permute-start | bytes 2211848 | tf_op jit(solution)/shard_map/ppermute | solution.py:483

commit v2 on v1

--- a/solution.py
+++ b/solution.py
@@ -1,3 +1,4 @@
+import functools
 import math
 
 import jax
@@ -12,6 +13,7 @@
 AXES = ("gx", "gy")
 LANES = 128
 CHUNK = 144
+SPLIT = (3, 2)
 PARTS = 4
 VMEM = 16 * 1024 * 1024
 
@@ -215,12 +217,13 @@
     return [pl.ds(start, CHUNK) for start in range(0, ref.shape[1], CHUNK)]
 
 
-def each_chunk(ref, body):
+def each_chunk(first, count, body):
     def step(j, carry):
-        body(pl.ds(pl.multiple_of(j * CHUNK, CHUNK), CHUNK))
+        near, whole = j * CHUNK, (first + j) * CHUNK
+        body(pl.ds(pl.multiple_of(whole, CHUNK), CHUNK), pl.ds(pl.multiple_of(near, CHUNK), CHUNK))
         return carry
 
-    lax.fori_loop(0, ref.shape[1] // CHUNK, step, 0)
+    lax.fori_loop(0, count, step, 0)
 
 
 def product_tables(matrices, group, first):
@@ -285,7 +288,7 @@
     blow = [-time_step * wind_ref[d] for d in range(2)]
     slope = slope_ref[...]
 
-    def body(at):
+    def body(at, _):
         for k in range(PARTS):
             part_ref[k, at] = chosen_product(tables, state_ref[k, at])
         state = flat(state_ref[:, at])
@@ -294,11 +297,11 @@
         ahead = state + total * share + early * flat(prev_ref[:, at])
         next_ref[:, at] = ahead.reshape(PARTS, CHUNK, LANES)
 
-    each_chunk(state_ref, body)
+    each_chunk(0, state_ref.shape[1] // CHUNK, body)
 
 
 def far_kernel(
-    state_ref, prev_ref, slot_ref, far_ref, part_ref, next_ref, tend_ref, ahead_ref, off_ref, on_ref
+    first, count, state_ref, prev_ref, slot_ref, far_ref, part_ref, next_ref, tend_ref, ahead_ref, off_ref, on_ref
 ):
     group = column_group(slot_ref)
     here = group < 8
@@ -309,26 +312,26 @@
     late = time_step * hermite(0)[1]
     early_1, late_1 = (time_step * w for w in hermite(1))
 
-    def body(at):
+    def body(at, here_at):
         ahead, force = [], []
         for k in range(PARTS):
             tend = jnp.where(here, part_ref[k, at], chosen_product(tables, state_ref[k, at]))
             tend = tend.astype(jnp.bfloat16)
-            tend_ref[k, at] = tend
+            tend_ref[k, here_at] = tend
             tend = tend.astype(jnp.float32)
             ahead.append(next_ref[k, at] + late * tend)
-            ahead_ref[k, at] = ahead[k]
+            ahead_ref[k, here_at] = ahead[k]
             forced = early_1 * prev_ref[k, at].astype(jnp.float32) + late_1 * tend
             force.append(jnp.where(inner, forced, tend))
         off, on = packed_halves(force, chosen)
         for k in range(2):
             middle = jnp.where(inner, ahead[k], pltpu.roll(ahead[k + 2], 64, 1)).astype(jnp.bfloat16)
-            off_ref[k, at] = middle
-            on_ref[k, at] = middle
-            off_ref[2 + k, at] = off[k].astype(jnp.bfloat16)
-            on_ref[2 + k, at] = on[k].astype(jnp.bfloat16)
-
-    each_chunk(state_ref, body)
+            off_ref[k, here_at] = middle
+            on_ref[k, here_at] = middle
+            off_ref[2 + k, here_at] = off[k].astype(jnp.bfloat16)
+            on_ref[2 + k, here_at] = on[k].astype(jnp.bfloat16)
+
+    each_chunk(first, count, body)
 
 
 def near_kernel(
@@ -377,7 +380,7 @@
     slope = slope_ref[...]
     early = time_step * hermite(0)[0]
 
-    def body(at):
+    def body(at, _):
         off, on = off_ref[:, at].astype(jnp.float32), on_ref[:, at].astype(jnp.float32)
         near = whole_halves(off[:2], on[:2], chosen)
         own_move = moved(flat(state_ref[:, at]), slope, blow_ref[0, 0], blow_ref[0, 1])
@@ -396,10 +399,11 @@
         near_ref[:, at] = near.reshape(PARTS, CHUNK, LANES)
         force_ref[:, at] = prev.astype(jnp.bfloat16).reshape(PARTS, CHUNK, LANES)
 
-    each_chunk(state_ref, body)
+    each_chunk(0, state_ref.shape[1] // CHUNK, body)
 
 
 def advance_kernel(
+    first,
     ahead_ref,
     add_ref,
     near_ref,
@@ -412,12 +416,11 @@
     sum_ref,
     outer_sum_ref,
     blow_ref,
-    out_hbm,
-    tend_hbm,
-    out_ref,
-    sems,
+    *rest,
 ):
-    tend_copy = pltpu.make_async_copy(tend_ref, tend_hbm, sems.at[0])
+    out_hbm, tend_hbm, out_ref, sems = rest[-4:]
+    count = tend_ref.shape[1]
+    tend_copy = pltpu.make_async_copy(tend_ref, tend_hbm.at[:, pl.ds(first * CHUNK, count)], sems.at[0])
     tend_copy.start()
     _, share = point_sets()
     quarter = lane_ids() // 32
@@ -436,13 +439,13 @@
         value = value.reshape(2 * CHUNK, LANES)
         return jnp.concatenate([value, pltpu.roll(value, 64, 1)], axis=0)
 
-    def body(at):
-        off, on = off_ref[:, at].astype(jnp.float32), on_ref[:, at].astype(jnp.float32)
+    def body(at, here_at):
+        off, on = off_ref[:, here_at].astype(jnp.float32), on_ref[:, here_at].astype(jnp.float32)
         off_mid, on_mid = middle(off[:2]), middle(on[:2])
         received = whole_halves(off[2:], on[2:], chosen)
-        own_prev, own_tend = flat(prev_ref[:, at]), flat(tend_ref[:, at])
+        own_prev, own_tend = flat(prev_ref[:, at]), flat(tend_ref[:, here_at])
         near_prev = flat(near_prev_ref[:, at])
-        own = flat(ahead_ref[:, at]) + flat(add_ref[:, at])
+        own = flat(ahead_ref[:, here_at]) + flat(add_ref[:, at])
         near = flat(near_ref[:, at]) + weights[0][1] * received
         near = jnp.where(inner, jnp.where(chosen, off_mid, on_mid), near)
         outer = jnp.where(chosen, on_mid, off_mid)
@@ -453,7 +456,7 @@
             if s == SUBSTEPS - 1:
                 total = gather([own_move, near_move], sums[:, :LANES])
                 out = own + total * share + own_force
-                out_ref[:, at] = out.reshape(PARTS, CHUNK, LANES)
+                out_ref[:, here_at] = out.reshape(PARTS, CHUNK, LANES)
                 break
             near_force = early * near_prev + late * received
             total = gather([own_move, near_move], sums)
@@ -467,9 +470,10 @@
             near = near + near_total * share + near_force
 
     copies = []
-    for j, at in enumerate(chunks(out_ref)):
-        body(at)
-        copies.append(pltpu.make_async_copy(out_ref.at[:, at], out_hbm.at[:, at], sems.at[1 + j]))
+    for j, here_at in enumerate(chunks(out_ref)):
+        at = pl.ds((first + j) * CHUNK, CHUNK)
+        body(at, here_at)
+        copies.append(pltpu.make_async_copy(out_ref.at[:, here_at], out_hbm.at[:, at], sems.at[1 + j]))
         copies[j].start()
     for copy in copies:
         copy.wait()
@@ -543,21 +547,26 @@
     )
     far_matrices = lax.ppermute(matrices, AXES, [(i, i ^ (devices // 2)) for i in range(devices)])
     off, on = exchanged(to_off, to_on)
-    part, ahead = call(
+    part, next_state = call(
         own_kernel,
         (state, prev, wind, targets, slope, slot, matrices),
         (like(4, f32), like(4, f32)),
         "own",
         10,
     )
-    tend, ahead, mid_off, mid_on = call(
-        far_kernel,
-        (state, prev, slot, far_matrices, part, ahead),
-        (like(4, bf16), like(4, f32), like(4, bf16), like(4, bf16)),
-        "far",
-        10,
-    )
-    mid_off, mid_on = exchanged(mid_off, mid_on)
+    halves = []
+    first = 0
+    for count in SPLIT:
+        size = count * CHUNK
+        tend, ahead, to_off, to_on = call(
+            functools.partial(far_kernel, first, count),
+            (state, prev, slot, far_matrices, part, next_state),
+            (like(4, bf16, size), like(4, f32, size), like(4, bf16, size), like(4, bf16, size)),
+            "far",
+            2 * count,
+        )
+        halves.append((first, count, tend, ahead, exchanged(to_off, to_on)))
+        first += count
     add, near, near_prev, sums, outer_sums, blow = call(
         near_kernel,
         (state, wind, targets, slope, off, on),
@@ -572,21 +581,27 @@
         "near",
         8,
     )
-    out, tend = call(
-        advance_kernel,
-        (ahead, add, near, near_prev, prev, tend, mid_off, mid_on, slope, sums, outer_sums, blow),
-        (
-            jax.ShapeDtypeStruct((PARTS, rows, LANES), f32),
-            jax.ShapeDtypeStruct((PARTS, rows, LANES), bf16),
-        ),
-        "advance",
-        24,
-        out_specs=(outer, outer),
-        scratch_shapes=[
-            pltpu.VMEM((PARTS, rows, LANES), f32),
-            pltpu.SemaphoreType.DMA((1 + rows // CHUNK,)),
-        ],
-    )
+    done = ()
+    for first, count, tend, ahead, (off, on) in halves:
+        ins = (ahead, add, near, near_prev, prev, tend, off, on, slope, sums, outer_sums, blow)
+        done = call(
+            functools.partial(advance_kernel, first),
+            ins + done,
+            (
+                jax.ShapeDtypeStruct((PARTS, rows, LANES), f32),
+                jax.ShapeDtypeStruct((PARTS, rows, LANES), bf16),
+            ),
+            "advance",
+            5 * count,
+            in_specs=[inner] * len(ins) + [outer] * len(done),
+            out_specs=(outer, outer),
+            scratch_shapes=[
+                pltpu.VMEM((PARTS, count * CHUNK, LANES), f32),
+                pltpu.SemaphoreType.DMA((1 + count,)),
+            ],
+            input_output_aliases={len(ins) + i: i for i in range(len(done))},
+        )
+    out, tend = done
     return (out.reshape(shape), tend.reshape(shape))
 
 

time: 40.8 us -> 37.3 us (0.914)
  waiting for transfers between devices: 11.1 us -> 2.12 us
  starting transfers between devices: 11.3 us -> 15.9 us
  Pallas kernels: 17.6 us -> 18.4 us
    ppermute x4 -> x6, waiting for transfers between devices: 11.1 us -> 2.12 us  [exchanged(): return (lax.ppermute(off, AXES, across), lax.ppermute(on, AXES, inside))]
    ppermute x4 -> x6, starting transfers between devices: 7.25 us -> 11.9 us  [exchanged(): return (lax.ppermute(off, AXES, across), lax.ppermute(on, AXES, inside))]
    pallas_call x5 -> x7, Pallas kernels: 17.6 us -> 18.4 us  [call(): pl.pallas_call(body, out_shape=outs, compiler_params=params, cost_estimat...]
  transfers between devices with their start and end apart: 5 -> 7, of which waited for: 2 -> 1; matrix products, arithmetic and copies ran while one was open for 0% -> 0% of each run, Pallas kernels for 22% -> 36%
where the time goes in v2:
time: 37.3 us; the launch traced here: 37.2 us
  Pallas kernels  18.4 us (49%)
  starting transfers between devices  15.9 us (43%)
  waiting for transfers between devices  2.12 us (6%)
  between operations  0.73 us (2%)
    pallas_call x7, Pallas kernels, call(): pl.pallas_call(body, out_shape=outs, compiler_params=params, cost_estimat...  18.4 us
    ppermute x6, starting transfers between devices, exchanged(): return (lax.ppermute(off, AXES, across), lax.ppermute(on, AXES, inside))  11.9 us
    ppermute x1, starting transfers between devices, per_device(): lax.ppermute(matrices, AXES, [(i, i ^ devices // 2) for i in range(device...  4.04 us
    ppermute x6, waiting for transfers between devices, exchanged(): return (lax.ppermute(off, AXES, across), lax.ppermute(on, AXES, inside))  2.12 us
  transfers between devices with their start and end apart: 7, of which 1 were waited for; matrix products, arithmetic and copies ran while one was open for 0% of the time, Pallas kernels for 36%

profile of v2, /device:TPU:0, one launch (start us, length us, event | category | flops | bytes accessed | tf_op | source)
XLA Modules:
  0.0 37.2 jit_solution(12477334655181626371)
XLA Ops:
  0.6 0.0 copy-start.1
  0.6 0.0 copy-start
  0.7 2.2 %pack.1 = (bf16[576,128]{1,0:T(8,128)(2,1)S(1)}, bf16[3,800,128]{2,1,0:T(8,128)(2,1)S(1)}, bf16[3,800,128]{2,1,0:T(8,128)(2,1)S(1)}, f32[8,128]{1,0:T(8,128)S(1)...) custom-call(f32[8,72,72]{2,1,0:T(8,128)} %inverse_hbm.1, ...), custom_call_target="tpu_custom_call" | custom-call | flops 754974720 | bytes 4903424 | tf_op jit(solution)/shard_map/pack/pallas_call | solution.py:512
  2.8 4.0 %collective-permute-start = (bf16[576,128]{1,0:T(8,128)(2,1)S(1)}, bf16[576,128]{1,0:T(8,128)(2,1)S(1)}, u32[]{:S(2)}, u32[]{:S(2)}) collective-permute-start(bf16[576,128]{1,0:T(8,128)(2,1)S(1)} %get-tuple-element.31.own_ref), channel_id=1, source_target_pairs={{0,64},{1,65},{2,66},{3,67},{4,68},{5,69},{6,70},{7,71},{8,72},{9,... | collective-permute-start | bytes 442376 | tf_op jit(solution)/shard_map/ppermute | solution.py:548
  6.9 4.5 %collective-permute-start.1 = (bf16[3,800,128]{2,1,0:T(8,128)(2,1)S(1)}, bf16[3,800,128]{2,1,0:T(8,128)(2,1)S(1)}, u32[]{:S(2)}, u32[]{:S(2)}) collective-permute-start(bf16[3,800,128]{2,1,0:T(8,128)(2,1)S(1)} %get-tuple-element.37), channel_id=1, source_target_pairs={{0,127},{1,2},{2,1},{3,4},{4,3},{5,6},{6,5},{7,8},{8,7},{9,10},{10... | collective-permute-start | bytes 1843208 | tf_op jit(solution)/shard_map/ppermute | solution.py:487
  11.4 0.0 collective-permute-start.2
  11.4 0.0 copy-done.1
  11.4 0.0 copy-done
  11.4 3.6 %own.1 = (f32[4,720,128]{2,1,0:T(8,128)S(1)}, f32[4,720,128]{2,1,0:T(8,128)S(1)}) custom-call(f32[4,720,128]{2,1,0:T(8,128)S(1)} %get-tuple-element.29.state_ref, bf16[4,720,128]{2,1,0:T(8,128)(2,1)S(1)} %get-tuple-element.30.prev_ref, f32[2,72,128]{2,1,0:T(8,128)S(1)} %get-tuple-element.32.wind_ref, f32[8,128]{1,0:T(8,128)S(1)} %get-tuple-element.33.target_ref, ...), custom_call_target="tpu_custom_call" | custom-call | flops 3774873600 | bytes 5137408 | tf_op jit(solution)/shard_map/own/pallas_call | solution.py:512
  15.0 0.0 collective-permute-done.far_ref
  15.0 1.8 %far.3 = (bf16[4,432,128]{2,1,0:T(8,128)(2,1)S(1)}, f32[4,432,128]{2,1,0:T(8,128)S(1)}, bf16[4,432,128]{2,1,0:T(8,128)(2,1)S(1)}, bf16[4,432,128]{2,1,0:T(8,128)(2,1)S(1)}) custom-call(f32[4,720,128]{2,1,0:T(8,128)S(1)} %get-tuple-element.29.state_ref, bf16[4,720,128]{2,1,0:T(8,128)(2,1)S(1)} %get-tuple-element.30.prev_ref, s32[1,128]{1,0:T(1,128)S(1)} %bitcast.6, ...), custom_call_target="tpu_custom_call" | custom-call | flops 2264924160 | bytes 10617856 | tf_op jit(solution)/shard_map/far/pallas_call | solution.py:512
  16.8 2.7 %collective-permute-start.5 = (bf16[4,432,128]{2,1,0:T(8,128)(2,1)S(1)}, bf16[4,432,128]{2,1,0:T(8,128)(2,1)S(1)}, u32[]{:S(2)}, u32[]{:S(2)}) collective-permute-start(bf16[4,432,128]{2,1,0:T(8,128)(2,1)S(1)} %get-tuple-element.50), channel_id=1, source_target_pairs={{0,127},{1,2},{2,1},{3,4},{4,3},{5,6},{6,5},{7,8},{8,7},{9,10},{10... | collective-permute-start | bytes 1327112 | tf_op jit(solution)/shard_map/ppermute | solution.py:487
  19.5 0.0 collective-permute-start.6
  19.5 1.2 %far.2 = (bf16[4,288,128]{2,1,0:T(8,128)(2,1)S(1)}, f32[4,288,128]{2,1,0:T(8,128)S(1)}, bf16[4,288,128]{2,1,0:T(8,128)(2,1)S(1)}, bf16[4,288,128]{2,1,0:T(8,128)(2,1)S(1)}) custom-call(f32[4,720,128]{2,1,0:T(8,128)S(1)} %get-tuple-element.29.state_ref, bf16[4,720,128]{2,1,0:T(8,128)(2,1)S(1)} %get-tuple-element.30.prev_ref, s32[1,128]{1,0:T(1,128)S(1)} %bitcast.7, ...), custom_call_target="tpu_custom_call" | custom-call | flops 1509949440 | bytes 10617856 | tf_op jit(solution)/shard_map/far/pallas_call | solution.py:512
  20.7 4.6 %collective-permute-start.3 = (bf16[4,288,128]{2,1,0:T(8,128)(2,1)S(1)}, bf16[4,288,128]{2,1,0:T(8,128)(2,1)S(1)}, u32[]{:S(2)}, u32[]{:S(2)}) collective-permute-start(bf16[4,288,128]{2,1,0:T(8,128)(2,1)S(1)} %get-tuple-element.43), channel_id=1, source_target_pairs={{0,127},{1,2},{2,1},{3,4},{4,3},{5,6},{6,5},{7,8},{8,7},{9,10},{10... | collective-permute-start | bytes 884744 | tf_op jit(solution)/shard_map/ppermute | solution.py:487
  25.3 0.0 collective-permute-done.1.off_ref
  25.4 0.0 collective-permute-start.4
  25.4 0.0 collective-permute-done.2.on_ref
  25.4 2.6 %near.1 = (f32[4,720,128]{2,1,0:T(8,128)S(1)}, f32[4,720,128]{2,1,0:T(8,128)S(1)}, bf16[4,720,128]{2,1,0:T(8,128)(2,1)S(1)}, bf16[256,256]{1,0:T(8,128)(2,1)S(1)...) custom-call(f32[4,720,128]{2,1,0:T(8,128)S(1)} %get-tuple-element.29.state_ref, ...), custom_call_target="tpu_custom_call" | custom-call | flops 3019898880 | bytes 5824512 | tf_op jit(solution)/shard_map/near/pallas_call | solution.py:512
  27.9 2.1 %collective-permute-done.5.off_ref = bf16[4,432,128]{2,1,0:T(8,128)(2,1)S(1)} collective-permute-done((bf16[4,432,128]{2,1,0:T(8,128)(2,1)S(1)}, bf16[4,432,128]{2,1,0:T(8,128)(2,1)S(1)}, u32[]{:S(2)}, u32[]{:S(2)}) %collective-permute-start.5) | collective-permute-done | bytes 442400 | tf_op jit(solution)/shard_map/ppermute | solution.py:487
  30.0 0.0 collective-permute-done.6.on_ref
  30.0 4.1 %advance.2 = (f32[4,720,128]{2,1,0:T(8,128)}, bf16[4,720,128]{2,1,0:T(8,128)(2,1)}) custom-call(f32[4,432,128]{2,1,0:T(8,128)S(1)} %get-tuple-element.48.ahead_ref, f32[4,720,128]{2,1,0:T(8,128)S(1)} %get-tuple-element.39.add_ref, f32[4,720,128]{2,1,0:T(8,128)S(1)} %get-tuple-element.40.near_ref, bf16[4,720,128]{2,1,0:T(8,128)(2,1)S(1)} %get-tuple-element.41.near_prev_ref, ...), custom_call_target="tpu_custom_call" | custom-call | flops 5662310400 | bytes 14303232 | tf_op jit(solution)/shard_map/advance/pallas_call | solution.py:512
  34.2 0.0 collective-permute-done.3.off_ref
  34.2 0.0 collective-permute-done.4.on_ref
  34.2 3.0 %advance.3 = (f32[4,720,128]{2,1,0:T(8,128)}, bf16[4,720,128]{2,1,0:T(8,128)(2,1)}) custom-call(f32[4,288,128]{2,1,0:T(8,128)S(1)} %get-tuple-element.36.ahead_ref, f32[4,720,128]{2,1,0:T(8,128)S(1)} %get-tuple-element.39.add_ref, f32[4,720,128]{2,1,0:T(8,128)S(1)} %get-tuple-element.40.near_ref, ...), custom_call_target="tpu_custom_call", output_to_operand_aliasing={{0}: (12, {}), {1}: (13, {})} | custom-call | flops 3774873600 | bytes 17252352 | tf_op jit(solution)/shard_map/advance/pallas_call | solution.py:512
Async XLA Ops:
  0.6 10.8 %copy-start.1 = (bf16[256,256]{1,0:T(8,128)(2,1)S(1)}, bf16[256,256]{1,0:T(8,128)(2,1)}, u32[]{:S(2)}) copy-start(bf16[256,256]{1,0:T(8,128)(2,1)} %constant.2.clone.slope_ref) | copy-start | bytes 393220
  0.6 10.7 %copy-start = (s32[128]{0:T(128)S(1)}, s32[128]{0:T(128)}, u32[]{:S(2)}) copy-start(s32[128]{0:T(128)} %param.11) | copy-start | bytes 1540
  2.8 12.1 %collective-permute-start = (bf16[576,128]{1,0:T(8,128)(2,1)S(1)}, bf16[576,128]{1,0:T(8,128)(2,1)S(1)}, u32[]{:S(2)}, u32[]{:S(2)}) collective-permute-start(bf16[576,128]{1,0:T(8,128)(2,1)S(1)} %get-tuple-element.31.own_ref), channel_id=1, source_target_pairs={{0,64},{1,65},{2,66},{3,67},{4,68},{5,69},{6,70},{7,71},{8,72},{9,... | collective-permute-start | bytes 442376 | tf_op jit(solution)/shard_map/ppermute | solution.py:548
  6.9 18.5 %collective-permute-start.1 = (bf16[3,800,128]{2,1,0:T(8,128)(2,1)S(1)}, bf16[3,800,128]{2,1,0:T(8,128)(2,1)S(1)}, u32[]{:S(2)}, u32[]{:S(2)}) collective-permute-start(bf16[3,800,128]{2,1,0:T(8,128)(2,1)S(1)} %get-tuple-element.37), channel_id=1, source_target_pairs={{0,127},{1,2},{2,1},{3,4},{4,3},{5,6},{6,5},{7,8},{8,7},{9,10},{10... | collective-permute-start | bytes 1843208 | tf_op jit(solution)/shard_map/ppermute | solution.py:487
  11.4 14.0 %collective-permute-start.2 = (bf16[3,800,128]{2,1,0:T(8,128)(2,1)S(1)}, bf16[3,800,128]{2,1,0:T(8,128)(2,1)S(1)}, u32[]{:S(2)}, u32[]{:S(2)}) collective-permute-start(bf16[3,800,128]{2,1,0:T(8,128)(2,1)S(1)} %get-tuple-element.38), channel_id=1, source_target_pairs={{0,1},{1,0},{2,3},{3,2},{4,5},{5,4},{6,7},{7,6},{8,9},{9,8},{10,11... | collective-permute-start | bytes 1843208 | tf_op jit(solution)/shard_map/ppermute | solution.py:487
  16.8 13.2 %collective-permute-start.5 = (bf16[4,432,128]{2,1,0:T(8,128)(2,1)S(1)}, bf16[4,432,128]{2,1,0:T(8,128)(2,1)S(1)}, u32[]{:S(2)}, u32[]{:S(2)}) collective-permute-start(bf16[4,432,128]{2,1,0:T(8,128)(2,1)S(1)} %get-tuple-element.50), channel_id=1, source_target_pairs={{0,127},{1,2},{2,1},{3,4},{4,3},{5,6},{6,5},{7,8},{8,7},{9,10},{10... | collective-permute-start | bytes 1327112 | tf_op jit(solution)/shard_map/ppermute | solution.py:487
  19.5 10.5 %collective-permute-start.6 = (bf16[4,432,128]{2,1,0:T(8,128)(2,1)S(1)}, bf16[4,432,128]{2,1,0:T(8,128)(2,1)S(1)}, u32[]{:S(2)}, u32[]{:S(2)}) collective-permute-start(bf16[4,432,128]{2,1,0:T(8,128)(2,1)S(1)} %get-tuple-element.51), channel_id=1, source_target_pairs={{0,1},{1,0},{2,3},{3,2},{4,5},{5,4},{6,7},{7,6},{8,9},{9,8},{10,11... | collective-permute-start | bytes 1327112 | tf_op jit(solution)/shard_map/ppermute | solution.py:487
  20.7 13.4 %collective-permute-start.3 = (bf16[4,288,128]{2,1,0:T(8,128)(2,1)S(1)}, bf16[4,288,128]{2,1,0:T(8,128)(2,1)S(1)}, u32[]{:S(2)}, u32[]{:S(2)}) collective-permute-start(bf16[4,288,128]{2,1,0:T(8,128)(2,1)S(1)} %get-tuple-element.43), channel_id=1, source_target_pairs={{0,127},{1,2},{2,1},{3,4},{4,3},{5,6},{6,5},{7,8},{8,7},{9,10},{10... | collective-permute-start | bytes 884744 | tf_op jit(solution)/shard_map/ppermute | solution.py:487
  25.4 8.8 %collective-permute-start.4 = (bf16[4,288,128]{2,1,0:T(8,128)(2,1)S(1)}, bf16[4,288,128]{2,1,0:T(8,128)(2,1)S(1)}, u32[]{:S(2)}, u32[]{:S(2)}) collective-permute-start(bf16[4,288,128]{2,1,0:T(8,128)(2,1)S(1)} %get-tuple-element.44), channel_id=1, source_target_pairs={{0,1},{1,0},{2,3},{3,2},{4,5},{5,4},{6,7},{7,6},{8,9},{9,8},{10,11... | collective-permute-start | bytes 884744 | tf_op jit(solution)/shard_map/ppermute | solution.py:487

commit v3 on v2

--- a/solution.py
+++ b/solution.py
@@ -223,27 +223,19 @@
         body(pl.ds(pl.multiple_of(whole, CHUNK), CHUNK), pl.ds(pl.multiple_of(near, CHUNK), CHUNK))
         return carry
 
-    lax.fori_loop(0, count, step, 0)
-
-
-def product_tables(matrices, group, first):
-    lev = 72
-    group = jnp.concatenate([group, group], axis=1)
-    picks = [jnp.broadcast_to(group == first + c, (lev, 2 * LANES)) for c in range(8)]
-    return jnp.concatenate([matrices, matrices], axis=1), picks
-
-
-def chosen_product(tables, pair):
-    matrices, picks = tables
+    lax.fori_loop(0, count, step, 0, unroll=True)
+
+
+def chosen_product(matrices, group, pair):
     lev = pair.shape[0] // 2
     blank = jnp.zeros((LANES - lev, 2 * LANES), jnp.float32)
     pair = jnp.concatenate([pair[:lev], pair[lev:]], axis=1)
     high = pair.astype(jnp.bfloat16).astype(jnp.float32)
     column = jnp.concatenate([high, blank, pair - high, blank], axis=0).astype(jnp.bfloat16)
     product = jnp.dot(matrices, column, preferred_element_type=jnp.float32)
-    chosen = jnp.zeros((lev, 2 * LANES), jnp.float32)
-    for c in range(8):
-        chosen = jnp.where(picks[c], product[c * lev : (c + 1) * lev], chosen)
+    chosen = product[:lev]
+    for c in range(1, matrices.shape[0] // lev):
+        chosen = jnp.where(group == c, product[c * lev : (c + 1) * lev], chosen)
     return jnp.concatenate([chosen[:, :LANES], chosen[:, LANES:]], axis=0)
 
 
@@ -273,56 +265,63 @@
     place = {
         "own": row,
         "near": jnp.where(row < 64, row + LANES, row - LANES),
+        "near turned": jnp.where(row < 64, row - 64, row + 64),
         "outer": jnp.where(row < 64, row - LANES, row + LANES),
+        "outer turned": jnp.where(row < 64, row + LANES + 64, row - LANES - 64),
     }[source]
     for s in range(2):
         total = total + ((place == targets[s : s + 1]) & slots[s]).astype(jnp.float32)
     return total.astype(jnp.bfloat16)
 
 
-def own_kernel(state_ref, prev_ref, wind_ref, target_ref, slope_ref, slot_ref, own_ref, part_ref, next_ref):
+def inner_lanes():
+    quarter = lane_ids() // 32
+    return (quarter == 1) | (quarter == 2)
+
+
+def physics_kernel(
+    first,
+    count,
+    state_ref,
+    prev_ref,
+    wind_ref,
+    target_ref,
+    slope_ref,
+    slot_ref,
+    own_ref,
+    far_ref,
+    tend_ref,
+    ahead_ref,
+    off_ref,
+    on_ref,
+):
     slots, share = point_sets()
     sums = sum_block("own", target_ref[...].astype(jnp.int32) - 32, slots, True)
-    tables = product_tables(own_ref[...], column_group(slot_ref), 0)
-    early = time_step * hermite(0)[0]
+    matrices = jnp.concatenate([own_ref[...], far_ref[...]], axis=0)
+    matrices = jnp.concatenate([matrices, matrices], axis=1)
+    group = column_group(slot_ref)
+    group = jnp.concatenate([group, group], axis=1)
+    inner = inner_lanes()
+    chosen = sides()
+    early, late = (time_step * w for w in hermite(0))
+    early_1, late_1 = (time_step * w for w in hermite(1))
     blow = [-time_step * wind_ref[d] for d in range(2)]
     slope = slope_ref[...]
 
-    def body(at, _):
-        for k in range(PARTS):
-            part_ref[k, at] = chosen_product(tables, state_ref[k, at])
-        state = flat(state_ref[:, at])
+    def body(at, here_at):
+        state, prev = flat(state_ref[:, at]), flat(prev_ref[:, at])
         motion = moved(state, slope, *blow)
         total = jnp.dot(motion, sums, preferred_element_type=jnp.float32)
-        ahead = state + total * share + early * flat(prev_ref[:, at])
-        next_ref[:, at] = ahead.reshape(PARTS, CHUNK, LANES)
-
-    each_chunk(0, state_ref.shape[1] // CHUNK, body)
-
-
-def far_kernel(
-    first, count, state_ref, prev_ref, slot_ref, far_ref, part_ref, next_ref, tend_ref, ahead_ref, off_ref, on_ref
-):
-    group = column_group(slot_ref)
-    here = group < 8
-    tables = product_tables(far_ref[...], group, 8)
-    quarter = lane_ids() // 32
-    inner = (quarter == 1) | (quarter == 2)
-    chosen = sides()
-    late = time_step * hermite(0)[1]
-    early_1, late_1 = (time_step * w for w in hermite(1))
-
-    def body(at, here_at):
+        start = state + total * share + early * prev
         ahead, force = [], []
         for k in range(PARTS):
-            tend = jnp.where(here, part_ref[k, at], chosen_product(tables, state_ref[k, at]))
-            tend = tend.astype(jnp.bfloat16)
+            rows = slice(k * CHUNK, (k + 1) * CHUNK)
+            tend = chosen_product(matrices, group, state_ref[k, at]).astype(jnp.bfloat16)
             tend_ref[k, here_at] = tend
             tend = tend.astype(jnp.float32)
-            ahead.append(next_ref[k, at] + late * tend)
+            ahead.append(start[rows] + late * tend)
             ahead_ref[k, here_at] = ahead[k]
-            forced = early_1 * prev_ref[k, at].astype(jnp.float32) + late_1 * tend
-            force.append(jnp.where(inner, forced, tend))
+            force.append(jnp.where(inner, early_1 * prev[rows] + late_1 * tend, tend))
         off, on = packed_halves(force, chosen)
         for k in range(2):
             middle = jnp.where(inner, ahead[k], pltpu.roll(ahead[k + 2], 64, 1)).astype(jnp.bfloat16)
@@ -345,7 +344,7 @@
     near_ref,
     force_ref,
     sum_ref,
-    outer_sum_ref,
+    edge_sum_ref,
     blow_ref,
 ):
     lev = wind_ref.shape[1]
@@ -370,12 +369,19 @@
     sum_ref[LANES:, :LANES] = sum_block("near", own_t, slots, False)
     sum_ref[:LANES, LANES:] = sum_block("own", near_t, slots, False)
     sum_ref[LANES:, LANES:] = sum_block("near", near_t, slots, True)
-    outer_sum_ref[...] = sum_block("outer", near_t, slots, False)
+    edge_sum_ref[0, :, :LANES] = sum_block("outer", near_t, slots, False)
+    edge_sum_ref[0, :, LANES:] = sum_block("outer turned", near_t, slots, False)
+    edge_sum_ref[1, :, :LANES] = sum_block("near", own_t, slots, False)
+    edge_sum_ref[1, :, LANES:] = sum_block("near turned", own_t, slots, False)
+    inner = inner_lanes()
     off_w, on_w = winds(off_ref), winds(on_ref)
     for d in range(2):
         blow_ref[0, d] = -time_step * wind_ref[d]
-        blow_ref[1, d] = -time_step * jnp.where(chosen, off_w[d], on_w[d])
-        blow_ref[2, d] = -time_step * jnp.where(chosen, on_w[d], off_w[d])
+        near_w = -time_step * jnp.where(chosen, off_w[d], on_w[d])
+        outer_w = -time_step * jnp.where(chosen, on_w[d], off_w[d])
+        blow_ref[1, d] = near_w
+        blow_ref[2, d] = jnp.where(inner, outer_w, pltpu.roll(outer_w, 64, 1))
+        blow_ref[3, d] = jnp.where(inner, pltpu.roll(near_w, 64, 1), near_w)
 
     slope = slope_ref[...]
     early = time_step * hermite(0)[0]
@@ -414,7 +420,7 @@
     on_ref,
     slope_ref,
     sum_ref,
-    outer_sum_ref,
+    edge_sum_ref,
     blow_ref,
     *rest,
 ):
@@ -423,8 +429,7 @@
     tend_copy = pltpu.make_async_copy(tend_ref, tend_hbm.at[:, pl.ds(first * CHUNK, count)], sems.at[0])
     tend_copy.start()
     _, share = point_sets()
-    quarter = lane_ids() // 32
-    inner = (quarter == 1) | (quarter == 2)
+    inner = inner_lanes()
     chosen = sides()
     slope, sums = slope_ref[...], sum_ref[...]
     weights = [tuple(time_step * w for w in hermite(s)) for s in range(SUBSTEPS)]
@@ -435,38 +440,41 @@
     def gather(pieces, matrix):
         return jnp.dot(jnp.concatenate(pieces, axis=1), matrix, preferred_element_type=jnp.float32)
 
-    def middle(value):
-        value = value.reshape(2 * CHUNK, LANES)
-        return jnp.concatenate([value, pltpu.roll(value, 64, 1)], axis=0)
+    def shared(value, which):
+        total = jnp.dot(value, edge_sum_ref[which], preferred_element_type=jnp.float32)
+        return jnp.concatenate([total[:, :LANES], total[:, LANES:]], axis=0)
 
     def body(at, here_at):
         off, on = off_ref[:, here_at].astype(jnp.float32), on_ref[:, here_at].astype(jnp.float32)
-        off_mid, on_mid = middle(off[:2]), middle(on[:2])
+        off_mid, on_mid = flat(off[:2]), flat(on[:2])
+        middle = [jnp.where(chosen, off_mid, on_mid), jnp.where(chosen, on_mid, off_mid)]
+        middle = jnp.concatenate([middle[0], pltpu.roll(middle[1], 64, 1)], axis=0)
+        outer = jnp.where(chosen == inner, on_mid, off_mid)
         received = whole_halves(off[2:], on[2:], chosen)
         own_prev, own_tend = flat(prev_ref[:, at]), flat(tend_ref[:, here_at])
         near_prev = flat(near_prev_ref[:, at])
         own = flat(ahead_ref[:, here_at]) + flat(add_ref[:, at])
         near = flat(near_ref[:, at]) + weights[0][1] * received
-        near = jnp.where(inner, jnp.where(chosen, off_mid, on_mid), near)
-        outer = jnp.where(chosen, on_mid, off_mid)
+        near = jnp.where(inner, middle, near)
         for s in range(1, SUBSTEPS):
             early, late = weights[s]
             own_force = early * own_prev + late * own_tend
-            own_move, near_move = advect(own, 0), advect(near, 1)
+            own_move = advect(own, 0)
             if s == SUBSTEPS - 1:
-                total = gather([own_move, near_move], sums[:, :LANES])
+                half = near.shape[0] // 2
+                near = jnp.where(inner, pltpu.roll(near[half:], 64, 1), near[:half])
+                total = jnp.dot(own_move, sums[:LANES, :LANES], preferred_element_type=jnp.float32)
+                total = total + shared(advect(near, 3), 1)
                 out = own + total * share + own_force
                 out_ref[:, here_at] = out.reshape(PARTS, CHUNK, LANES)
                 break
             near_force = early * near_prev + late * received
-            total = gather([own_move, near_move], sums)
+            total = gather([own_move, advect(near, 1)], sums)
             own = own + total[:, :LANES] * share + own_force
             near_total = total[:, LANES:]
             if s == 1:
                 near_force = jnp.where(inner, received, near_force)
-                near_total = near_total + jnp.dot(
-                    advect(outer, 2), outer_sum_ref[...], preferred_element_type=jnp.float32
-                )
+                near_total = near_total + shared(advect(outer, 2), 0)
             near = near + near_total * share + near_force
 
     copies = []
@@ -547,27 +555,20 @@
     )
     far_matrices = lax.ppermute(matrices, AXES, [(i, i ^ (devices // 2)) for i in range(devices)])
     off, on = exchanged(to_off, to_on)
-    part, next_state = call(
-        own_kernel,
-        (state, prev, wind, targets, slope, slot, matrices),
-        (like(4, f32), like(4, f32)),
-        "own",
-        10,
-    )
     halves = []
     first = 0
     for count in SPLIT:
         size = count * CHUNK
         tend, ahead, to_off, to_on = call(
-            functools.partial(far_kernel, first, count),
-            (state, prev, slot, far_matrices, part, next_state),
+            functools.partial(physics_kernel, first, count),
+            (state, prev, wind, targets, slope, slot, matrices, far_matrices),
             (like(4, bf16, size), like(4, f32, size), like(4, bf16, size), like(4, bf16, size)),
-            "far",
-            2 * count,
+            "physics",
+            5 * count,
         )
         halves.append((first, count, tend, ahead, exchanged(to_off, to_on)))
         first += count
-    add, near, near_prev, sums, outer_sums, blow = call(
+    add, near, near_prev, sums, edge_sums, blow = call(
         near_kernel,
         (state, wind, targets, slope, off, on),
         (
@@ -575,15 +576,15 @@
             like(4, f32),
             like(4, bf16),
             table(bf16, 2 * LANES, 2 * LANES),
-            table(bf16, LANES, LANES),
-            table(f32, 3, 2, lev, LANES),
+            table(bf16, 2, LANES, 2 * LANES),
+            table(f32, 4, 2, lev, LANES),
         ),
         "near",
         8,
     )
     done = ()
     for first, count, tend, ahead, (off, on) in halves:
-        ins = (ahead, add, near, near_prev, prev, tend, off, on, slope, sums, outer_sums, blow)
+        ins = (ahead, add, near, near_prev, prev, tend, off, on, slope, sums, edge_sums, blow)
         done = call(
             functools.partial(advance_kernel, first),
             ins + done,

time: 37.3 us -> 37.4 us (level)
  Pallas kernels: 18.4 us -> 15.9 us
  waiting for transfers between devices: 2.12 us -> 4.17 us
  starting transfers between devices: 15.9 us -> 16.3 us
    pallas_call x7 -> x6, Pallas kernels: 18.4 us -> 15.9 us  [call(): pl.pallas_call(body, out_shape=outs, compiler_params=params, cost_estimat...]
    ppermute x6, waiting for transfers between devices: 2.12 us -> 4.17 us  [exchanged(): return (lax.ppermute(off, AXES, across), lax.ppermute(on, AXES, inside))]
    ppermute x6, starting transfers between devices: 11.9 us -> 12.3 us  [exchanged(): return (lax.ppermute(off, AXES, across), lax.ppermute(on, AXES, inside))]
  transfers between devices with their start and end apart: 7 -> 7, of which waited for: 1 -> 2; matrix products, arithmetic and copies ran while one was open for 0% -> 0% of each run, Pallas kernels for 36% -> 29%
where the time goes in v3:
time: 37.4 us; the launch traced here: 37.2 us
  starting transfers between devices  16.3 us (44%)
  Pallas kernels  15.9 us (43%)
  waiting for transfers between devices  4.17 us (11%)
  between operations  0.86 us (2%)
    pallas_call x6, Pallas kernels, call(): pl.pallas_call(body, out_shape=outs, compiler_params=params, cost_estimat...  15.9 us
    ppermute x6, starting transfers between devices, exchanged(): return (lax.ppermute(off, AXES, across), lax.ppermute(on, AXES, inside))  12.3 us
    ppermute x6, waiting for transfers between devices, exchanged(): return (lax.ppermute(off, AXES, across), lax.ppermute(on, AXES, inside))  4.17 us
    ppermute x1, starting transfers between devices, per_device(): lax.ppermute(matrices, AXES, [(i, i ^ devices // 2) for i in range(device...  4.04 us
  transfers between devices with their start and end apart: 7, of which 2 were waited for; matrix products, arithmetic and copies ran while one was open for 0% of the time, Pallas kernels for 29%

profile of v3, /device:TPU:0, one launch (start us, length us, event | category | flops | bytes accessed | tf_op | source)
XLA Modules:
  0.0 37.2 jit_solution(5491469315901135756)
XLA Ops:
  0.6 0.0 copy-start.1
  0.6 0.0 copy-start
  0.7 2.2 %pack.1 = (bf16[576,128]{1,0:T(8,128)(2,1)S(1)}, bf16[3,800,128]{2,1,0:T(8,128)(2,1)S(1)}, bf16[3,800,128]{2,1,0:T(8,128)(2,1)S(1)}, f32[8,128]{1,0:T(8,128)S(1)...) custom-call(f32[8,72,72]{2,1,0:T(8,128)} %inverse_hbm.1, ...), custom_call_target="tpu_custom_call" | custom-call | flops 754974720 | bytes 4903424 | tf_op jit(solution)/shard_map/pack/pallas_call | solution.py:520
  2.8 4.0 %collective-permute-start = (bf16[576,128]{1,0:T(8,128)(2,1)S(1)}, bf16[576,128]{1,0:T(8,128)(2,1)S(1)}, u32[]{:S(2)}, u32[]{:S(2)}) collective-permute-start(bf16[576,128]{1,0:T(8,128)(2,1)S(1)} %get-tuple-element.31.own_ref), channel_id=1, source_target_pairs={{0,64},{1,65},{2,66},{3,67},{4,68},{5,69},{6,70},{7,71},{8,72},{9,... | collective-permute-start | bytes 442376 | tf_op jit(solution)/shard_map/ppermute | solution.py:556
  6.9 4.5 %collective-permute-start.1 = (bf16[3,800,128]{2,1,0:T(8,128)(2,1)S(1)}, bf16[3,800,128]{2,1,0:T(8,128)(2,1)S(1)}, u32[]{:S(2)}, u32[]{:S(2)}) collective-permute-start(bf16[3,800,128]{2,1,0:T(8,128)(2,1)S(1)} %get-tuple-element.33), channel_id=1, source_target_pairs={{0,127},{1,2},{2,1},{3,4},{4,3},{5,6},{6,5},{7,8},{8,7},{9,10},{10... | collective-permute-start | bytes 1843208 | tf_op jit(solution)/shard_map/ppermute | solution.py:495
  11.4 0.0 collective-permute-start.2
  11.4 0.0 collective-permute-done.far_ref
  11.4 0.0 copy-done.1
  11.4 0.0 copy-done
  11.4 2.9 %physics.3 = (bf16[4,432,128]{2,1,0:T(8,128)(2,1)S(1)}, f32[4,432,128]{2,1,0:T(8,128)S(1)}, bf16[4,432,128]{2,1,0:T(8,128)(2,1)S(1)}, bf16[4,432,128]{2,1,0:T(8,128)(2,1)S(1)}) custom-call(f32[4,720,128]{2,1,0:T(8,128)S(1)} %get-tuple-element.27.state_ref, bf16[4,720,128]{2,1,0:T(8,128)(2,1)S(1)} %get-tuple-element.28.prev_ref, ...), custom_call_target="tpu_custom_call" | custom-call | flops 5662310400 | bytes 5432320 | tf_op jit(solution)/shard_map/physics/pallas_call | solution.py:520
  14.3 6.0 %collective-permute-start.5 = (bf16[4,432,128]{2,1,0:T(8,128)(2,1)S(1)}, bf16[4,432,128]{2,1,0:T(8,128)(2,1)S(1)}, u32[]{:S(2)}, u32[]{:S(2)}) collective-permute-start(bf16[4,432,128]{2,1,0:T(8,128)(2,1)S(1)} %get-tuple-element.46), channel_id=1, source_target_pairs={{0,127},{1,2},{2,1},{3,4},{4,3},{5,6},{6,5},{7,8},{8,7},{9,10},{10... | collective-permute-start | bytes 1327112 | tf_op jit(solution)/shard_map/ppermute | solution.py:495
  20.3 0.0 collective-permute-start.6
  20.3 2.1 %physics.2 = (bf16[4,288,128]{2,1,0:T(8,128)(2,1)S(1)}, f32[4,288,128]{2,1,0:T(8,128)S(1)}, bf16[4,288,128]{2,1,0:T(8,128)(2,1)S(1)}, bf16[4,288,128]{2,1,0:T(8,128)(2,1)S(1)}) custom-call(f32[4,720,128]{2,1,0:T(8,128)S(1)} %get-tuple-element.27.state_ref, bf16[4,720,128]{2,1,0:T(8,128)(2,1)S(1)} %get-tuple-element.28.prev_ref, ...), custom_call_target="tpu_custom_call" | custom-call | flops 3774873600 | bytes 5432320 | tf_op jit(solution)/shard_map/physics/pallas_call | solution.py:520
  22.4 1.7 %collective-permute-start.3 = (bf16[4,288,128]{2,1,0:T(8,128)(2,1)S(1)}, bf16[4,288,128]{2,1,0:T(8,128)(2,1)S(1)}, u32[]{:S(2)}, u32[]{:S(2)}) collective-permute-start(bf16[4,288,128]{2,1,0:T(8,128)(2,1)S(1)} %get-tuple-element.39), channel_id=1, source_target_pairs={{0,127},{1,2},{2,1},{3,4},{4,3},{5,6},{6,5},{7,8},{8,7},{9,10},{10... | collective-permute-start | bytes 884744 | tf_op jit(solution)/shard_map/ppermute | solution.py:495
  24.1 0.0 collective-permute-done.1.off_ref
  24.1 0.0 collective-permute-start.4
  24.1 0.0 collective-permute-done.2.on_ref
  24.1 1.7 %near.1 = (f32[4,720,128]{2,1,0:T(8,128)S(1)}, f32[4,720,128]{2,1,0:T(8,128)S(1)}, bf16[4,720,128]{2,1,0:T(8,128)(2,1)S(1)}, bf16[256,256]{1,0:T(8,128)(2,1)S(1)...) custom-call(f32[4,720,128]{2,1,0:T(8,128)S(1)} %get-tuple-element.27.state_ref, ...), custom_call_target="tpu_custom_call" | custom-call | flops 3019898880 | bytes 5824512 | tf_op jit(solution)/shard_map/near/pallas_call | solution.py:520
  25.9 1.7 %collective-permute-done.5.off_ref = bf16[4,432,128]{2,1,0:T(8,128)(2,1)S(1)} collective-permute-done((bf16[4,432,128]{2,1,0:T(8,128)(2,1)S(1)}, bf16[4,432,128]{2,1,0:T(8,128)(2,1)S(1)}, u32[]{:S(2)}, u32[]{:S(2)}) %collective-permute-start.5) | collective-permute-done | bytes 442400 | tf_op jit(solution)/shard_map/ppermute | solution.py:495
  27.6 0.0 collective-permute-done.6.on_ref
  27.6 4.0 %advance.2 = (f32[4,720,128]{2,1,0:T(8,128)}, bf16[4,720,128]{2,1,0:T(8,128)(2,1)}) custom-call(f32[4,432,128]{2,1,0:T(8,128)S(1)} %get-tuple-element.44.ahead_ref, f32[4,720,128]{2,1,0:T(8,128)S(1)} %get-tuple-element.35.add_ref, f32[4,720,128]{2,1,0:T(8,128)S(1)} %get-tuple-element.36.near_ref, bf16[4,720,128]{2,1,0:T(8,128)(2,1)S(1)} %get-tuple-element.37.near_prev_ref, ...), custom_call_target="tpu_custom_call" | custom-call | flops 5662310400 | bytes 14647296 | tf_op jit(solution)/shard_map/advance/pallas_call | solution.py:520
  31.6 2.4 %collective-permute-done.3.off_ref = bf16[4,288,128]{2,1,0:T(8,128)(2,1)S(1)} collective-permute-done((bf16[4,288,128]{2,1,0:T(8,128)(2,1)S(1)}, bf16[4,288,128]{2,1,0:T(8,128)(2,1)S(1)}, u32[]{:S(2)}, u32[]{:S(2)}) %collective-permute-start.3) | collective-permute-done | bytes 294944 | tf_op jit(solution)/shard_map/ppermute | solution.py:495
  34.1 0.0 collective-permute-done.4.on_ref
  34.1 3.0 %advance.3 = (f32[4,720,128]{2,1,0:T(8,128)}, bf16[4,720,128]{2,1,0:T(8,128)(2,1)}) custom-call(f32[4,288,128]{2,1,0:T(8,128)S(1)} %get-tuple-element.32.ahead_ref, f32[4,720,128]{2,1,0:T(8,128)S(1)} %get-tuple-element.35.add_ref, f32[4,720,128]{2,1,0:T(8,128)S(1)} %get-tuple-element.36.near_ref, ...), custom_call_target="tpu_custom_call", output_to_operand_aliasing={{0}: (12, {}), {1}: (13, {})} | custom-call | flops 3774873600 | bytes 17596416 | tf_op jit(solution)/shard_map/advance/pallas_call | solution.py:520
Async XLA Ops:
  0.6 10.8 %copy-start.1 = (bf16[256,256]{1,0:T(8,128)(2,1)S(1)}, bf16[256,256]{1,0:T(8,128)(2,1)}, u32[]{:S(2)}) copy-start(bf16[256,256]{1,0:T(8,128)(2,1)} %constant.2.clone.slope_ref) | copy-start | bytes 393220
  0.6 10.8 %copy-start = (s32[128]{0:T(128)S(1)}, s32[128]{0:T(128)}, u32[]{:S(2)}) copy-start(s32[128]{0:T(128)} %param.11) | copy-start | bytes 1540
  2.8 8.6 %collective-permute-start = (bf16[576,128]{1,0:T(8,128)(2,1)S(1)}, bf16[576,128]{1,0:T(8,128)(2,1)S(1)}, u32[]{:S(2)}, u32[]{:S(2)}) collective-permute-start(bf16[576,128]{1,0:T(8,128)(2,1)S(1)} %get-tuple-element.31.own_ref), channel_id=1, source_target_pairs={{0,64},{1,65},{2,66},{3,67},{4,68},{5,69},{6,70},{7,71},{8,72},{9,... | collective-permute-start | bytes 442376 | tf_op jit(solution)/shard_map/ppermute | solution.py:556
  6.9 17.3 %collective-permute-start.1 = (bf16[3,800,128]{2,1,0:T(8,128)(2,1)S(1)}, bf16[3,800,128]{2,1,0:T(8,128)(2,1)S(1)}, u32[]{:S(2)}, u32[]{:S(2)}) collective-permute-start(bf16[3,800,128]{2,1,0:T(8,128)(2,1)S(1)} %get-tuple-element.33), channel_id=1, source_target_pairs={{0,127},{1,2},{2,1},{3,4},{4,3},{5,6},{6,5},{7,8},{8,7},{9,10},{10... | collective-permute-start | bytes 1843208 | tf_op jit(solution)/shard_map/ppermute | solution.py:495
  11.4 12.8 %collective-permute-start.2 = (bf16[3,800,128]{2,1,0:T(8,128)(2,1)S(1)}, bf16[3,800,128]{2,1,0:T(8,128)(2,1)S(1)}, u32[]{:S(2)}, u32[]{:S(2)}) collective-permute-start(bf16[3,800,128]{2,1,0:T(8,128)(2,1)S(1)} %get-tuple-element.34), channel_id=1, source_target_pairs={{0,1},{1,0},{2,3},{3,2},{4,5},{5,4},{6,7},{7,6},{8,9},{9,8},{10,11... | collective-permute-start | bytes 1843208 | tf_op jit(solution)/shard_map/ppermute | solution.py:495
  14.3 13.2 %collective-permute-start.5 = (bf16[4,432,128]{2,1,0:T(8,128)(2,1)S(1)}, bf16[4,432,128]{2,1,0:T(8,128)(2,1)S(1)}, u32[]{:S(2)}, u32[]{:S(2)}) collective-permute-start(bf16[4,432,128]{2,1,0:T(8,128)(2,1)S(1)} %get-tuple-element.46), channel_id=1, source_target_pairs={{0,127},{1,2},{2,1},{3,4},{4,3},{5,6},{6,5},{7,8},{8,7},{9,10},{10... | collective-permute-start | bytes 1327112 | tf_op jit(solution)/shard_map/ppermute | solution.py:495
  20.3 7.2 %collective-permute-start.6 = (bf16[4,432,128]{2,1,0:T(8,128)(2,1)S(1)}, bf16[4,432,128]{2,1,0:T(8,128)(2,1)S(1)}, u32[]{:S(2)}, u32[]{:S(2)}) collective-permute-start(bf16[4,432,128]{2,1,0:T(8,128)(2,1)S(1)} %get-tuple-element.47), channel_id=1, source_target_pairs={{0,1},{1,0},{2,3},{3,2},{4,5},{5,4},{6,7},{7,6},{8,9},{9,8},{10,11... | collective-permute-start | bytes 1327112 | tf_op jit(solution)/shard_map/ppermute | solution.py:495
  22.4 11.7 %collective-permute-start.3 = (bf16[4,288,128]{2,1,0:T(8,128)(2,1)S(1)}, bf16[4,288,128]{2,1,0:T(8,128)(2,1)S(1)}, u32[]{:S(2)}, u32[]{:S(2)}) collective-permute-start(bf16[4,288,128]{2,1,0:T(8,128)(2,1)S(1)} %get-tuple-element.39), channel_id=1, source_target_pairs={{0,127},{1,2},{2,1},{3,4},{4,3},{5,6},{6,5},{7,8},{8,7},{9,10},{10... | collective-permute-start | bytes 884744 | tf_op jit(solution)/shard_map/ppermute | solution.py:495
  24.1 9.9 %collective-permute-start.4 = (bf16[4,288,128]{2,1,0:T(8,128)(2,1)S(1)}, bf16[4,288,128]{2,1,0:T(8,128)(2,1)S(1)}, u32[]{:S(2)}, u32[]{:S(2)}) collective-permute-start(bf16[4,288,128]{2,1,0:T(8,128)(2,1)S(1)} %get-tuple-element.40), channel_id=1, source_target_pairs={{0,1},{1,0},{2,3},{3,2},{4,5},{5,4},{6,7},{7,6},{8,9},{9,8},{10,11... | collective-permute-start | bytes 884744 | tf_op jit(solution)/shard_map/ppermute | solution.py:495

commit v4 on v3

--- a/solution.py
+++ b/solution.py
@@ -226,17 +226,21 @@
     lax.fori_loop(0, count, step, 0, unroll=True)
 
 
-def chosen_product(matrices, group, pair):
+def chosen_product(matrices, group, pair, chosen=None, first=0):
     lev = pair.shape[0] // 2
     blank = jnp.zeros((LANES - lev, 2 * LANES), jnp.float32)
     pair = jnp.concatenate([pair[:lev], pair[lev:]], axis=1)
     high = pair.astype(jnp.bfloat16).astype(jnp.float32)
     column = jnp.concatenate([high, blank, pair - high, blank], axis=0).astype(jnp.bfloat16)
     product = jnp.dot(matrices, column, preferred_element_type=jnp.float32)
-    chosen = product[:lev]
-    for c in range(1, matrices.shape[0] // lev):
-        chosen = jnp.where(group == c, product[c * lev : (c + 1) * lev], chosen)
-    return jnp.concatenate([chosen[:, :LANES], chosen[:, LANES:]], axis=0)
+    for c in range(matrices.shape[0] // lev):
+        part = product[c * lev : (c + 1) * lev]
+        chosen = part if chosen is None else jnp.where(group == first + c, part, chosen)
+    return chosen
+
+
+def as_rows(pair):
+    return jnp.concatenate([pair[:, :LANES], pair[:, LANES:]], axis=0)
 
 
 def column_group(slot_ref):
@@ -277,6 +281,81 @@
 def inner_lanes():
     quarter = lane_ids() // 32
     return (quarter == 1) | (quarter == 2)
+
+
+class Physics:
+    def __init__(self, slot_ref, matrix_refs):
+        matrices = jnp.concatenate([ref[...] for ref in matrix_refs], axis=0)
+        self.matrices = jnp.concatenate([matrices, matrices], axis=1)
+        group = column_group(slot_ref)
+        self.group = jnp.concatenate([group, group], axis=1)
+        self.inner = inner_lanes()
+        self.chosen = sides()
+
+    def begin(self, wind_ref, target_ref, slope_ref):
+        slots, self.share = point_sets()
+        self.sums = sum_block("own", target_ref[...].astype(jnp.int32) - 32, slots, True)
+        self.blow = [-time_step * wind_ref[d] for d in range(2)]
+        self.slope = slope_ref[...]
+
+    def start(self, state, prev):
+        motion = moved(state, self.slope, *self.blow)
+        total = jnp.dot(motion, self.sums, preferred_element_type=jnp.float32)
+        return state + total * self.share + time_step * hermite(0)[0] * prev
+
+    def finish(self, start, prev, tends, here_at, tend_ref, ahead_ref, off_ref, on_ref):
+        late = time_step * hermite(0)[1]
+        early_1, late_1 = (time_step * w for w in hermite(1))
+        ahead, force = [], []
+        for k, tend in enumerate(tends):
+            tend = tend.astype(jnp.bfloat16)
+            tend_ref[k, here_at] = tend
+            tend = tend.astype(jnp.float32)
+            ahead.append(start[k] + late * tend)
+            ahead_ref[k, here_at] = ahead[k]
+            force.append(jnp.where(self.inner, early_1 * prev[k] + late_1 * tend, tend))
+        off, on = packed_halves(force, self.chosen)
+        for k in range(2):
+            middle = jnp.where(self.inner, ahead[k], pltpu.roll(ahead[k + 2], 64, 1))
+            middle = middle.astype(jnp.bfloat16)
+            off_ref[k, here_at] = middle
+            on_ref[k, here_at] = middle
+            off_ref[2 + k, here_at] = off[k].astype(jnp.bfloat16)
+            on_ref[2 + k, here_at] = on[k].astype(jnp.bfloat16)
+
+
+def own_kernel(
+    first, count, state_ref, prev_ref, wind_ref, target_ref, slope_ref, slot_ref, own_ref, part_ref, start_ref
+):
+    physics = Physics(slot_ref, [own_ref])
+    physics.begin(wind_ref, target_ref, slope_ref)
+    def body(at, here_at):
+        start = physics.start(flat(state_ref[:, at]), flat(prev_ref[:, at]))
+        start_ref[:, here_at] = start.reshape(PARTS, CHUNK, LANES)
+        for k in range(PARTS):
+            chosen = chosen_product(physics.matrices, physics.group, state_ref[k, at])
+            part_ref[k, here_at] = as_rows(chosen)
+
+    each_chunk(first, count, body)
+
+
+def far_kernel(
+    first, count, state_ref, prev_ref, slot_ref, far_ref, part_ref, start_ref, tend_ref, ahead_ref, off_ref, on_ref
+):
+    physics = Physics(slot_ref, [far_ref])
+
+    def body(at, here_at):
+        tends = []
+        for k in range(PARTS):
+            pair = part_ref[k, here_at]
+            lev = pair.shape[0] // 2
+            pair = jnp.concatenate([pair[:lev], pair[lev:]], axis=1)
+            tends.append(as_rows(chosen_product(physics.matrices, physics.group, state_ref[k, at], pair, 8)))
+        start = [start_ref[k, here_at] for k in range(PARTS)]
+        prev = [prev_ref[k, at].astype(jnp.float32) for k in range(PARTS)]
+        physics.finish(start, prev, tends, here_at, tend_ref, ahead_ref, off_ref, on_ref)
+
+    each_chunk(first, count, body)
 
 
 def physics_kernel(
@@ -295,40 +374,18 @@
     off_ref,
     on_ref,
 ):
-    slots, share = point_sets()
-    sums = sum_block("own", target_ref[...].astype(jnp.int32) - 32, slots, True)
-    matrices = jnp.concatenate([own_ref[...], far_ref[...]], axis=0)
-    matrices = jnp.concatenate([matrices, matrices], axis=1)
-    group = column_group(slot_ref)
-    group = jnp.concatenate([group, group], axis=1)
-    inner = inner_lanes()
-    chosen = sides()
-    early, late = (time_step * w for w in hermite(0))
-    early_1, late_1 = (time_step * w for w in hermite(1))
-    blow = [-time_step * wind_ref[d] for d in range(2)]
-    slope = slope_ref[...]
+    physics = Physics(slot_ref, [own_ref, far_ref])
+    physics.begin(wind_ref, target_ref, slope_ref)
 
     def body(at, here_at):
-        state, prev = flat(state_ref[:, at]), flat(prev_ref[:, at])
-        motion = moved(state, slope, *blow)
-        total = jnp.dot(motion, sums, preferred_element_type=jnp.float32)
-        start = state + total * share + early * prev
-        ahead, force = [], []
-        for k in range(PARTS):
-            rows = slice(k * CHUNK, (k + 1) * CHUNK)
-            tend = chosen_product(matrices, group, state_ref[k, at]).astype(jnp.bfloat16)
-            tend_ref[k, here_at] = tend
-            tend = tend.astype(jnp.float32)
-            ahead.append(start[rows] + late * tend)
-            ahead_ref[k, here_at] = ahead[k]
-            force.append(jnp.where(inner, early_1 * prev[rows] + late_1 * tend, tend))
-        off, on = packed_halves(force, chosen)
-        for k in range(2):
-            middle = jnp.where(inner, ahead[k], pltpu.roll(ahead[k + 2], 64, 1)).astype(jnp.bfloat16)
-            off_ref[k, here_at] = middle
-            on_ref[k, here_at] = middle
-            off_ref[2 + k, here_at] = off[k].astype(jnp.bfloat16)
-            on_ref[2 + k, here_at] = on[k].astype(jnp.bfloat16)
+        start = physics.start(flat(state_ref[:, at]), flat(prev_ref[:, at]))
+        start = [start[k * CHUNK : (k + 1) * CHUNK] for k in range(PARTS)]
+        prev = [prev_ref[k, at].astype(jnp.float32) for k in range(PARTS)]
+        tends = [
+            as_rows(chosen_product(physics.matrices, physics.group, state_ref[k, at]))
+            for k in range(PARTS)
+        ]
+        physics.finish(start, prev, tends, here_at, tend_ref, ahead_ref, off_ref, on_ref)
 
     each_chunk(first, count, body)
 
@@ -557,14 +614,25 @@
     off, on = exchanged(to_off, to_on)
     halves = []
     first = 0
+    shared = (wind, targets, slope, slot, matrices)
     for count in SPLIT:
         size = count * CHUNK
+        outs = (like(4, bf16, size), like(4, f32, size), like(4, bf16, size), like(4, bf16, size))
+        if first == 0:
+            part, start = call(
+                functools.partial(own_kernel, first, count),
+                (state, prev) + shared,
+                (like(4, f32, size), like(4, f32, size)),
+                "own",
+                3 * count,
+            )
+            ins = (state, prev, slot, far_matrices, part, start)
+            body, name = far_kernel, "far"
+        else:
+            ins = (state, prev) + shared + (far_matrices,)
+            body, name = physics_kernel, "physics"
         tend, ahead, to_off, to_on = call(
-            functools.partial(physics_kernel, first, count),
-            (state, prev, wind, targets, slope, slot, matrices, far_matrices),
-            (like(4, bf16, size), like(4, f32, size), like(4, bf16, size), like(4, bf16, size)),
-            "physics",
-            5 * count,
+            functools.partial(body, first, count), ins, outs, name, 5 * count
         )
         halves.append((first, count, tend, ahead, exchanged(to_off, to_on)))
         first += count

time: 37.4 us -> 35.8 us (0.957)
  waiting for transfers between devices: 4.17 us -> 2.74 us
  starting transfers between devices: 16.3 us -> 15.9 us
    ppermute x6, waiting for transfers between devices: 4.17 us -> 2.73 us  [exchanged(): return (lax.ppermute(off, AXES, across), lax.ppermute(on, AXES, inside))]
    ppermute x6, starting transfers between devices: 12.3 us -> 11.9 us  [exchanged(): return (lax.ppermute(off, AXES, across), lax.ppermute(on, AXES, inside))]
    pallas_call x6 -> x7, Pallas kernels: 15.9 us -> 16.1 us  [call(): pl.pallas_call(body, out_shape=outs, compiler_params=params, cost_estimat...]
  transfers between devices with their start and end apart: 7 -> 7, of which waited for: 2 -> 2; matrix products, arithmetic and copies ran while one was open for 0% -> 0% of each run, Pallas kernels for 29% -> 31%
where the time goes in v4:
time: 35.8 us; the launch traced here: 35.6 us
  Pallas kernels  16.1 us (45%)
  starting transfers between devices  15.9 us (44%)
  waiting for transfers between devices  2.74 us (8%)
  between operations  0.87 us (2%)
    pallas_call x7, Pallas kernels, call(): pl.pallas_call(body, out_shape=outs, compiler_params=params, cost_estimat...  16.1 us
    ppermute x6, starting transfers between devices, exchanged(): return (lax.ppermute(off, AXES, across), lax.ppermute(on, AXES, inside))  11.9 us
    ppermute x1, starting transfers between devices, per_device(): lax.ppermute(matrices, AXES, [(i, i ^ devices // 2) for i in range(device...  4.04 us
    ppermute x6, waiting for transfers between devices, exchanged(): return (lax.ppermute(off, AXES, across), lax.ppermute(on, AXES, inside))  2.73 us
  transfers between devices with their start and end apart: 7, of which 2 were waited for; matrix products, arithmetic and copies ran while one was open for 0% of the time, Pallas kernels for 31%

profile of v4, /device:TPU:0, one launch (start us, length us, event | category | flops | bytes accessed | tf_op | source)
XLA Modules:
  0.0 35.6 jit_solution(13519190815550533379)
XLA Ops:
  0.6 0.0 copy-start.1
  0.6 0.0 copy-start
  0.7 2.2 %pack.1 = (bf16[576,128]{1,0:T(8,128)(2,1)S(1)}, bf16[3,800,128]{2,1,0:T(8,128)(2,1)S(1)}, bf16[3,800,128]{2,1,0:T(8,128)(2,1)S(1)}, f32[8,128]{1,0:T(8,128)S(1)...) custom-call(f32[8,72,72]{2,1,0:T(8,128)} %inverse_hbm.1, ...), custom_call_target="tpu_custom_call" | custom-call | flops 754974720 | bytes 4903424 | tf_op jit(solution)/shard_map/pack/pallas_call | solution.py:577
  2.8 4.0 %collective-permute-start = (bf16[576,128]{1,0:T(8,128)(2,1)S(1)}, bf16[576,128]{1,0:T(8,128)(2,1)S(1)}, u32[]{:S(2)}, u32[]{:S(2)}) collective-permute-start(bf16[576,128]{1,0:T(8,128)(2,1)S(1)} %get-tuple-element.33.own_ref), channel_id=1, source_target_pairs={{0,64},{1,65},{2,66},{3,67},{4,68},{5,69},{6,70},{7,71},{8,72},{9,... | collective-permute-start | bytes 442376 | tf_op jit(solution)/shard_map/ppermute | solution.py:613
  6.9 4.5 %collective-permute-start.1 = (bf16[3,800,128]{2,1,0:T(8,128)(2,1)S(1)}, bf16[3,800,128]{2,1,0:T(8,128)(2,1)S(1)}, u32[]{:S(2)}, u32[]{:S(2)}) collective-permute-start(bf16[3,800,128]{2,1,0:T(8,128)(2,1)S(1)} %get-tuple-element.35), channel_id=1, source_target_pairs={{0,127},{1,2},{2,1},{3,4},{4,3},{5,6},{6,5},{7,8},{8,7},{9,10},{10... | collective-permute-start | bytes 1843208 | tf_op jit(solution)/shard_map/ppermute | solution.py:552
  11.4 0.0 collective-permute-start.2
  11.4 0.0 copy-done.1
  11.4 0.0 copy-done
  11.4 1.8 %own.1 = (f32[4,432,128]{2,1,0:T(8,128)S(1)}, f32[4,432,128]{2,1,0:T(8,128)S(1)}) custom-call(f32[4,720,128]{2,1,0:T(8,128)S(1)} %get-tuple-element.29.state_ref, bf16[4,720,128]{2,1,0:T(8,128)(2,1)S(1)} %get-tuple-element.30.prev_ref, f32[2,72,128]{2,1,0:T(8,128)S(1)} %get-tuple-element.31.wind_ref, f32[8,128]{1,0:T(8,128)S(1)} %get-tuple-element.32.target_ref, ...), custom_call_target="tpu_custom_call" | custom-call | flops 3397386240 | bytes 5137408 | tf_op jit(solution)/shard_map/own/pallas_call | solution.py:577
  13.2 0.0 collective-permute-done.far_ref
  13.2 1.3 %far.1 = (bf16[4,432,128]{2,1,0:T(8,128)(2,1)S(1)}, f32[4,432,128]{2,1,0:T(8,128)S(1)}, bf16[4,432,128]{2,1,0:T(8,128)(2,1)S(1)}, bf16[4,432,128]{2,1,0:T(8,128)(2,1)S(1)}) custom-call(f32[4,720,128]{2,1,0:T(8,128)S(1)} %get-tuple-element.29.state_ref, bf16[4,720,128]{2,1,0:T(8,128)(2,1)S(1)} %get-tuple-element.30.prev_ref, s32[1,128]{1,0:T(1,128)S(1)} %bitcast.6, ...), custom_call_target="tpu_custom_call" | custom-call | flops 5662310400 | bytes 8258560 | tf_op jit(solution)/shard_map/far/pallas_call | solution.py:577
  14.5 4.2 %collective-permute-start.5 = (bf16[4,432,128]{2,1,0:T(8,128)(2,1)S(1)}, bf16[4,432,128]{2,1,0:T(8,128)(2,1)S(1)}, u32[]{:S(2)}, u32[]{:S(2)}) collective-permute-start(bf16[4,432,128]{2,1,0:T(8,128)(2,1)S(1)} %get-tuple-element.50), channel_id=1, source_target_pairs={{0,127},{1,2},{2,1},{3,4},{4,3},{5,6},{6,5},{7,8},{8,7},{9,10},{10... | collective-permute-start | bytes 1327112 | tf_op jit(solution)/shard_map/ppermute | solution.py:552
  18.7 0.0 collective-permute-start.6
  18.7 2.1 %physics.1 = (bf16[4,288,128]{2,1,0:T(8,128)(2,1)S(1)}, f32[4,288,128]{2,1,0:T(8,128)S(1)}, bf16[4,288,128]{2,1,0:T(8,128)(2,1)S(1)}, bf16[4,288,128]{2,1,0:T(8,128)(2,1)S(1)}) custom-call(f32[4,720,128]{2,1,0:T(8,128)S(1)} %get-tuple-element.29.state_ref, bf16[4,720,128]{2,1,0:T(8,128)(2,1)S(1)} %get-tuple-element.30.prev_ref, ...), custom_call_target="tpu_custom_call" | custom-call | flops 3774873600 | bytes 5432320 | tf_op jit(solution)/shard_map/physics/pallas_call | solution.py:577
  20.8 3.1 %collective-permute-start.3 = (bf16[4,288,128]{2,1,0:T(8,128)(2,1)S(1)}, bf16[4,288,128]{2,1,0:T(8,128)(2,1)S(1)}, u32[]{:S(2)}, u32[]{:S(2)}) collective-permute-start(bf16[4,288,128]{2,1,0:T(8,128)(2,1)S(1)} %get-tuple-element.41), channel_id=1, source_target_pairs={{0,127},{1,2},{2,1},{3,4},{4,3},{5,6},{6,5},{7,8},{8,7},{9,10},{10... | collective-permute-start | bytes 884744 | tf_op jit(solution)/shard_map/ppermute | solution.py:552
  23.9 0.0 collective-permute-done.1.off_ref
  23.9 0.0 collective-permute-start.4
  23.9 0.0 collective-permute-done.2.on_ref
  23.9 1.7 %near.1 = (f32[4,720,128]{2,1,0:T(8,128)S(1)}, f32[4,720,128]{2,1,0:T(8,128)S(1)}, bf16[4,720,128]{2,1,0:T(8,128)(2,1)S(1)}, bf16[256,256]{1,0:T(8,128)(2,1)S(1)...) custom-call(f32[4,720,128]{2,1,0:T(8,128)S(1)} %get-tuple-element.29.state_ref, ...), custom_call_target="tpu_custom_call" | custom-call | flops 3019898880 | bytes 5824512 | tf_op jit(solution)/shard_map/near/pallas_call | solution.py:577
  25.7 2.1 %collective-permute-done.5.off_ref = bf16[4,432,128]{2,1,0:T(8,128)(2,1)S(1)} collective-permute-done((bf16[4,432,128]{2,1,0:T(8,128)(2,1)S(1)}, bf16[4,432,128]{2,1,0:T(8,128)(2,1)S(1)}, u32[]{:S(2)}, u32[]{:S(2)}) %collective-permute-start.5) | collective-permute-done | bytes 442400 | tf_op jit(solution)/shard_map/ppermute | solution.py:552
  27.8 0.0 collective-permute-done.6.on_ref
  27.8 4.1 %advance.2 = (f32[4,720,128]{2,1,0:T(8,128)}, bf16[4,720,128]{2,1,0:T(8,128)(2,1)}) custom-call(f32[4,432,128]{2,1,0:T(8,128)S(1)} %get-tuple-element.48.ahead_ref, f32[4,720,128]{2,1,0:T(8,128)S(1)} %get-tuple-element.37.add_ref, f32[4,720,128]{2,1,0:T(8,128)S(1)} %get-tuple-element.38.near_ref, bf16[4,720,128]{2,1,0:T(8,128)(2,1)S(1)} %get-tuple-element.39.near_prev_ref, ...), custom_call_target="tpu_custom_call" | custom-call | flops 5662310400 | bytes 14647296 | tf_op jit(solution)/shard_map/advance/pallas_call | solution.py:577
  31.8 0.6 %collective-permute-done.3.off_ref = bf16[4,288,128]{2,1,0:T(8,128)(2,1)S(1)} collective-permute-done((bf16[4,288,128]{2,1,0:T(8,128)(2,1)S(1)}, bf16[4,288,128]{2,1,0:T(8,128)(2,1)S(1)}, u32[]{:S(2)}, u32[]{:S(2)}) %collective-permute-start.3) | collective-permute-done | bytes 294944 | tf_op jit(solution)/shard_map/ppermute | solution.py:552
  32.5 0.0 collective-permute-done.4.on_ref
  32.5 3.0 %advance.3 = (f32[4,720,128]{2,1,0:T(8,128)}, bf16[4,720,128]{2,1,0:T(8,128)(2,1)}) custom-call(f32[4,288,128]{2,1,0:T(8,128)S(1)} %get-tuple-element.34.ahead_ref, f32[4,720,128]{2,1,0:T(8,128)S(1)} %get-tuple-element.37.add_ref, f32[4,720,128]{2,1,0:T(8,128)S(1)} %get-tuple-element.38.near_ref, ...), custom_call_target="tpu_custom_call", output_to_operand_aliasing={{0}: (12, {}), {1}: (13, {})} | custom-call | flops 3774873600 | bytes 17596416 | tf_op jit(solution)/shard_map/advance/pallas_call | solution.py:577
Async XLA Ops:
  0.6 10.8 %copy-start.1 = (bf16[256,256]{1,0:T(8,128)(2,1)S(1)}, bf16[256,256]{1,0:T(8,128)(2,1)}, u32[]{:S(2)}) copy-start(bf16[256,256]{1,0:T(8,128)(2,1)} %constant.2.clone.slope_ref) | copy-start | bytes 393220
  0.6 10.7 %copy-start = (s32[128]{0:T(128)S(1)}, s32[128]{0:T(128)}, u32[]{:S(2)}) copy-start(s32[128]{0:T(128)} %param.11) | copy-start | bytes 1540
  2.8 10.4 %collective-permute-start = (bf16[576,128]{1,0:T(8,128)(2,1)S(1)}, bf16[576,128]{1,0:T(8,128)(2,1)S(1)}, u32[]{:S(2)}, u32[]{:S(2)}) collective-permute-start(bf16[576,128]{1,0:T(8,128)(2,1)S(1)} %get-tuple-element.33.own_ref), channel_id=1, source_target_pairs={{0,64},{1,65},{2,66},{3,67},{4,68},{5,69},{6,70},{7,71},{8,72},{9,... | collective-permute-start | bytes 442376 | tf_op jit(solution)/shard_map/ppermute | solution.py:613
  6.9 17.1 %collective-permute-start.1 = (bf16[3,800,128]{2,1,0:T(8,128)(2,1)S(1)}, bf16[3,800,128]{2,1,0:T(8,128)(2,1)S(1)}, u32[]{:S(2)}, u32[]{:S(2)}) collective-permute-start(bf16[3,800,128]{2,1,0:T(8,128)(2,1)S(1)} %get-tuple-element.35), channel_id=1, source_target_pairs={{0,127},{1,2},{2,1},{3,4},{4,3},{5,6},{6,5},{7,8},{8,7},{9,10},{10... | collective-permute-start | bytes 1843208 | tf_op jit(solution)/shard_map/ppermute | solution.py:552
  11.4 12.6 %collective-permute-start.2 = (bf16[3,800,128]{2,1,0:T(8,128)(2,1)S(1)}, bf16[3,800,128]{2,1,0:T(8,128)(2,1)S(1)}, u32[]{:S(2)}, u32[]{:S(2)}) collective-permute-start(bf16[3,800,128]{2,1,0:T(8,128)(2,1)S(1)} %get-tuple-element.36), channel_id=1, source_target_pairs={{0,1},{1,0},{2,3},{3,2},{4,5},{5,4},{6,7},{7,6},{8,9},{9,8},{10,11... | collective-permute-start | bytes 1843208 | tf_op jit(solution)/shard_map/ppermute | solution.py:552
  14.5 13.2 %collective-permute-start.5 = (bf16[4,432,128]{2,1,0:T(8,128)(2,1)S(1)}, bf16[4,432,128]{2,1,0:T(8,128)(2,1)S(1)}, u32[]{:S(2)}, u32[]{:S(2)}) collective-permute-start(bf16[4,432,128]{2,1,0:T(8,128)(2,1)S(1)} %get-tuple-element.50), channel_id=1, source_target_pairs={{0,127},{1,2},{2,1},{3,4},{4,3},{5,6},{6,5},{7,8},{8,7},{9,10},{10... | collective-permute-start | bytes 1327112 | tf_op jit(solution)/shard_map/ppermute | solution.py:552
  18.7 9.0 %collective-permute-start.6 = (bf16[4,432,128]{2,1,0:T(8,128)(2,1)S(1)}, bf16[4,432,128]{2,1,0:T(8,128)(2,1)S(1)}, u32[]{:S(2)}, u32[]{:S(2)}) collective-permute-start(bf16[4,432,128]{2,1,0:T(8,128)(2,1)S(1)} %get-tuple-element.51), channel_id=1, source_target_pairs={{0,1},{1,0},{2,3},{3,2},{4,5},{5,4},{6,7},{7,6},{8,9},{9,8},{10,11... | collective-permute-start | bytes 1327112 | tf_op jit(solution)/shard_map/ppermute | solution.py:552
  20.8 11.7 %collective-permute-start.3 = (bf16[4,288,128]{2,1,0:T(8,128)(2,1)S(1)}, bf16[4,288,128]{2,1,0:T(8,128)(2,1)S(1)}, u32[]{:S(2)}, u32[]{:S(2)}) collective-permute-start(bf16[4,288,128]{2,1,0:T(8,128)(2,1)S(1)} %get-tuple-element.41), channel_id=1, source_target_pairs={{0,127},{1,2},{2,1},{3,4},{4,3},{5,6},{6,5},{7,8},{8,7},{9,10},{10... | collective-permute-start | bytes 884744 | tf_op jit(solution)/shard_map/ppermute | solution.py:552
  23.9 8.5 %collective-permute-start.4 = (bf16[4,288,128]{2,1,0:T(8,128)(2,1)S(1)}, bf16[4,288,128]{2,1,0:T(8,128)(2,1)S(1)}, u32[]{:S(2)}, u32[]{:S(2)}) collective-permute-start(bf16[4,288,128]{2,1,0:T(8,128)(2,1)S(1)} %get-tuple-element.42), channel_id=1, source_target_pairs={{0,1},{1,0},{2,3},{3,2},{4,5},{5,4},{6,7},{7,6},{8,9},{9,8},{10,11... | collective-permute-start | bytes 884744 | tf_op jit(solution)/shard_map/ppermute | solution.py:552

commit v5 on v4

--- a/solution.py
+++ b/solution.py
@@ -148,6 +148,29 @@
     return jnp.concatenate([direct, pltpu.roll(turned, 64, 1)], axis=0)
 
 
+def packed_matrices(matrix):
+    lane = lane_ids()
+    half = len(matrix) // 2
+    rows = [jnp.where(lane < 64, matrix[c], pltpu.roll(matrix[c + half], 64, 1)) for c in range(half)]
+    rest = jnp.zeros_like(matrix[0])
+    for c, value in enumerate(matrix):
+        rest = jnp.where(lane // 8 == c, pltpu.roll(value, (8 * c - 64) % LANES, 1), rest)
+    return jnp.concatenate(rows + [rest, jnp.zeros((8, LANES), jnp.float32)], axis=0)
+
+
+def unpacked_matrices(packed):
+    lane = lane_ids()
+    lev, half = 72, 4
+    rest = packed[half * lev : (half + 1) * lev]
+    rows = []
+    for c in range(2 * half):
+        main = packed[c % half * lev : (c % half + 1) * lev]
+        main = main if c < half else pltpu.roll(main, 64, 1)
+        tail = jnp.where(lane < lev, pltpu.roll(rest, (64 - 8 * c) % LANES, 1), 0.0)
+        rows.append(jnp.where(lane < 64, main, tail))
+    return jnp.concatenate(rows, axis=0)
+
+
 def pack_kernel(
     inverse_hbm,
     wind_hbm,
@@ -155,6 +178,7 @@
     state_hbm,
     prev_hbm,
     matrix_ref,
+    packed_ref,
     off_ref,
     on_ref,
     target_ref,
@@ -178,6 +202,7 @@
     blank = jnp.zeros((lev, LANES - lev), jnp.float32)
     matrix = [jnp.concatenate([inverse_ref[c] - eye, blank], axis=1) for c in range(groups)]
     matrix_ref[...] = jnp.concatenate(matrix, axis=0).astype(jnp.bfloat16)
+    packed_ref[...] = packed_matrices(matrix).astype(jnp.bfloat16)
     copies[1].wait()
     copies[2].wait()
     devices = lax.axis_size(AXES)
@@ -185,13 +210,13 @@
     targets = edge_targets(links_ref, lax.axis_index(AXES) * elements, elements * devices)
     target_ref[...] = targets
     end = off_ref.shape[1]
-    filler = jnp.zeros((24, LANES), jnp.float32)
+    filler = jnp.zeros((8, LANES), jnp.float32)
     flat_wind = wind_ref[...].reshape(2 * lev, LANES)
     for k in range(3):
         piece = jnp.concatenate([flat_wind[48 * k : 48 * k + 48], targets, filler], axis=0)
         piece = piece.astype(jnp.bfloat16)
-        off_ref[k, end - 80 : end] = piece
-        on_ref[k, end - 80 : end] = piece
+        off_ref[k, end - 64 : end] = piece
+        on_ref[k, end - 64 : end] = piece
     chosen = sides()
     odd = jnp.where(on_odd(), 3, 0)
     quarter = lane_ids() // 32
@@ -285,12 +310,15 @@
 
 class Physics:
     def __init__(self, slot_ref, matrix_refs):
-        matrices = jnp.concatenate([ref[...] for ref in matrix_refs], axis=0)
-        self.matrices = jnp.concatenate([matrices, matrices], axis=1)
+        self.take(jnp.concatenate([ref[...] for ref in matrix_refs], axis=0) if matrix_refs else None)
         group = column_group(slot_ref)
         self.group = jnp.concatenate([group, group], axis=1)
         self.inner = inner_lanes()
         self.chosen = sides()
+
+    def take(self, matrices):
+        if matrices is not None:
+            self.matrices = jnp.concatenate([matrices, matrices], axis=1)
 
     def begin(self, wind_ref, target_ref, slope_ref):
         slots, self.share = point_sets()
@@ -340,9 +368,24 @@
 
 
 def far_kernel(
-    first, count, state_ref, prev_ref, slot_ref, far_ref, part_ref, start_ref, tend_ref, ahead_ref, off_ref, on_ref
+    first,
+    count,
+    state_ref,
+    prev_ref,
+    slot_ref,
+    packed_ref,
+    part_ref,
+    start_ref,
+    tend_ref,
+    ahead_ref,
+    off_ref,
+    on_ref,
+    far_ref,
 ):
-    physics = Physics(slot_ref, [far_ref])
+    physics = Physics(slot_ref, [])
+    matrices = unpacked_matrices(packed_ref[...].astype(jnp.float32)).astype(jnp.bfloat16)
+    far_ref[...] = matrices
+    physics.take(matrices)
 
     def body(at, here_at):
         tends = []
@@ -397,20 +440,17 @@
     slope_ref,
     off_ref,
     on_ref,
-    add_ref,
-    near_ref,
-    force_ref,
-    sum_ref,
-    edge_sum_ref,
-    blow_ref,
+    prev_ref,
+    *rest,
 ):
+    parts, (own_ref, near_ref, near_add_ref, force_ref, sum_ref, edge_sum_ref, blow_ref) = rest[:-7], rest[-7:]
     lev = wind_ref.shape[1]
     slots, share = point_sets()
     chosen = sides()
     end = off_ref.shape[1]
 
     def extra(ref, k):
-        return ref[k, end - 80 : end].astype(jnp.float32)
+        return ref[k, end - 64 : end].astype(jnp.float32)
 
     def winds(ref):
         whole = jnp.concatenate([extra(ref, k)[:48] for k in range(3)], axis=0)
@@ -422,14 +462,21 @@
     own_t = target_ref[...].astype(jnp.int32) - 32
     near_t = jnp.where(chosen, targets(off_ref), targets(on_ref))
     near_t = near_t + jnp.where(lane_ids() < 64, LANES, -LANES)
-    sum_ref[:LANES, :LANES] = sum_block("own", own_t, slots, True)
-    sum_ref[LANES:, :LANES] = sum_block("near", own_t, slots, False)
-    sum_ref[:LANES, LANES:] = sum_block("own", near_t, slots, False)
-    sum_ref[LANES:, LANES:] = sum_block("near", near_t, slots, True)
-    edge_sum_ref[0, :, :LANES] = sum_block("outer", near_t, slots, False)
-    edge_sum_ref[0, :, LANES:] = sum_block("outer turned", near_t, slots, False)
-    edge_sum_ref[1, :, :LANES] = sum_block("near", own_t, slots, False)
-    edge_sum_ref[1, :, LANES:] = sum_block("near turned", own_t, slots, False)
+    own_sums = jnp.concatenate(
+        [sum_block("own", own_t, slots, True), sum_block("own", near_t, slots, False)], axis=1
+    )
+    near_sums = jnp.concatenate(
+        [sum_block("near", own_t, slots, False), sum_block("near", near_t, slots, True)], axis=1
+    )
+    sum_ref[:LANES] = own_sums
+    sum_ref[LANES:] = near_sums
+    nothing = jnp.zeros((LANES, LANES), jnp.bfloat16)
+    for k, turn in enumerate(("", " turned")):
+        edge_sum_ref[k, :LANES] = near_sums
+        edge_sum_ref[k, LANES:, :LANES] = nothing
+        edge_sum_ref[k, LANES:, LANES:] = sum_block("outer" + turn, near_t, slots, False)
+        edge_sum_ref[2 + k, :LANES, :LANES] = own_sums[:, :LANES]
+        edge_sum_ref[2 + k, LANES:, :LANES] = sum_block("near" + turn, own_t, slots, False)
     inner = inner_lanes()
     off_w, on_w = winds(off_ref), winds(on_ref)
     for d in range(2):
@@ -442,37 +489,49 @@
 
     slope = slope_ref[...]
     early = time_step * hermite(0)[0]
-
-    def body(at, _):
+    early_1, late_1 = (time_step * w for w in hermite(1))
+    own_blow = (blow_ref[0, 0], blow_ref[0, 1])
+    near_blow = (blow_ref[1, 0], blow_ref[1, 1])
+
+    def body(at, here_at, tend_ref, ahead_ref):
         off, on = off_ref[:, at].astype(jnp.float32), on_ref[:, at].astype(jnp.float32)
         near = whole_halves(off[:2], on[:2], chosen)
-        own_move = moved(flat(state_ref[:, at]), slope, blow_ref[0, 0], blow_ref[0, 1])
-        near_move = moved(near, slope, blow_ref[1, 0], blow_ref[1, 1])
-        total = jnp.dot(near_move, sum_ref[LANES:], preferred_element_type=jnp.float32)
+        own_move = moved(flat(state_ref[:, at]), slope, *own_blow)
+        near_move = moved(near, slope, *near_blow)
+        total = jnp.dot(near_move, near_sums, preferred_element_type=jnp.float32)
         near_total = total[:, LANES:] + jnp.dot(
-            own_move, sum_ref[:LANES, LANES:], preferred_element_type=jnp.float32
+            own_move, own_sums[:, LANES:], preferred_element_type=jnp.float32
         )
-        add_ref[:, at] = (total[:, :LANES] * share).reshape(PARTS, CHUNK, LANES)
-        prev = [jnp.where(chosen, off[2], on[2])]
+        kept = [jnp.where(chosen, off[2], on[2])]
         for k in range(1, PARTS):
             turned = [pltpu.roll(side[2], LANES - 32 * k, 1) for side in (off, on)]
-            prev.append(jnp.where(chosen, *turned))
-        prev = jnp.concatenate(prev, axis=0)
-        near = near + near_total * share + early * prev
+            kept.append(jnp.where(chosen, *turned))
+        kept = jnp.concatenate(kept, axis=0)
+        near = near + near_total * share + early * kept
         near_ref[:, at] = near.reshape(PARTS, CHUNK, LANES)
-        force_ref[:, at] = prev.astype(jnp.bfloat16).reshape(PARTS, CHUNK, LANES)
-
-    each_chunk(0, state_ref.shape[1] // CHUNK, body)
+        force_ref[:, at] = kept.astype(jnp.bfloat16).reshape(PARTS, CHUNK, LANES)
+        own = flat(ahead_ref[:, here_at]) + total[:, :LANES] * share
+        total = jnp.dot(moved(own, slope, *own_blow), own_sums, preferred_element_type=jnp.float32)
+        force = early_1 * flat(prev_ref[:, at]) + late_1 * flat(tend_ref[:, here_at])
+        own = own + total[:, :LANES] * share + force
+        own_ref[:, at] = own.reshape(PARTS, CHUNK, LANES)
+        near_add_ref[:, at] = (total[:, LANES:] * share).reshape(PARTS, CHUNK, LANES)
+
+    first = 0
+    for tend_ref, ahead_ref in zip(parts[::2], parts[1::2]):
+        for j, here_at in enumerate(chunks(tend_ref)):
+            body(pl.ds((first + j) * CHUNK, CHUNK), here_at, tend_ref, ahead_ref)
+        first += tend_ref.shape[1] // CHUNK
 
 
 def advance_kernel(
     first,
-    ahead_ref,
-    add_ref,
+    last,
+    own_ref,
     near_ref,
+    near_add_ref,
     near_prev_ref,
     prev_ref,
-    tend_ref,
     off_ref,
     on_ref,
     slope_ref,
@@ -481,14 +540,22 @@
     blow_ref,
     *rest,
 ):
-    out_hbm, tend_hbm, out_ref, sems = rest[-4:]
-    count = tend_ref.shape[1]
-    tend_copy = pltpu.make_async_copy(tend_ref, tend_hbm.at[:, pl.ds(first * CHUNK, count)], sems.at[0])
-    tend_copy.start()
+    if last:
+        tend_ref, done_ref, out_hbm, out_ref, sems = rest
+        copies = [pltpu.make_async_copy(done_ref, out_hbm.at[:, pl.ds(0, done_ref.shape[1])], sems.at[0])]
+    else:
+        *tend_refs, out_ref, tend_hbm, sems = rest
+        tend_ref = tend_refs[0]
+        copies, row = [], 0
+        for k, ref in enumerate(tend_refs):
+            copies.append(pltpu.make_async_copy(ref, tend_hbm.at[:, pl.ds(row, ref.shape[1])], sems.at[k]))
+            row += ref.shape[1]
+    for copy in copies:
+        copy.start()
     _, share = point_sets()
     inner = inner_lanes()
     chosen = sides()
-    slope, sums = slope_ref[...], sum_ref[...]
+    slope = slope_ref[...]
     weights = [tuple(time_step * w for w in hermite(s)) for s in range(SUBSTEPS)]
 
     def advect(value, unit):
@@ -497,9 +564,13 @@
     def gather(pieces, matrix):
         return jnp.dot(jnp.concatenate(pieces, axis=1), matrix, preferred_element_type=jnp.float32)
 
-    def shared(value, which):
-        total = jnp.dot(value, edge_sum_ref[which], preferred_element_type=jnp.float32)
-        return jnp.concatenate([total[:, :LANES], total[:, LANES:]], axis=0)
+    def gather_shared(whole, packed, which, width):
+        half = packed.shape[0]
+        parts = [
+            gather([whole[k * half : (k + 1) * half], packed], edge_sum_ref[which + k, :, :width])
+            for k in range(2)
+        ]
+        return jnp.concatenate(parts, axis=0)
 
     def body(at, here_at):
         off, on = off_ref[:, here_at].astype(jnp.float32), on_ref[:, here_at].astype(jnp.float32)
@@ -510,39 +581,31 @@
         received = whole_halves(off[2:], on[2:], chosen)
         own_prev, own_tend = flat(prev_ref[:, at]), flat(tend_ref[:, here_at])
         near_prev = flat(near_prev_ref[:, at])
-        own = flat(ahead_ref[:, here_at]) + flat(add_ref[:, at])
-        near = flat(near_ref[:, at]) + weights[0][1] * received
-        near = jnp.where(inner, middle, near)
-        for s in range(1, SUBSTEPS):
-            early, late = weights[s]
-            own_force = early * own_prev + late * own_tend
-            own_move = advect(own, 0)
-            if s == SUBSTEPS - 1:
-                half = near.shape[0] // 2
-                near = jnp.where(inner, pltpu.roll(near[half:], 64, 1), near[:half])
-                total = jnp.dot(own_move, sums[:LANES, :LANES], preferred_element_type=jnp.float32)
-                total = total + shared(advect(near, 3), 1)
-                out = own + total * share + own_force
-                out_ref[:, here_at] = out.reshape(PARTS, CHUNK, LANES)
-                break
-            near_force = early * near_prev + late * received
-            total = gather([own_move, advect(near, 1)], sums)
-            own = own + total[:, :LANES] * share + own_force
-            near_total = total[:, LANES:]
-            if s == 1:
-                near_force = jnp.where(inner, received, near_force)
-                near_total = near_total + shared(advect(outer, 2), 0)
-            near = near + near_total * share + near_force
-
-    copies = []
+        early, late = weights[1]
+        near = jnp.where(inner, middle, flat(near_ref[:, at]) + weights[0][1] * received)
+        total = gather_shared(advect(near, 1), advect(outer, 2), 0, 2 * LANES)
+        own = flat(own_ref[:, at]) + total[:, :LANES] * share
+        force = jnp.where(inner, received, early * near_prev + late * received)
+        near = near + total[:, LANES:] * share + flat(near_add_ref[:, at]) + force
+        early, late = weights[2]
+        total = gather([advect(own, 0), advect(near, 1)], sum_ref[...])
+        own = own + total[:, :LANES] * share + (early * own_prev + late * own_tend)
+        near = near + total[:, LANES:] * share + (early * near_prev + late * received)
+        early, late = weights[3]
+        half = near.shape[0] // 2
+        near = jnp.where(inner, pltpu.roll(near[half:], 64, 1), near[:half])
+        total = gather_shared(advect(own, 0), advect(near, 3), 2, LANES)
+        out = own + total * share + (early * own_prev + late * own_tend)
+        out_ref[:, here_at] = out.reshape(PARTS, CHUNK, LANES)
+
     for j, here_at in enumerate(chunks(out_ref)):
         at = pl.ds((first + j) * CHUNK, CHUNK)
         body(at, here_at)
-        copies.append(pltpu.make_async_copy(out_ref.at[:, here_at], out_hbm.at[:, at], sems.at[1 + j]))
-        copies[j].start()
+        if last:
+            copies.append(pltpu.make_async_copy(out_ref.at[:, here_at], out_hbm.at[:, at], sems.at[1 + j]))
+            copies[-1].start()
     for copy in copies:
         copy.wait()
-    tend_copy.wait()
 
 
 def exchanged(off, on):
@@ -580,7 +643,7 @@
 
     slot = swap_slot.reshape(1, LANES)
     slope = jnp.asarray(derivative_matrix())
-    message = like(3, bf16, rows + 80)
+    message = like(3, bf16, rows + 64)
     inputs = (
         inverse,
         wind,
@@ -589,11 +652,12 @@
         prev_tendency.reshape(PARTS, rows, LANES),
     )
     inputs = tuple(pltpu.with_memory_space_constraint(array, pltpu.HBM) for array in inputs)
-    matrices, to_off, to_on, targets, wind, state, prev = call(
+    matrices, packed, to_off, to_on, targets, wind, state, prev = call(
         pack_kernel,
         inputs,
         (
             table(bf16, inverse.shape[0] * lev, LANES),
+            table(bf16, 368, LANES),
             message,
             message,
             table(f32, 8, LANES),
@@ -610,7 +674,7 @@
             pltpu.SemaphoreType.DMA((3 + 2 * PARTS,)),
         ],
     )
-    far_matrices = lax.ppermute(matrices, AXES, [(i, i ^ (devices // 2)) for i in range(devices)])
+    far_packed = lax.ppermute(packed, AXES, [(i, i ^ (devices // 2)) for i in range(devices)])
     off, on = exchanged(to_off, to_on)
     halves = []
     first = 0
@@ -626,51 +690,61 @@
                 "own",
                 3 * count,
             )
-            ins = (state, prev, slot, far_matrices, part, start)
+            ins = (state, prev, slot, far_packed, part, start)
             body, name = far_kernel, "far"
+            outs += (table(bf16, *matrices.shape),)
         else:
             ins = (state, prev) + shared + (far_matrices,)
             body, name = physics_kernel, "physics"
-        tend, ahead, to_off, to_on = call(
+        tend, ahead, to_off, to_on, *more = call(
             functools.partial(body, first, count), ins, outs, name, 5 * count
         )
+        far_matrices = more[0] if more else far_matrices
         halves.append((first, count, tend, ahead, exchanged(to_off, to_on)))
         first += count
-    add, near, near_prev, sums, edge_sums, blow = call(
+    parts = sum(((tend, ahead) for _, _, tend, ahead, _ in halves), ())
+    own, near, near_add, near_prev, sums, edge_sums, blow = call(
         near_kernel,
-        (state, wind, targets, slope, off, on),
+        (state, wind, targets, slope, off, on, prev) + parts,
         (
+            like(4, f32),
             like(4, f32),
             like(4, f32),
             like(4, bf16),
             table(bf16, 2 * LANES, 2 * LANES),
-            table(bf16, 2, LANES, 2 * LANES),
+            table(bf16, 4, 2 * LANES, 2 * LANES),
             table(f32, 4, 2, lev, LANES),
         ),
         "near",
-        8,
+        16,
     )
-    done = ()
-    for first, count, tend, ahead, (off, on) in halves:
-        ins = (ahead, add, near, near_prev, prev, tend, off, on, slope, sums, edge_sums, blow)
-        done = call(
-            functools.partial(advance_kernel, first),
-            ins + done,
-            (
-                jax.ShapeDtypeStruct((PARTS, rows, LANES), f32),
-                jax.ShapeDtypeStruct((PARTS, rows, LANES), bf16),
-            ),
-            "advance",
-            5 * count,
-            in_specs=[inner] * len(ins) + [outer] * len(done),
-            out_specs=(outer, outer),
-            scratch_shapes=[
-                pltpu.VMEM((PARTS, count * CHUNK, LANES), f32),
-                pltpu.SemaphoreType.DMA((1 + count,)),
-            ],
-            input_output_aliases={len(ins) + i: i for i in range(len(done))},
-        )
-    out, tend = done
+    tends = tuple(tend for _, _, tend, _, _ in halves)
+    out_spec = jax.ShapeDtypeStruct((PARTS, rows, LANES), f32)
+    tend_spec = jax.ShapeDtypeStruct((PARTS, rows, LANES), bf16)
+    for part, (first, count, tend, _, (off, on)) in enumerate(halves):
+        ins = (own, near, near_add, near_prev, prev, off, on, slope, sums, edge_sums, blow)
+        size = count * CHUNK
+        if part == 0:
+            done, tend_out = call(
+                functools.partial(advance_kernel, first, False),
+                ins + tends,
+                (like(4, f32, size), tend_spec),
+                "advance",
+                5 * count,
+                out_specs=(inner, outer),
+                scratch_shapes=[pltpu.SemaphoreType.DMA((len(tends),))],
+            )
+        else:
+            (out,) = call(
+                functools.partial(advance_kernel, first, True),
+                ins + (tend, done),
+                (out_spec,),
+                "advance",
+                5 * count,
+                out_specs=(outer,),
+                scratch_shapes=[pltpu.VMEM((PARTS, size, LANES), f32), pltpu.SemaphoreType.DMA((1 + count,))],
+            )
+    tend = tend_out
     return (out.reshape(shape), tend.reshape(shape))
 
 

time: 35.8 us -> 34.8 us (0.972); the launches traced: 35.6 us -> 34.2 us
  waiting for transfers between devices: 2.74 us -> 0.96 us
  Pallas kernels: 16.1 us -> 16.5 us
    ppermute x6, waiting for transfers between devices: 2.73 us -> 0.96 us  [exchanged(): return (lax.ppermute(off, AXES, across), lax.ppermute(on, AXES, inside))]
  transfers between devices with their start and end apart: 7 -> 7, of which waited for: 2 -> 2; matrix products, arithmetic and copies ran while one was open for 0% -> 0% of each run, Pallas kernels for 31% -> 34%
where the time goes in v5:
time: 34.8 us; the launch traced here: 34.2 us
  Pallas kernels  16.5 us (47%)
  starting transfers between devices  15.9 us (46%)
  waiting for transfers between devices  0.96 us (3%)
  between operations  0.87 us (2%)
    pallas_call x7, Pallas kernels, call(): pl.pallas_call(body, out_shape=outs, compiler_params=params, cost_estimat...  16.5 us
    ppermute x6, starting transfers between devices, exchanged(): return (lax.ppermute(off, AXES, across), lax.ppermute(on, AXES, inside))  11.9 us
    ppermute x1, starting transfers between devices, per_device(): lax.ppermute(packed, AXES, [(i, i ^ devices // 2) for i in range(devices)])  4.04 us
    ppermute x6, waiting for transfers between devices, exchanged(): return (lax.ppermute(off, AXES, across), lax.ppermute(on, AXES, inside))  0.96 us
  transfers between devices with their start and end apart: 7, of which 2 were waited for; matrix products, arithmetic and copies ran while one was open for 0% of the time, Pallas kernels for 34%

profile of v5, /device:TPU:0, one launch (start us, length us, event | category | flops | bytes accessed | tf_op | source)
XLA Modules:
  0.0 34.2 jit_solution(14096884808262347175)
XLA Ops:
  0.6 0.0 copy-start.1
  0.6 0.0 copy-start
  0.7 2.2 %pack.1 = (bf16[576,128]{1,0:T(8,128)(2,1)S(1)}, bf16[368,128]{1,0:T(8,128)(2,1)S(1)}, bf16[3,784,128]{2,1,0:T(8,128)(2,1)S(1)}, bf16[3,784,128]{2,1,0:T(8,128)(...) custom-call(f32[8,72,72]{2,1,0:T(8,128)} %inverse_hbm.1, ...), custom_call_target="tpu_custom_call" | custom-call | flops 754974720 | bytes 4903424 | tf_op jit(solution)/shard_map/pack/pallas_call | solution.py:640
  2.8 4.0 %collective-permute-start.2 = (bf16[368,128]{1,0:T(8,128)(2,1)S(1)}, bf16[368,128]{1,0:T(8,128)(2,1)S(1)}, u32[]{:S(2)}, u32[]{:S(2)}) collective-permute-start(bf16[368,128]{1,0:T(8,128)(2,1)S(1)} %get-tuple-element.36), channel_id=1, source_target_pairs={{0,64},{1,65},{2,66},{3,67},{4,68},{5,69},{6,70},{7,71},{8,72},{9,... | collective-permute-start | bytes 282632 | tf_op jit(solution)/shard_map/ppermute | solution.py:677
  6.9 4.5 %collective-permute-start = (bf16[3,784,128]{2,1,0:T(8,128)(2,1)S(1)}, bf16[3,784,128]{2,1,0:T(8,128)(2,1)S(1)}, u32[]{:S(2)}, u32[]{:S(2)}) collective-permute-start(bf16[3,784,128]{2,1,0:T(8,128)(2,1)S(1)} %get-tuple-element.33), channel_id=1, source_target_pairs={{0,127},{1,2},{2,1},{3,4},{4,3},{5,6},{6,5},{7,8},{8,7},{9,10},{10... | collective-permute-start | bytes 1806344 | tf_op jit(solution)/shard_map/ppermute | solution.py:615
  11.4 0.0 collective-permute-start.1
  11.4 0.0 copy-done.1
  11.4 0.0 copy-done
  11.4 1.8 %own.1 = (f32[4,432,128]{2,1,0:T(8,128)S(1)}, f32[4,432,128]{2,1,0:T(8,128)S(1)}) custom-call(f32[4,720,128]{2,1,0:T(8,128)S(1)} %get-tuple-element.30.state_ref, bf16[4,720,128]{2,1,0:T(8,128)(2,1)S(1)} %get-tuple-element.35.prev_ref, f32[2,72,128]{2,1,0:T(8,128)S(1)} %get-tuple-element.31.wind_ref, f32[8,128]{1,0:T(8,128)S(1)} %get-tuple-element.32.target_ref, ...), custom_call_target="tpu_custom_call" | custom-call | flops 3397386240 | bytes 5137408 | tf_op jit(solution)/shard_map/own/pallas_call | solution.py:640
  13.2 0.0 collective-permute-done.2.packed_ref
  13.2 1.4 %far.1 = (bf16[4,432,128]{2,1,0:T(8,128)(2,1)S(1)}, f32[4,432,128]{2,1,0:T(8,128)S(1)}, bf16[4,432,128]{2,1,0:T(8,128)(2,1)S(1)}, bf16[4,432,128]{2,1,0:T(8,128)(2,1)S(1)}, bf16[576,128]{1,0:T(8,128)(2,1)S(1)}) custom-call(f32[4,720,128]{2,1,0:T(8,128)S(1)} %get-tuple-element.30.state_ref, bf16[4,720,128]{2,1,0:T(8,128)(2,1)S(1)} %get-tuple-element.35.prev_ref, ...), custom_call_target="tpu_custom_call" | custom-call | flops 5662310400 | bytes 8152064 | tf_op jit(solution)/shard_map/far/pallas_call | solution.py:640
  14.6 2.9 %collective-permute-start.5 = (bf16[4,432,128]{2,1,0:T(8,128)(2,1)S(1)}, bf16[4,432,128]{2,1,0:T(8,128)(2,1)S(1)}, u32[]{:S(2)}, u32[]{:S(2)}) collective-permute-start(bf16[4,432,128]{2,1,0:T(8,128)(2,1)S(1)} %get-tuple-element.54), channel_id=1, source_target_pairs={{0,127},{1,2},{2,1},{3,4},{4,3},{5,6},{6,5},{7,8},{8,7},{9,10},{10... | collective-permute-start | bytes 1327112 | tf_op jit(solution)/shard_map/ppermute | solution.py:615
  17.5 0.0 collective-permute-start.6
  17.5 2.1 %physics.1 = (bf16[4,288,128]{2,1,0:T(8,128)(2,1)S(1)}, f32[4,288,128]{2,1,0:T(8,128)S(1)}, bf16[4,288,128]{2,1,0:T(8,128)(2,1)S(1)}, bf16[4,288,128]{2,1,0:T(8,128)(2,1)S(1)}) custom-call(f32[4,720,128]{2,1,0:T(8,128)S(1)} %get-tuple-element.30.state_ref, bf16[4,720,128]{2,1,0:T(8,128)(2,1)S(1)} %get-tuple-element.35.prev_ref, ...), custom_call_target="tpu_custom_call" | custom-call | flops 3774873600 | bytes 5432320 | tf_op jit(solution)/shard_map/physics/pallas_call | solution.py:640
  19.6 4.4 %collective-permute-start.3 = (bf16[4,288,128]{2,1,0:T(8,128)(2,1)S(1)}, bf16[4,288,128]{2,1,0:T(8,128)(2,1)S(1)}, u32[]{:S(2)}, u32[]{:S(2)}) collective-permute-start(bf16[4,288,128]{2,1,0:T(8,128)(2,1)S(1)} %get-tuple-element.49), channel_id=1, source_target_pairs={{0,127},{1,2},{2,1},{3,4},{4,3},{5,6},{6,5},{7,8},{8,7},{9,10},{10... | collective-permute-start | bytes 884744 | tf_op jit(solution)/shard_map/ppermute | solution.py:615
  24.0 0.0 collective-permute-done.off_ref
  24.0 0.0 collective-permute-start.4
  24.0 0.0 collective-permute-done.1.on_ref
  24.0 2.9 %near.1 = (f32[4,720,128]{2,1,0:T(8,128)S(1)}, f32[4,720,128]{2,1,0:T(8,128)S(1)}, f32[4,720,128]{2,1,0:T(8,128)S(1)}, bf16[4,720,128]{2,1,0:T(8,128)(2,1)S(1)},...) custom-call(f32[4,720,128]{2,1,0:T(8,128)S(1)} %get-tuple-element.30.state_ref, ...), custom_call_target="tpu_custom_call" | custom-call | flops 6039797760 | bytes 11673600 | tf_op jit(solution)/shard_map/near/pallas_call | solution.py:640
  26.9 0.9 %collective-permute-done.5.off_ref = bf16[4,432,128]{2,1,0:T(8,128)(2,1)S(1)} collective-permute-done((bf16[4,432,128]{2,1,0:T(8,128)(2,1)S(1)}, bf16[4,432,128]{2,1,0:T(8,128)(2,1)S(1)}, u32[]{:S(2)}, u32[]{:S(2)}) %collective-permute-start.5) | collective-permute-done | bytes 442400 | tf_op jit(solution)/shard_map/ppermute | solution.py:615
  27.8 0.0 collective-permute-done.6.on_ref
  27.8 3.3 %advance.2 = (f32[4,432,128]{2,1,0:T(8,128)S(1)}, bf16[4,720,128]{2,1,0:T(8,128)(2,1)}) custom-call(f32[4,720,128]{2,1,0:T(8,128)S(1)} %get-tuple-element.45.own_ref, f32[4,720,128]{2,1,0:T(8,128)S(1)} %get-tuple-element.46.near_ref, f32[4,720,128]{2,1,0:T(8,128)S(1)} %get-tuple-element.47.near_add_ref, ...), custom_call_target="tpu_custom_call" | custom-call | flops 5662310400 | bytes 17203200 | tf_op jit(solution)/shard_map/advance/pallas_call | solution.py:640
  31.2 0.1 collective-permute-done.3.off_ref
  31.2 0.0 collective-permute-done.4.on_ref
  31.2 2.8 %advance.3 = f32[4,720,128]{2,1,0:T(8,128)} custom-call(f32[4,720,128]{2,1,0:T(8,128)S(1)} %get-tuple-element.45.own_ref, f32[4,720,128]{2,1,0:T(8,128)S(1)} %get-tuple-element.46.near_ref, f32[4,720,128]{2,1,0:T(8,128)S(1)} %get-tuple-element.47.near_add_ref, bf16[4,720,128]{2,1,0:T(8,128)(2,1)S(1)} %get-tuple-element.48.near_prev_ref, ...), custom_call_target="tpu_custom_call" | custom-call | flops 3774873600 | bytes 17498112 | tf_op jit(solution)/shard_map/advance/pallas_call | solution.py:640
Async XLA Ops:
  0.6 10.8 %copy-start.1 = (bf16[256,256]{1,0:T(8,128)(2,1)S(1)}, bf16[256,256]{1,0:T(8,128)(2,1)}, u32[]{:S(2)}) copy-start(bf16[256,256]{1,0:T(8,128)(2,1)} %constant.2.clone.slope_ref) | copy-start | bytes 393220
  0.6 10.7 %copy-start = (s32[128]{0:T(128)S(1)}, s32[128]{0:T(128)}, u32[]{:S(2)}) copy-start(s32[128]{0:T(128)} %param.11) | copy-start | bytes 1540
  2.8 10.4 %collective-permute-start.2 = (bf16[368,128]{1,0:T(8,128)(2,1)S(1)}, bf16[368,128]{1,0:T(8,128)(2,1)S(1)}, u32[]{:S(2)}, u32[]{:S(2)}) collective-permute-start(bf16[368,128]{1,0:T(8,128)(2,1)S(1)} %get-tuple-element.36), channel_id=1, source_target_pairs={{0,64},{1,65},{2,66},{3,67},{4,68},{5,69},{6,70},{7,71},{8,72},{9,... | collective-permute-start | bytes 282632 | tf_op jit(solution)/shard_map/ppermute | solution.py:677
  6.9 17.1 %collective-permute-start = (bf16[3,784,128]{2,1,0:T(8,128)(2,1)S(1)}, bf16[3,784,128]{2,1,0:T(8,128)(2,1)S(1)}, u32[]{:S(2)}, u32[]{:S(2)}) collective-permute-start(bf16[3,784,128]{2,1,0:T(8,128)(2,1)S(1)} %get-tuple-element.33), channel_id=1, source_target_pairs={{0,127},{1,2},{2,1},{3,4},{4,3},{5,6},{6,5},{7,8},{8,7},{9,10},{10... | collective-permute-start | bytes 1806344 | tf_op jit(solution)/shard_map/ppermute | solution.py:615
  11.4 12.6 %collective-permute-start.1 = (bf16[3,784,128]{2,1,0:T(8,128)(2,1)S(1)}, bf16[3,784,128]{2,1,0:T(8,128)(2,1)S(1)}, u32[]{:S(2)}, u32[]{:S(2)}) collective-permute-start(bf16[3,784,128]{2,1,0:T(8,128)(2,1)S(1)} %get-tuple-element.34), channel_id=1, source_target_pairs={{0,1},{1,0},{2,3},{3,2},{4,5},{5,4},{6,7},{7,6},{8,9},{9,8},{10,11... | collective-permute-start | bytes 1806344 | tf_op jit(solution)/shard_map/ppermute | solution.py:615
  14.6 13.2 %collective-permute-start.5 = (bf16[4,432,128]{2,1,0:T(8,128)(2,1)S(1)}, bf16[4,432,128]{2,1,0:T(8,128)(2,1)S(1)}, u32[]{:S(2)}, u32[]{:S(2)}) collective-permute-start(bf16[4,432,128]{2,1,0:T(8,128)(2,1)S(1)} %get-tuple-element.54), channel_id=1, source_target_pairs={{0,127},{1,2},{2,1},{3,4},{4,3},{5,6},{6,5},{7,8},{8,7},{9,10},{10... | collective-permute-start | bytes 1327112 | tf_op jit(solution)/shard_map/ppermute | solution.py:615
  17.5 10.3 %collective-permute-start.6 = (bf16[4,432,128]{2,1,0:T(8,128)(2,1)S(1)}, bf16[4,432,128]{2,1,0:T(8,128)(2,1)S(1)}, u32[]{:S(2)}, u32[]{:S(2)}) collective-permute-start(bf16[4,432,128]{2,1,0:T(8,128)(2,1)S(1)} %get-tuple-element.55), channel_id=1, source_target_pairs={{0,1},{1,0},{2,3},{3,2},{4,5},{5,4},{6,7},{7,6},{8,9},{9,8},{10,11... | collective-permute-start | bytes 1327112 | tf_op jit(solution)/shard_map/ppermute | solution.py:615
  19.6 11.7 %collective-permute-start.3 = (bf16[4,288,128]{2,1,0:T(8,128)(2,1)S(1)}, bf16[4,288,128]{2,1,0:T(8,128)(2,1)S(1)}, u32[]{:S(2)}, u32[]{:S(2)}) collective-permute-start(bf16[4,288,128]{2,1,0:T(8,128)(2,1)S(1)} %get-tuple-element.49), channel_id=1, source_target_pairs={{0,127},{1,2},{2,1},{3,4},{4,3},{5,6},{6,5},{7,8},{8,7},{9,10},{10... | collective-permute-start | bytes 884744 | tf_op jit(solution)/shard_map/ppermute | solution.py:615
  24.0 7.3 %collective-permute-start.4 = (bf16[4,288,128]{2,1,0:T(8,128)(2,1)S(1)}, bf16[4,288,128]{2,1,0:T(8,128)(2,1)S(1)}, u32[]{:S(2)}, u32[]{:S(2)}) collective-permute-start(bf16[4,288,128]{2,1,0:T(8,128)(2,1)S(1)} %get-tuple-element.50), channel_id=1, source_target_pairs={{0,1},{1,0},{2,3},{3,2},{4,5},{5,4},{6,7},{7,6},{8,9},{9,8},{10,11... | collective-permute-start | bytes 884744 | tf_op jit(solution)/shard_map/ppermute | solution.py:615

commit v6 on v5

--- a/solution.py
+++ b/solution.py
@@ -190,8 +190,8 @@
     sems,
 ):
     pairs = [(inverse_hbm, inverse_ref), (wind_hbm, wind_ref), (links_hbm, links_ref)]
-    for k in range(PARTS):
-        pairs += [(state_hbm.at[k], state_ref.at[k]), (prev_hbm.at[k], prev_ref.at[k])]
+    for at in chunks(state_ref):
+        pairs += [(state_hbm.at[:, at], state_ref.at[:, at]), (prev_hbm.at[:, at], prev_ref.at[:, at])]
     copies = [pltpu.make_async_copy(a, b, sems.at[i]) for i, (a, b) in enumerate(pairs)]
     for copy in copies:
         copy.start()
@@ -220,9 +220,9 @@
     chosen = sides()
     odd = jnp.where(on_odd(), 3, 0)
     quarter = lane_ids() // 32
-    for copy in copies[3:]:
-        copy.wait()
-    for at in chunks(state_ref):
+    for j, at in enumerate(chunks(state_ref)):
+        copies[3 + 2 * j].wait()
+        copies[4 + 2 * j].wait()
         off, on = packed_halves([state_ref[k, at] for k in range(PARTS)], chosen)
         for k in range(2):
             off_ref[k, at] = off[k].astype(jnp.bfloat16)
@@ -438,8 +438,8 @@
     wind_ref,
     target_ref,
     slope_ref,
+    on_ref,
     off_ref,
-    on_ref,
     prev_ref,
     *rest,
 ):
@@ -532,8 +532,8 @@
     near_add_ref,
     near_prev_ref,
     prev_ref,
+    on_ref,
     off_ref,
-    on_ref,
     slope_ref,
     sum_ref,
     edge_sum_ref,
@@ -602,8 +602,13 @@
         at = pl.ds((first + j) * CHUNK, CHUNK)
         body(at, here_at)
         if last:
-            copies.append(pltpu.make_async_copy(out_ref.at[:, here_at], out_hbm.at[:, at], sems.at[1 + j]))
-            copies[-1].start()
+            for k in range(PARTS):
+                copies.append(
+                    pltpu.make_async_copy(
+                        out_ref.at[k, here_at], out_hbm.at[k, at], sems.at[1 + PARTS * j + k]
+                    )
+                )
+                copies[-1].start()
     for copy in copies:
         copy.wait()
 
@@ -612,7 +617,8 @@
     count = lax.axis_size(AXES)
     across = [(i, (i + 1) % count if i % 2 else (i - 1) % count) for i in range(count)]
     inside = [(i, i ^ 1) for i in range(count)]
-    return lax.ppermute(off, AXES, across), lax.ppermute(on, AXES, inside)
+    on = lax.ppermute(on, AXES, inside)
+    return lax.ppermute(off, AXES, across), on
 
 
 def per_device(state, prev_tendency, wind, edge_links, swap_slot, inverse):
@@ -671,7 +677,7 @@
         scratch_shapes=[
             pltpu.VMEM(inverse.shape, f32),
             pltpu.VMEM(edge_links.shape, jnp.int32),
-            pltpu.SemaphoreType.DMA((3 + 2 * PARTS,)),
+            pltpu.SemaphoreType.DMA((3 + 2 * (rows // CHUNK),)),
         ],
     )
     far_packed = lax.ppermute(packed, AXES, [(i, i ^ (devices // 2)) for i in range(devices)])
@@ -705,7 +711,7 @@
     parts = sum(((tend, ahead) for _, _, tend, ahead, _ in halves), ())
     own, near, near_add, near_prev, sums, edge_sums, blow = call(
         near_kernel,
-        (state, wind, targets, slope, off, on, prev) + parts,
+        (state, wind, targets, slope, on, off, prev) + parts,
         (
             like(4, f32),
             like(4, f32),
@@ -722,7 +728,7 @@
     out_spec = jax.ShapeDtypeStruct((PARTS, rows, LANES), f32)
     tend_spec = jax.ShapeDtypeStruct((PARTS, rows, LANES), bf16)
     for part, (first, count, tend, _, (off, on)) in enumerate(halves):
-        ins = (own, near, near_add, near_prev, prev, off, on, slope, sums, edge_sums, blow)
+        ins = (own, near, near_add, near_prev, prev, on, off, slope, sums, edge_sums, blow)
         size = count * CHUNK
         if part == 0:
             done, tend_out = call(
@@ -742,7 +748,7 @@
                 "advance",
                 5 * count,
                 out_specs=(outer,),
-                scratch_shapes=[pltpu.VMEM((PARTS, size, LANES), f32), pltpu.SemaphoreType.DMA((1 + count,))],
+                scratch_shapes=[pltpu.VMEM((PARTS, size, LANES), f32), pltpu.SemaphoreType.DMA((1 + PARTS * count,))],
             )
     tend = tend_out
     return (out.reshape(shape), tend.reshape(shape))

time: 34.8 us -> 36.3 us (1.043); the launches traced: 34.2 us -> 36.2 us
  starting transfers between devices: 15.9 us -> 17.2 us
  waiting for transfers between devices: 0.96 us -> 1.74 us
    ppermute x6, starting transfers between devices: 11.9 us -> 13.2 us  [the longest x3 13 us: exchanged(): return (lax.ppermute(off, AXES, across), on)]
    ppermute x6, waiting for transfers between devices: 0.96 us -> 1.73 us  [the longest x3 1.73 us: exchanged(): return (lax.ppermute(off, AXES, across), on)]
  transfers between devices with their start and end apart: 7 -> 7, of which waited for: 2 -> 2; matrix products, arithmetic and copies ran while one was open for 0% -> 0% of each run, Pallas kernels for 34% -> 32%
where the time goes in v6:
time: 36.3 us; the launch traced here: 36.2 us
  starting transfers between devices  17.2 us (47%)
  Pallas kernels  16.4 us (45%)
  waiting for transfers between devices  1.74 us (5%)
  between operations  0.9 us (2%)
    pallas_call x7, Pallas kernels, call(): pl.pallas_call(body, out_shape=outs, compiler_params=params, cost_estimat...  16.4 us
    ppermute x3, starting transfers between devices, exchanged(): return (lax.ppermute(off, AXES, across), on)  13 us
    ppermute x1, starting transfers between devices, per_device(): lax.ppermute(packed, AXES, [(i, i ^ devices // 2) for i in range(devices)])  4.04 us
    ppermute x3, waiting for transfers between devices, exchanged(): return (lax.ppermute(off, AXES, across), on)  1.73 us
  transfers between devices with their start and end apart: 7, of which 2 were waited for; matrix products, arithmetic and copies ran while one was open for 0% of the time, Pallas kernels for 32%

profile of v6, /device:TPU:0, one launch (start us, length us, event | category | flops | bytes accessed | tf_op | source)
XLA Modules:
  0.0 36.2 jit_solution(9997567686136710033)
XLA Ops:
  0.6 0.0 copy-start.1
  0.6 0.0 copy-start
  0.7 2.0 %pack.1 = (bf16[576,128]{1,0:T(8,128)(2,1)S(1)}, bf16[368,128]{1,0:T(8,128)(2,1)S(1)}, bf16[3,784,128]{2,1,0:T(8,128)(2,1)S(1)}, bf16[3,784,128]{2,1,0:T(8,128)(...) custom-call(f32[8,72,72]{2,1,0:T(8,128)} %inverse_hbm.1, ...), custom_call_target="tpu_custom_call" | custom-call | flops 754974720 | bytes 4903424 | tf_op jit(solution)/shard_map/pack/pallas_call | solution.py:646
  2.7 4.0 %collective-permute-start.2 = (bf16[368,128]{1,0:T(8,128)(2,1)S(1)}, bf16[368,128]{1,0:T(8,128)(2,1)S(1)}, u32[]{:S(2)}, u32[]{:S(2)}) collective-permute-start(bf16[368,128]{1,0:T(8,128)(2,1)S(1)} %get-tuple-element.36), channel_id=1, source_target_pairs={{0,64},{1,65},{2,66},{3,67},{4,68},{5,69},{6,70},{7,71},{8,72},{9,... | collective-permute-start | bytes 282632 | tf_op jit(solution)/shard_map/ppermute | solution.py:683
  6.7 0.0 collective-permute-start
  6.7 5.5 %collective-permute-start.1 = (bf16[3,784,128]{2,1,0:T(8,128)(2,1)S(1)}, bf16[3,784,128]{2,1,0:T(8,128)(2,1)S(1)}, u32[]{:S(2)}, u32[]{:S(2)}) collective-permute-start(bf16[3,784,128]{2,1,0:T(8,128)(2,1)S(1)} %get-tuple-element.34), channel_id=1, source_target_pairs={{0,127},{1,2},{2,1},{3,4},{4,3},{5,6},{6,5},{7,8},{8,7},{9,10},{10... | collective-permute-start | bytes 1806344 | tf_op jit(solution)/shard_map/ppermute | solution.py:621
  12.2 0.0 copy-done.1
  12.2 0.0 copy-done
  12.2 1.8 %own.1 = (f32[4,432,128]{2,1,0:T(8,128)S(1)}, f32[4,432,128]{2,1,0:T(8,128)S(1)}) custom-call(f32[4,720,128]{2,1,0:T(8,128)S(1)} %get-tuple-element.30.state_ref, bf16[4,720,128]{2,1,0:T(8,128)(2,1)S(1)} %get-tuple-element.35.prev_ref, f32[2,72,128]{2,1,0:T(8,128)S(1)} %get-tuple-element.31.wind_ref, f32[8,128]{1,0:T(8,128)S(1)} %get-tuple-element.32.target_ref, ...), custom_call_target="tpu_custom_call" | custom-call | flops 3397386240 | bytes 5137408 | tf_op jit(solution)/shard_map/own/pallas_call | solution.py:646
  14.0 0.0 collective-permute-done.2.packed_ref
  14.0 1.4 %far.1 = (bf16[4,432,128]{2,1,0:T(8,128)(2,1)S(1)}, f32[4,432,128]{2,1,0:T(8,128)S(1)}, bf16[4,432,128]{2,1,0:T(8,128)(2,1)S(1)}, bf16[4,432,128]{2,1,0:T(8,128)(2,1)S(1)}, bf16[576,128]{1,0:T(8,128)(2,1)S(1)}) custom-call(f32[4,720,128]{2,1,0:T(8,128)S(1)} %get-tuple-element.30.state_ref, bf16[4,720,128]{2,1,0:T(8,128)(2,1)S(1)} %get-tuple-element.35.prev_ref, ...), custom_call_target="tpu_custom_call" | custom-call | flops 5662310400 | bytes 8152064 | tf_op jit(solution)/shard_map/far/pallas_call | solution.py:646
  15.4 0.1 collective-permute-start.5
  15.5 3.7 %collective-permute-start.6 = (bf16[4,432,128]{2,1,0:T(8,128)(2,1)S(1)}, bf16[4,432,128]{2,1,0:T(8,128)(2,1)S(1)}, u32[]{:S(2)}, u32[]{:S(2)}) collective-permute-start(bf16[4,432,128]{2,1,0:T(8,128)(2,1)S(1)} %get-tuple-element.55), channel_id=1, source_target_pairs={{0,127},{1,2},{2,1},{3,4},{4,3},{5,6},{6,5},{7,8},{8,7},{9,10},{10... | collective-permute-start | bytes 1327112 | tf_op jit(solution)/shard_map/ppermute | solution.py:621
  19.2 2.1 %physics.1 = (bf16[4,288,128]{2,1,0:T(8,128)(2,1)S(1)}, f32[4,288,128]{2,1,0:T(8,128)S(1)}, bf16[4,288,128]{2,1,0:T(8,128)(2,1)S(1)}, bf16[4,288,128]{2,1,0:T(8,128)(2,1)S(1)}) custom-call(f32[4,720,128]{2,1,0:T(8,128)S(1)} %get-tuple-element.30.state_ref, bf16[4,720,128]{2,1,0:T(8,128)(2,1)S(1)} %get-tuple-element.35.prev_ref, ...), custom_call_target="tpu_custom_call" | custom-call | flops 3774873600 | bytes 5432320 | tf_op jit(solution)/shard_map/physics/pallas_call | solution.py:646
  21.2 0.1 collective-permute-start.3
  21.3 0.0 collective-permute-done.on_ref
  21.3 3.8 %collective-permute-start.4 = (bf16[4,288,128]{2,1,0:T(8,128)(2,1)S(1)}, bf16[4,288,128]{2,1,0:T(8,128)(2,1)S(1)}, u32[]{:S(2)}, u32[]{:S(2)}) collective-permute-start(bf16[4,288,128]{2,1,0:T(8,128)(2,1)S(1)} %get-tuple-element.50), channel_id=1, source_target_pairs={{0,127},{1,2},{2,1},{3,4},{4,3},{5,6},{6,5},{7,8},{8,7},{9,10},{10... | collective-permute-start | bytes 884744 | tf_op jit(solution)/shard_map/ppermute | solution.py:621
  25.1 0.0 collective-permute-done.1.off_ref
  25.1 2.9 %near.1 = (f32[4,720,128]{2,1,0:T(8,128)S(1)}, f32[4,720,128]{2,1,0:T(8,128)S(1)}, f32[4,720,128]{2,1,0:T(8,128)S(1)}, bf16[4,720,128]{2,1,0:T(8,128)(2,1)S(1)},...) custom-call(f32[4,720,128]{2,1,0:T(8,128)S(1)} %get-tuple-element.30.state_ref, ...), custom_call_target="tpu_custom_call" | custom-call | flops 6039797760 | bytes 11673600 | tf_op jit(solution)/shard_map/near/pallas_call | solution.py:646
  28.1 0.0 collective-permute-done.5.on_ref
  28.1 0.6 %collective-permute-done.6.off_ref = bf16[4,432,128]{2,1,0:T(8,128)(2,1)S(1)} collective-permute-done((bf16[4,432,128]{2,1,0:T(8,128)(2,1)S(1)}, bf16[4,432,128]{2,1,0:T(8,128)(2,1)S(1)}, u32[]{:S(2)}, u32[]{:S(2)}) %collective-permute-start.6) | collective-permute-done | bytes 442400 | tf_op jit(solution)/shard_map/ppermute | solution.py:621
  28.7 3.3 %advance.2 = (f32[4,432,128]{2,1,0:T(8,128)S(1)}, bf16[4,720,128]{2,1,0:T(8,128)(2,1)}) custom-call(f32[4,720,128]{2,1,0:T(8,128)S(1)} %get-tuple-element.45.own_ref, f32[4,720,128]{2,1,0:T(8,128)S(1)} %get-tuple-element.46.near_ref, f32[4,720,128]{2,1,0:T(8,128)S(1)} %get-tuple-element.47.near_add_ref, ...), custom_call_target="tpu_custom_call" | custom-call | flops 5662310400 | bytes 17203200 | tf_op jit(solution)/shard_map/advance/pallas_call | solution.py:646
  32.0 0.0 collective-permute-done.3.on_ref
  32.0 1.1 %collective-permute-done.4.off_ref = bf16[4,288,128]{2,1,0:T(8,128)(2,1)S(1)} collective-permute-done((bf16[4,288,128]{2,1,0:T(8,128)(2,1)S(1)}, bf16[4,288,128]{2,1,0:T(8,128)(2,1)S(1)}, u32[]{:S(2)}, u32[]{:S(2)}) %collective-permute-start.4) | collective-permute-done | bytes 294944 | tf_op jit(solution)/shard_map/ppermute | solution.py:621
  33.2 2.9 %advance.3 = f32[4,720,128]{2,1,0:T(8,128)} custom-call(f32[4,720,128]{2,1,0:T(8,128)S(1)} %get-tuple-element.45.own_ref, f32[4,720,128]{2,1,0:T(8,128)S(1)} %get-tuple-element.46.near_ref, f32[4,720,128]{2,1,0:T(8,128)S(1)} %get-tuple-element.47.near_add_ref, bf16[4,720,128]{2,1,0:T(8,128)(2,1)S(1)} %get-tuple-element.48.near_prev_ref, ...), custom_call_target="tpu_custom_call" | custom-call | flops 3774873600 | bytes 17498112 | tf_op jit(solution)/shard_map/advance/pallas_call | solution.py:646
Async XLA Ops:
  0.6 11.6 %copy-start.1 = (bf16[256,256]{1,0:T(8,128)(2,1)S(1)}, bf16[256,256]{1,0:T(8,128)(2,1)}, u32[]{:S(2)}) copy-start(bf16[256,256]{1,0:T(8,128)(2,1)} %constant.2.clone.slope_ref) | copy-start | bytes 393220
  0.6 11.6 %copy-start = (s32[128]{0:T(128)S(1)}, s32[128]{0:T(128)}, u32[]{:S(2)}) copy-start(s32[128]{0:T(128)} %param.11) | copy-start | bytes 1540
  2.7 11.3 %collective-permute-start.2 = (bf16[368,128]{1,0:T(8,128)(2,1)S(1)}, bf16[368,128]{1,0:T(8,128)(2,1)S(1)}, u32[]{:S(2)}, u32[]{:S(2)}) collective-permute-start(bf16[368,128]{1,0:T(8,128)(2,1)S(1)} %get-tuple-element.36), channel_id=1, source_target_pairs={{0,64},{1,65},{2,66},{3,67},{4,68},{5,69},{6,70},{7,71},{8,72},{9,... | collective-permute-start | bytes 282632 | tf_op jit(solution)/shard_map/ppermute | solution.py:683
  6.7 14.6 %collective-permute-start = (bf16[3,784,128]{2,1,0:T(8,128)(2,1)S(1)}, bf16[3,784,128]{2,1,0:T(8,128)(2,1)S(1)}, u32[]{:S(2)}, u32[]{:S(2)}) collective-permute-start(bf16[3,784,128]{2,1,0:T(8,128)(2,1)S(1)} %get-tuple-element.33), channel_id=1, source_target_pairs={{0,1},{1,0},{2,3},{3,2},{4,5},{5,4},{6,7},{7,6},{8,9},{9,8},{10,11... | collective-permute-start | bytes 1806344 | tf_op jit(solution)/shard_map/ppermute | solution.py:620
  6.7 18.4 %collective-permute-start.1 = (bf16[3,784,128]{2,1,0:T(8,128)(2,1)S(1)}, bf16[3,784,128]{2,1,0:T(8,128)(2,1)S(1)}, u32[]{:S(2)}, u32[]{:S(2)}) collective-permute-start(bf16[3,784,128]{2,1,0:T(8,128)(2,1)S(1)} %get-tuple-element.34), channel_id=1, source_target_pairs={{0,127},{1,2},{2,1},{3,4},{4,3},{5,6},{6,5},{7,8},{8,7},{9,10},{10... | collective-permute-start | bytes 1806344 | tf_op jit(solution)/shard_map/ppermute | solution.py:621
  15.4 12.7 %collective-permute-start.5 = (bf16[4,432,128]{2,1,0:T(8,128)(2,1)S(1)}, bf16[4,432,128]{2,1,0:T(8,128)(2,1)S(1)}, u32[]{:S(2)}, u32[]{:S(2)}) collective-permute-start(bf16[4,432,128]{2,1,0:T(8,128)(2,1)S(1)} %get-tuple-element.54), channel_id=1, source_target_pairs={{0,1},{1,0},{2,3},{3,2},{4,5},{5,4},{6,7},{7,6},{8,9},{9,8},{10,11... | collective-permute-start | bytes 1327112 | tf_op jit(solution)/shard_map/ppermute | solution.py:620
  15.5 13.2 %collective-permute-start.6 = (bf16[4,432,128]{2,1,0:T(8,128)(2,1)S(1)}, bf16[4,432,128]{2,1,0:T(8,128)(2,1)S(1)}, u32[]{:S(2)}, u32[]{:S(2)}) collective-permute-start(bf16[4,432,128]{2,1,0:T(8,128)(2,1)S(1)} %get-tuple-element.55), channel_id=1, source_target_pairs={{0,127},{1,2},{2,1},{3,4},{4,3},{5,6},{6,5},{7,8},{8,7},{9,10},{10... | collective-permute-start | bytes 1327112 | tf_op jit(solution)/shard_map/ppermute | solution.py:621
  21.2 10.8 %collective-permute-start.3 = (bf16[4,288,128]{2,1,0:T(8,128)(2,1)S(1)}, bf16[4,288,128]{2,1,0:T(8,128)(2,1)S(1)}, u32[]{:S(2)}, u32[]{:S(2)}) collective-permute-start(bf16[4,288,128]{2,1,0:T(8,128)(2,1)S(1)} %get-tuple-element.49), channel_id=1, source_target_pairs={{0,1},{1,0},{2,3},{3,2},{4,5},{5,4},{6,7},{7,6},{8,9},{9,8},{10,11... | collective-permute-start | bytes 884744 | tf_op jit(solution)/shard_map/ppermute | solution.py:620
  21.3 11.8 %collective-permute-start.4 = (bf16[4,288,128]{2,1,0:T(8,128)(2,1)S(1)}, bf16[4,288,128]{2,1,0:T(8,128)(2,1)S(1)}, u32[]{:S(2)}, u32[]{:S(2)}) collective-permute-start(bf16[4,288,128]{2,1,0:T(8,128)(2,1)S(1)} %get-tuple-element.50), channel_id=1, source_target_pairs={{0,127},{1,2},{2,1},{3,4},{4,3},{5,6},{6,5},{7,8},{8,7},{9,10},{10... | collective-permute-start | bytes 884744 | tf_op jit(solution)/shard_map/ppermute | solution.py:621

commit v7 on v6

--- a/solution.py
+++ b/solution.py
@@ -242,23 +242,28 @@
     return [pl.ds(start, CHUNK) for start in range(0, ref.shape[1], CHUNK)]
 
 
-def each_chunk(first, count, body):
-    def step(j, carry):
-        near, whole = j * CHUNK, (first + j) * CHUNK
-        body(pl.ds(pl.multiple_of(whole, CHUNK), CHUNK), pl.ds(pl.multiple_of(near, CHUNK), CHUNK))
-        return carry
-
-    lax.fori_loop(0, count, step, 0, unroll=True)
-
-
-def chosen_product(matrices, group, pair, chosen=None, first=0):
+def in_turns(first, count, stages):
+    running = []
+    for j in range(count):
+        running.append(stages(pl.ds((first + j) * CHUNK, CHUNK), pl.ds(j * CHUNK, CHUNK), j))
+    waiting, started = list(running), []
+    while waiting or started:
+        if waiting:
+            started.append(waiting.pop(0))
+        started = [one for one in started if next(one, started) is not started]
+
+
+def column_pair(pair):
     lev = pair.shape[0] // 2
     blank = jnp.zeros((LANES - lev, 2 * LANES), jnp.float32)
     pair = jnp.concatenate([pair[:lev], pair[lev:]], axis=1)
     high = pair.astype(jnp.bfloat16).astype(jnp.float32)
-    column = jnp.concatenate([high, blank, pair - high, blank], axis=0).astype(jnp.bfloat16)
-    product = jnp.dot(matrices, column, preferred_element_type=jnp.float32)
-    for c in range(matrices.shape[0] // lev):
+    return jnp.concatenate([high, blank, pair - high, blank], axis=0).astype(jnp.bfloat16)
+
+
+def chosen_rows(product, group, chosen=None, first=0):
+    lev = 72
+    for c in range(product.shape[0] // lev):
         part = product[c * lev : (c + 1) * lev]
         chosen = part if chosen is None else jnp.where(group == first + c, part, chosen)
     return chosen
@@ -300,7 +305,7 @@
     }[source]
     for s in range(2):
         total = total + ((place == targets[s : s + 1]) & slots[s]).astype(jnp.float32)
-    return total.astype(jnp.bfloat16)
+    return (total * point_sets()[1]).astype(jnp.bfloat16)
 
 
 def inner_lanes():
@@ -321,15 +326,36 @@
             self.matrices = jnp.concatenate([matrices, matrices], axis=1)
 
     def begin(self, wind_ref, target_ref, slope_ref):
-        slots, self.share = point_sets()
+        slots, _ = point_sets()
         self.sums = sum_block("own", target_ref[...].astype(jnp.int32) - 32, slots, True)
         self.blow = [-time_step * wind_ref[d] for d in range(2)]
         self.slope = slope_ref[...]
 
-    def start(self, state, prev):
-        motion = moved(state, self.slope, *self.blow)
+    def motion(self, state):
+        return moved(state, self.slope, *self.blow)
+
+    def start(self, state, prev, motion):
         total = jnp.dot(motion, self.sums, preferred_element_type=jnp.float32)
-        return state + total * self.share + time_step * hermite(0)[0] * prev
+        return state + total + time_step * hermite(0)[0] * prev
+
+    def products(self, pairs, others=None, first=0):
+        ahead, rows = None, []
+
+        def choose(k):
+            other = None
+            if others:
+                lev = others[k].shape[0] // 2
+                other = jnp.concatenate([others[k][:lev], others[k][lev:]], axis=1)
+            return as_rows(chosen_rows(ahead, self.group, other, first))
+
+        for k, pair in enumerate(pairs):
+            product = jnp.dot(self.matrices, column_pair(pair), preferred_element_type=jnp.float32)
+            if k:
+                rows.append(choose(k - 1))
+            ahead = product
+            yield
+        rows.append(choose(len(pairs) - 1))
+        return rows
 
     def finish(self, start, prev, tends, here_at, tend_ref, ahead_ref, off_ref, on_ref):
         late = time_step * hermite(0)[1]
@@ -357,14 +383,18 @@
 ):
     physics = Physics(slot_ref, [own_ref])
     physics.begin(wind_ref, target_ref, slope_ref)
-    def body(at, here_at):
-        start = physics.start(flat(state_ref[:, at]), flat(prev_ref[:, at]))
+    def stages(at, here_at, _):
+        state = flat(state_ref[:, at])
+        motion = physics.motion(state)
+        yield
+        start = physics.start(state, flat(prev_ref[:, at]), motion)
         start_ref[:, here_at] = start.reshape(PARTS, CHUNK, LANES)
-        for k in range(PARTS):
-            chosen = chosen_product(physics.matrices, physics.group, state_ref[k, at])
-            part_ref[k, here_at] = as_rows(chosen)
-
-    each_chunk(first, count, body)
+        yield
+        parts = yield from physics.products([state_ref[k, at] for k in range(PARTS)])
+        for k, part in enumerate(parts):
+            part_ref[k, here_at] = part
+
+    in_turns(first, count, stages)
 
 
 def far_kernel(
@@ -387,18 +417,15 @@
     far_ref[...] = matrices
     physics.take(matrices)
 
-    def body(at, here_at):
-        tends = []
-        for k in range(PARTS):
-            pair = part_ref[k, here_at]
-            lev = pair.shape[0] // 2
-            pair = jnp.concatenate([pair[:lev], pair[lev:]], axis=1)
-            tends.append(as_rows(chosen_product(physics.matrices, physics.group, state_ref[k, at], pair, 8)))
+    def stages(at, here_at, _):
+        tends = yield from physics.products(
+            [state_ref[k, at] for k in range(PARTS)], [part_ref[k, here_at] for k in range(PARTS)], 8
+        )
         start = [start_ref[k, here_at] for k in range(PARTS)]
         prev = [prev_ref[k, at].astype(jnp.float32) for k in range(PARTS)]
         physics.finish(start, prev, tends, here_at, tend_ref, ahead_ref, off_ref, on_ref)
 
-    each_chunk(first, count, body)
+    in_turns(first, count, stages)
 
 
 def physics_kernel(
@@ -420,17 +447,18 @@
     physics = Physics(slot_ref, [own_ref, far_ref])
     physics.begin(wind_ref, target_ref, slope_ref)
 
-    def body(at, here_at):
-        start = physics.start(flat(state_ref[:, at]), flat(prev_ref[:, at]))
+    def stages(at, here_at, _):
+        state = flat(state_ref[:, at])
+        motion = physics.motion(state)
+        yield
+        start = physics.start(state, flat(prev_ref[:, at]), motion)
         start = [start[k * CHUNK : (k + 1) * CHUNK] for k in range(PARTS)]
+        yield
+        tends = yield from physics.products([state_ref[k, at] for k in range(PARTS)])
         prev = [prev_ref[k, at].astype(jnp.float32) for k in range(PARTS)]
-        tends = [
-            as_rows(chosen_product(physics.matrices, physics.group, state_ref[k, at]))
-            for k in range(PARTS)
-        ]
         physics.finish(start, prev, tends, here_at, tend_ref, ahead_ref, off_ref, on_ref)
 
-    each_chunk(first, count, body)
+    in_turns(first, count, stages)
 
 
 def near_kernel(
@@ -438,14 +466,15 @@
     wind_ref,
     target_ref,
     slope_ref,
+    off_ref,
     on_ref,
-    off_ref,
     prev_ref,
     *rest,
 ):
-    parts, (own_ref, near_ref, near_add_ref, force_ref, sum_ref, edge_sum_ref, blow_ref) = rest[:-7], rest[-7:]
+    parts, outs = rest[:-8], rest[-8:]
+    own_ref, near_ref, near_add_ref, own_force_ref, near_force_ref, sum_ref, edge_sum_ref, blow_ref = outs
     lev = wind_ref.shape[1]
-    slots, share = point_sets()
+    slots, _ = point_sets()
     chosen = sides()
     end = off_ref.shape[1]
 
@@ -490,14 +519,16 @@
     slope = slope_ref[...]
     early = time_step * hermite(0)[0]
     early_1, late_1 = (time_step * w for w in hermite(1))
+    early_2, late_2 = (time_step * w for w in hermite(2))
     own_blow = (blow_ref[0, 0], blow_ref[0, 1])
     near_blow = (blow_ref[1, 0], blow_ref[1, 1])
 
-    def body(at, here_at, tend_ref, ahead_ref):
+    def stages(at, here_at, tend_ref, ahead_ref):
         off, on = off_ref[:, at].astype(jnp.float32), on_ref[:, at].astype(jnp.float32)
         near = whole_halves(off[:2], on[:2], chosen)
         own_move = moved(flat(state_ref[:, at]), slope, *own_blow)
         near_move = moved(near, slope, *near_blow)
+        yield
         total = jnp.dot(near_move, near_sums, preferred_element_type=jnp.float32)
         near_total = total[:, LANES:] + jnp.dot(
             own_move, own_sums[:, LANES:], preferred_element_type=jnp.float32
@@ -506,22 +537,27 @@
         for k in range(1, PARTS):
             turned = [pltpu.roll(side[2], LANES - 32 * k, 1) for side in (off, on)]
             kept.append(jnp.where(chosen, *turned))
-        kept = jnp.concatenate(kept, axis=0)
-        near = near + near_total * share + early * kept
+        kept = jnp.where(inner, 0.0, jnp.concatenate(kept, axis=0))
+        near = near + near_total + early * kept
         near_ref[:, at] = near.reshape(PARTS, CHUNK, LANES)
-        force_ref[:, at] = kept.astype(jnp.bfloat16).reshape(PARTS, CHUNK, LANES)
-        own = flat(ahead_ref[:, here_at]) + total[:, :LANES] * share
-        total = jnp.dot(moved(own, slope, *own_blow), own_sums, preferred_element_type=jnp.float32)
-        force = early_1 * flat(prev_ref[:, at]) + late_1 * flat(tend_ref[:, here_at])
-        own = own + total[:, :LANES] * share + force
+        near_force_ref[:, at] = (early_2 * kept).reshape(PARTS, CHUNK, LANES)
+        own = flat(ahead_ref[:, here_at]) + total[:, :LANES]
+        yield
+        own_move = moved(own, slope, *own_blow)
+        yield
+        total = jnp.dot(own_move, own_sums, preferred_element_type=jnp.float32)
+        own_prev, own_tend = flat(prev_ref[:, at]), flat(tend_ref[:, here_at])
+        own = own + total[:, :LANES] + (early_1 * own_prev + late_1 * own_tend)
         own_ref[:, at] = own.reshape(PARTS, CHUNK, LANES)
-        near_add_ref[:, at] = (total[:, LANES:] * share).reshape(PARTS, CHUNK, LANES)
-
-    first = 0
+        own_force = early_2 * own_prev + late_2 * own_tend
+        own_force_ref[:, at] = own_force.reshape(PARTS, CHUNK, LANES)
+        near_add = total[:, LANES:] + early_1 * kept
+        near_add_ref[:, at] = near_add.reshape(PARTS, CHUNK, LANES)
+
+    places = []
     for tend_ref, ahead_ref in zip(parts[::2], parts[1::2]):
-        for j, here_at in enumerate(chunks(tend_ref)):
-            body(pl.ds((first + j) * CHUNK, CHUNK), here_at, tend_ref, ahead_ref)
-        first += tend_ref.shape[1] // CHUNK
+        places += [(here_at, tend_ref, ahead_ref) for here_at in chunks(tend_ref)]
+    in_turns(0, len(places), lambda at, _, j: stages(at, *places[j]))
 
 
 def advance_kernel(
@@ -530,10 +566,10 @@
     own_ref,
     near_ref,
     near_add_ref,
-    near_prev_ref,
-    prev_ref,
+    own_force_ref,
+    near_force_ref,
+    off_ref,
     on_ref,
-    off_ref,
     slope_ref,
     sum_ref,
     edge_sum_ref,
@@ -552,11 +588,10 @@
             row += ref.shape[1]
     for copy in copies:
         copy.start()
-    _, share = point_sets()
     inner = inner_lanes()
     chosen = sides()
     slope = slope_ref[...]
-    weights = [tuple(time_step * w for w in hermite(s)) for s in range(SUBSTEPS)]
+    lates = [time_step * hermite(s)[1] for s in range(SUBSTEPS)]
 
     def advect(value, unit):
         return moved(value, slope, blow_ref[unit, 0], blow_ref[unit, 1])
@@ -572,35 +607,34 @@
         ]
         return jnp.concatenate(parts, axis=0)
 
-    def body(at, here_at):
+    def stages(at, here_at, j):
         off, on = off_ref[:, here_at].astype(jnp.float32), on_ref[:, here_at].astype(jnp.float32)
         off_mid, on_mid = flat(off[:2]), flat(on[:2])
         middle = [jnp.where(chosen, off_mid, on_mid), jnp.where(chosen, on_mid, off_mid)]
         middle = jnp.concatenate([middle[0], pltpu.roll(middle[1], 64, 1)], axis=0)
         outer = jnp.where(chosen == inner, on_mid, off_mid)
         received = whole_halves(off[2:], on[2:], chosen)
-        own_prev, own_tend = flat(prev_ref[:, at]), flat(tend_ref[:, here_at])
-        near_prev = flat(near_prev_ref[:, at])
-        early, late = weights[1]
-        near = jnp.where(inner, middle, flat(near_ref[:, at]) + weights[0][1] * received)
-        total = gather_shared(advect(near, 1), advect(outer, 2), 0, 2 * LANES)
-        own = flat(own_ref[:, at]) + total[:, :LANES] * share
-        force = jnp.where(inner, received, early * near_prev + late * received)
-        near = near + total[:, LANES:] * share + flat(near_add_ref[:, at]) + force
-        early, late = weights[2]
-        total = gather([advect(own, 0), advect(near, 1)], sum_ref[...])
-        own = own + total[:, :LANES] * share + (early * own_prev + late * own_tend)
-        near = near + total[:, LANES:] * share + (early * near_prev + late * received)
-        early, late = weights[3]
+        near = jnp.where(inner, middle, flat(near_ref[:, at]) + lates[0] * received)
+        moves = advect(near, 1), advect(outer, 2)
+        yield
+        total = gather_shared(*moves, 0, 2 * LANES)
+        own = flat(own_ref[:, at]) + total[:, :LANES]
+        force = received * jnp.where(inner, 1.0, lates[1])
+        near = near + total[:, LANES:] + (flat(near_add_ref[:, at]) + force)
+        yield
+        moves = [advect(own, 0), advect(near, 1)]
+        yield
+        total = gather(moves, sum_ref[...])
+        own = own + total[:, :LANES] + flat(own_force_ref[:, at])
+        near = near + total[:, LANES:] + (flat(near_force_ref[:, at]) + lates[2] * received)
+        yield
         half = near.shape[0] // 2
         near = jnp.where(inner, pltpu.roll(near[half:], 64, 1), near[:half])
-        total = gather_shared(advect(own, 0), advect(near, 3), 2, LANES)
-        out = own + total * share + (early * own_prev + late * own_tend)
+        moves = advect(own, 0), advect(near, 3)
+        yield
+        total = gather_shared(*moves, 2, LANES)
+        out = own + total + lates[3] * flat(tend_ref[:, here_at])
         out_ref[:, here_at] = out.reshape(PARTS, CHUNK, LANES)
-
-    for j, here_at in enumerate(chunks(out_ref)):
-        at = pl.ds((first + j) * CHUNK, CHUNK)
-        body(at, here_at)
         if last:
             for k in range(PARTS):
                 copies.append(
@@ -609,6 +643,8 @@
                     )
                 )
                 copies[-1].start()
+
+    in_turns(first, out_ref.shape[1] // CHUNK, stages)
     for copy in copies:
         copy.wait()
 
@@ -709,14 +745,15 @@
         halves.append((first, count, tend, ahead, exchanged(to_off, to_on)))
         first += count
     parts = sum(((tend, ahead) for _, _, tend, ahead, _ in halves), ())
-    own, near, near_add, near_prev, sums, edge_sums, blow = call(
+    own, near, near_add, own_force, near_force, sums, edge_sums, blow = call(
         near_kernel,
-        (state, wind, targets, slope, on, off, prev) + parts,
+        (state, wind, targets, slope, off, on, prev) + parts,
         (
             like(4, f32),
             like(4, f32),
             like(4, f32),
-            like(4, bf16),
+            like(4, f32),
+            like(4, f32),
             table(bf16, 2 * LANES, 2 * LANES),
             table(bf16, 4, 2 * LANES, 2 * LANES),
             table(f32, 4, 2, lev, LANES),
@@ -728,7 +765,7 @@
     out_spec = jax.ShapeDtypeStruct((PARTS, rows, LANES), f32)
     tend_spec = jax.ShapeDtypeStruct((PARTS, rows, LANES), bf16)
     for part, (first, count, tend, _, (off, on)) in enumerate(halves):
-        ins = (own, near, near_add, near_prev, prev, on, off, slope, sums, edge_sums, blow)
+        ins = (own, near, near_add, own_force, near_force, off, on, slope, sums, edge_sums, blow)
         size = count * CHUNK
         if part == 0:
             done, tend_out = call(

time: 36.3 us -> 33.9 us (0.934)
  starting transfers between devices: 17.2 us -> 15.9 us
  Pallas kernels: 16.4 us -> 15.2 us
    pallas_call x7, Pallas kernels: 16.4 us -> 15.2 us  [call(): pl.pallas_call(body, out_shape=outs, compiler_params=params, cost_estimat...]
    ppermute x3, starting transfers between devices: 13 us -> 11.9 us  [exchanged(): return (lax.ppermute(off, AXES, across), on)]
  transfers between devices with their start and end apart: 7 -> 7, of which waited for: 2 -> 2; matrix products, arithmetic and copies ran while one was open for 0% -> 0% of each run, Pallas kernels for 32% -> 31%
where the time goes in v7:
time: 33.9 us; the launch traced here: 33.7 us
  starting transfers between devices  15.9 us (47%)
  Pallas kernels  15.2 us (45%)
  waiting for transfers between devices  1.74 us (5%)
  between operations  0.87 us (3%)
    pallas_call x7, Pallas kernels, call(): pl.pallas_call(body, out_shape=outs, compiler_params=params, cost_estimat...  15.2 us
    ppermute x3, starting transfers between devices, exchanged(): return (lax.ppermute(off, AXES, across), on)  11.9 us
    ppermute x1, starting transfers between devices, per_device(): lax.ppermute(packed, AXES, [(i, i ^ devices // 2) for i in range(devices)])  4.04 us
    ppermute x3, waiting for transfers between devices, exchanged(): return (lax.ppermute(off, AXES, across), on)  1.73 us
  transfers between devices with their start and end apart: 7, of which 2 were waited for; matrix products, arithmetic and copies ran while one was open for 0% of the time, Pallas kernels for 31%

profile of v7, /device:TPU:0, one launch (start us, length us, event | category | flops | bytes accessed | tf_op | source)
XLA Modules:
  0.0 33.7 jit_solution(13580358391353683790)
XLA Ops:
  0.6 0.0 copy-start.1
  0.6 0.0 copy-start
  0.7 2.0 %pack.1 = (bf16[576,128]{1,0:T(8,128)(2,1)S(1)}, bf16[368,128]{1,0:T(8,128)(2,1)S(1)}, bf16[3,784,128]{2,1,0:T(8,128)(2,1)S(1)}, bf16[3,784,128]{2,1,0:T(8,128)(...) custom-call(f32[8,72,72]{2,1,0:T(8,128)} %inverse_hbm.1, ...), custom_call_target="tpu_custom_call" | custom-call | flops 754974720 | bytes 4903424 | tf_op jit(solution)/shard_map/pack/pallas_call | solution.py:682
  2.7 4.0 %collective-permute-start.2 = (bf16[368,128]{1,0:T(8,128)(2,1)S(1)}, bf16[368,128]{1,0:T(8,128)(2,1)S(1)}, u32[]{:S(2)}, u32[]{:S(2)}) collective-permute-start(bf16[368,128]{1,0:T(8,128)(2,1)S(1)} %get-tuple-element.37), channel_id=1, source_target_pairs={{0,64},{1,65},{2,66},{3,67},{4,68},{5,69},{6,70},{7,71},{8,72},{9,... | collective-permute-start | bytes 282632 | tf_op jit(solution)/shard_map/ppermute | solution.py:719
  6.7 4.5 %collective-permute-start = (bf16[3,784,128]{2,1,0:T(8,128)(2,1)S(1)}, bf16[3,784,128]{2,1,0:T(8,128)(2,1)S(1)}, u32[]{:S(2)}, u32[]{:S(2)}) collective-permute-start(bf16[3,784,128]{2,1,0:T(8,128)(2,1)S(1)} %get-tuple-element.34), channel_id=1, source_target_pairs={{0,127},{1,2},{2,1},{3,4},{4,3},{5,6},{6,5},{7,8},{8,7},{9,10},{10... | collective-permute-start | bytes 1806344 | tf_op jit(solution)/shard_map/ppermute | solution.py:657
  11.2 0.0 collective-permute-start.1
  11.2 0.0 copy-done.1
  11.2 0.0 copy-done
  11.2 1.8 %own.1 = (f32[4,432,128]{2,1,0:T(8,128)S(1)}, f32[4,432,128]{2,1,0:T(8,128)S(1)}) custom-call(f32[4,720,128]{2,1,0:T(8,128)S(1)} %get-tuple-element.31.state_ref, bf16[4,720,128]{2,1,0:T(8,128)(2,1)S(1)} %get-tuple-element.36.prev_ref, f32[2,72,128]{2,1,0:T(8,128)S(1)} %get-tuple-element.32.wind_ref, f32[8,128]{1,0:T(8,128)S(1)} %get-tuple-element.33.target_ref, ...), custom_call_target="tpu_custom_call" | custom-call | flops 3397386240 | bytes 5137408 | tf_op jit(solution)/shard_map/own/pallas_call | solution.py:682
  13.0 0.0 collective-permute-done.2.packed_ref
  13.0 1.3 %far.1 = (bf16[4,432,128]{2,1,0:T(8,128)(2,1)S(1)}, f32[4,432,128]{2,1,0:T(8,128)S(1)}, bf16[4,432,128]{2,1,0:T(8,128)(2,1)S(1)}, bf16[4,432,128]{2,1,0:T(8,128)(2,1)S(1)}, bf16[576,128]{1,0:T(8,128)(2,1)S(1)}) custom-call(f32[4,720,128]{2,1,0:T(8,128)S(1)} %get-tuple-element.31.state_ref, bf16[4,720,128]{2,1,0:T(8,128)(2,1)S(1)} %get-tuple-element.36.prev_ref, ...), custom_call_target="tpu_custom_call" | custom-call | flops 5662310400 | bytes 8152064 | tf_op jit(solution)/shard_map/far/pallas_call | solution.py:682
  14.3 2.9 %collective-permute-start.5 = (bf16[4,432,128]{2,1,0:T(8,128)(2,1)S(1)}, bf16[4,432,128]{2,1,0:T(8,128)(2,1)S(1)}, u32[]{:S(2)}, u32[]{:S(2)}) collective-permute-start(bf16[4,432,128]{2,1,0:T(8,128)(2,1)S(1)} %get-tuple-element.56), channel_id=1, source_target_pairs={{0,127},{1,2},{2,1},{3,4},{4,3},{5,6},{6,5},{7,8},{8,7},{9,10},{10... | collective-permute-start | bytes 1327112 | tf_op jit(solution)/shard_map/ppermute | solution.py:657
  17.3 0.0 collective-permute-start.6
  17.3 2.0 %physics.1 = (bf16[4,288,128]{2,1,0:T(8,128)(2,1)S(1)}, f32[4,288,128]{2,1,0:T(8,128)S(1)}, bf16[4,288,128]{2,1,0:T(8,128)(2,1)S(1)}, bf16[4,288,128]{2,1,0:T(8,128)(2,1)S(1)}) custom-call(f32[4,720,128]{2,1,0:T(8,128)S(1)} %get-tuple-element.31.state_ref, bf16[4,720,128]{2,1,0:T(8,128)(2,1)S(1)} %get-tuple-element.36.prev_ref, ...), custom_call_target="tpu_custom_call" | custom-call | flops 3774873600 | bytes 5432320 | tf_op jit(solution)/shard_map/physics/pallas_call | solution.py:682
  19.3 4.4 %collective-permute-start.3 = (bf16[4,288,128]{2,1,0:T(8,128)(2,1)S(1)}, bf16[4,288,128]{2,1,0:T(8,128)(2,1)S(1)}, u32[]{:S(2)}, u32[]{:S(2)}) collective-permute-start(bf16[4,288,128]{2,1,0:T(8,128)(2,1)S(1)} %get-tuple-element.51), channel_id=1, source_target_pairs={{0,127},{1,2},{2,1},{3,4},{4,3},{5,6},{6,5},{7,8},{8,7},{9,10},{10... | collective-permute-start | bytes 884744 | tf_op jit(solution)/shard_map/ppermute | solution.py:657
  23.7 0.0 collective-permute-done.off_ref
  23.7 0.0 collective-permute-start.4
  23.7 0.0 collective-permute-done.1.on_ref
  23.7 2.9 %near.1 = (f32[4,720,128]{2,1,0:T(8,128)S(1)}, f32[4,720,128]{2,1,0:T(8,128)S(1)}, f32[4,720,128]{2,1,0:T(8,128)S(1)}, f32[4,720,128]{2,1,0:T(8,128)S(1)}, f32[4...) custom-call(f32[4,720,128]{2,1,0:T(8,128)S(1)} %get-tuple-element.31, ...), custom_call_target="tpu_custom_call" | custom-call | flops 6039797760 | bytes 11673600 | tf_op jit(solution)/shard_map/near/pallas_call | solution.py:682
  26.6 0.9 %collective-permute-done.5.off_ref = bf16[4,432,128]{2,1,0:T(8,128)(2,1)S(1)} collective-permute-done((bf16[4,432,128]{2,1,0:T(8,128)(2,1)S(1)}, bf16[4,432,128]{2,1,0:T(8,128)(2,1)S(1)}, u32[]{:S(2)}, u32[]{:S(2)}) %collective-permute-start.5) | collective-permute-done | bytes 442400 | tf_op jit(solution)/shard_map/ppermute | solution.py:657
  27.6 0.0 collective-permute-done.6.on_ref
  27.6 2.5 %advance.2 = (f32[4,432,128]{2,1,0:T(8,128)S(1)}, bf16[4,720,128]{2,1,0:T(8,128)(2,1)}) custom-call(f32[4,720,128]{2,1,0:T(8,128)S(1)} %get-tuple-element.46.own_ref, f32[4,720,128]{2,1,0:T(8,128)S(1)} %get-tuple-element.47.near_ref, f32[4,720,128]{2,1,0:T(8,128)S(1)} %get-tuple-element.48.near_add_ref, f32[4,720,128]{2,1,0:T(8,128)S(1)} %get-tuple-element.49.own_force_ref, ...), custom_call_target="tpu_custom_call" | custom-call | flops 5662310400 | bytes 20152320 | tf_op jit(solution)/shard_map/advance/pallas_call | solution.py:682
  30.1 0.8 %collective-permute-done.3.off_ref = bf16[4,288,128]{2,1,0:T(8,128)(2,1)S(1)} collective-permute-done((bf16[4,288,128]{2,1,0:T(8,128)(2,1)S(1)}, bf16[4,288,128]{2,1,0:T(8,128)(2,1)S(1)}, u32[]{:S(2)}, u32[]{:S(2)}) %collective-permute-start.3) | collective-permute-done | bytes 294944 | tf_op jit(solution)/shard_map/ppermute | solution.py:657
  30.9 0.0 collective-permute-done.4.on_ref
  30.9 2.6 %advance.3 = f32[4,720,128]{2,1,0:T(8,128)} custom-call(f32[4,720,128]{2,1,0:T(8,128)S(1)} %get-tuple-element.46.own_ref, f32[4,720,128]{2,1,0:T(8,128)S(1)} %get-tuple-element.47.near_ref, f32[4,720,128]{2,1,0:T(8,128)S(1)} %get-tuple-element.48.near_add_ref, f32[4,720,128]{2,1,0:T(8,128)S(1)} %get-tuple-element.49.own_force_ref, ...), custom_call_target="tpu_custom_call" | custom-call | flops 3774873600 | bytes 20447232 | tf_op jit(solution)/shard_map/advance/pallas_call | solution.py:682
Async XLA Ops:
  0.6 10.6 %copy-start.1 = (bf16[256,256]{1,0:T(8,128)(2,1)S(1)}, bf16[256,256]{1,0:T(8,128)(2,1)}, u32[]{:S(2)}) copy-start(bf16[256,256]{1,0:T(8,128)(2,1)} %constant.2.clone.slope_ref) | copy-start | bytes 393220
  0.6 10.6 %copy-start = (s32[128]{0:T(128)S(1)}, s32[128]{0:T(128)}, u32[]{:S(2)}) copy-start(s32[128]{0:T(128)} %param.11) | copy-start | bytes 1540
  2.7 10.3 %collective-permute-start.2 = (bf16[368,128]{1,0:T(8,128)(2,1)S(1)}, bf16[368,128]{1,0:T(8,128)(2,1)S(1)}, u32[]{:S(2)}, u32[]{:S(2)}) collective-permute-start(bf16[368,128]{1,0:T(8,128)(2,1)S(1)} %get-tuple-element.37), channel_id=1, source_target_pairs={{0,64},{1,65},{2,66},{3,67},{4,68},{5,69},{6,70},{7,71},{8,72},{9,... | collective-permute-start | bytes 282632 | tf_op jit(solution)/shard_map/ppermute | solution.py:719
  6.7 17.0 %collective-permute-start = (bf16[3,784,128]{2,1,0:T(8,128)(2,1)S(1)}, bf16[3,784,128]{2,1,0:T(8,128)(2,1)S(1)}, u32[]{:S(2)}, u32[]{:S(2)}) collective-permute-start(bf16[3,784,128]{2,1,0:T(8,128)(2,1)S(1)} %get-tuple-element.34), channel_id=1, source_target_pairs={{0,127},{1,2},{2,1},{3,4},{4,3},{5,6},{6,5},{7,8},{8,7},{9,10},{10... | collective-permute-start | bytes 1806344 | tf_op jit(solution)/shard_map/ppermute | solution.py:657
  11.2 12.5 %collective-permute-start.1 = (bf16[3,784,128]{2,1,0:T(8,128)(2,1)S(1)}, bf16[3,784,128]{2,1,0:T(8,128)(2,1)S(1)}, u32[]{:S(2)}, u32[]{:S(2)}) collective-permute-start(bf16[3,784,128]{2,1,0:T(8,128)(2,1)S(1)} %get-tuple-element.35), channel_id=1, source_target_pairs={{0,1},{1,0},{2,3},{3,2},{4,5},{5,4},{6,7},{7,6},{8,9},{9,8},{10,11... | collective-permute-start | bytes 1806344 | tf_op jit(solution)/shard_map/ppermute | solution.py:656
  14.3 13.2 %collective-permute-start.5 = (bf16[4,432,128]{2,1,0:T(8,128)(2,1)S(1)}, bf16[4,432,128]{2,1,0:T(8,128)(2,1)S(1)}, u32[]{:S(2)}, u32[]{:S(2)}) collective-permute-start(bf16[4,432,128]{2,1,0:T(8,128)(2,1)S(1)} %get-tuple-element.56), channel_id=1, source_target_pairs={{0,127},{1,2},{2,1},{3,4},{4,3},{5,6},{6,5},{7,8},{8,7},{9,10},{10... | collective-permute-start | bytes 1327112 | tf_op jit(solution)/shard_map/ppermute | solution.py:657
  17.3 10.3 %collective-permute-start.6 = (bf16[4,432,128]{2,1,0:T(8,128)(2,1)S(1)}, bf16[4,432,128]{2,1,0:T(8,128)(2,1)S(1)}, u32[]{:S(2)}, u32[]{:S(2)}) collective-permute-start(bf16[4,432,128]{2,1,0:T(8,128)(2,1)S(1)} %get-tuple-element.57), channel_id=1, source_target_pairs={{0,1},{1,0},{2,3},{3,2},{4,5},{5,4},{6,7},{7,6},{8,9},{9,8},{10,11... | collective-permute-start | bytes 1327112 | tf_op jit(solution)/shard_map/ppermute | solution.py:656
  19.3 11.7 %collective-permute-start.3 = (bf16[4,288,128]{2,1,0:T(8,128)(2,1)S(1)}, bf16[4,288,128]{2,1,0:T(8,128)(2,1)S(1)}, u32[]{:S(2)}, u32[]{:S(2)}) collective-permute-start(bf16[4,288,128]{2,1,0:T(8,128)(2,1)S(1)} %get-tuple-element.51), channel_id=1, source_target_pairs={{0,127},{1,2},{2,1},{3,4},{4,3},{5,6},{6,5},{7,8},{8,7},{9,10},{10... | collective-permute-start | bytes 884744 | tf_op jit(solution)/shard_map/ppermute | solution.py:657
  23.7 7.3 %collective-permute-start.4 = (bf16[4,288,128]{2,1,0:T(8,128)(2,1)S(1)}, bf16[4,288,128]{2,1,0:T(8,128)(2,1)S(1)}, u32[]{:S(2)}, u32[]{:S(2)}) collective-permute-start(bf16[4,288,128]{2,1,0:T(8,128)(2,1)S(1)} %get-tuple-element.52), channel_id=1, source_target_pairs={{0,1},{1,0},{2,3},{3,2},{4,5},{5,4},{6,7},{7,6},{8,9},{9,8},{10,11... | collective-permute-start | bytes 884744 | tf_op jit(solution)/shard_map/ppermute | solution.py:656

commit v8 on v7

--- a/solution.py
+++ b/solution.py
@@ -148,6 +148,19 @@
     return jnp.concatenate([direct, pltpu.roll(turned, 64, 1)], axis=0)
 
 
+def mixed(*generators):
+    values = {}
+    while len(values) < len(generators):
+        for i, one in enumerate(generators):
+            if i not in values:
+                try:
+                    next(one)
+                except StopIteration as end:
+                    values[i] = end.value
+        yield
+    return [values[i] for i in range(len(generators))]
+
+
 def packed_matrices(matrix):
     lane = lane_ids()
     half = len(matrix) // 2
@@ -169,6 +182,26 @@
         tail = jnp.where(lane < lev, pltpu.roll(rest, (64 - 8 * c) % LANES, 1), 0.0)
         rows.append(jnp.where(lane < 64, main, tail))
     return jnp.concatenate(rows, axis=0)
+
+
+def leaving_tables(slot_ref, keep_ref, spread_ref, far_group_ref):
+    slot = slot_ref[...]
+    leaving = slot // LANES != lax.axis_index(AXES)
+    row = lax.broadcasted_iota(jnp.int32, (LANES, LANES), 0)
+    col = lax.broadcasted_iota(jnp.int32, (LANES, LANES), 1)
+    ones = jnp.broadcast_to(leaving, (8, LANES)).astype(jnp.float32)
+    rank = jnp.dot(ones, (row <= col).astype(jnp.float32), preferred_element_type=jnp.float32)
+    yield
+    rank = (rank[0:1] + 0.5).astype(jnp.int32) - 1
+    spread = [(leaving & (rank + 64 * k == row)).astype(jnp.float32) for k in range(2)]
+    yield
+    keep = [jnp.transpose(half) for half in spread]
+    yield
+    for k in range(2):
+        spread_ref[:, k * LANES : (k + 1) * LANES] = spread[k].astype(jnp.bfloat16)
+        keep_ref[k * LANES : (k + 1) * LANES] = keep[k].astype(jnp.bfloat16)
+    group = jnp.broadcast_to(slot % LANES // 16, (8, LANES)).astype(jnp.float32)
+    far_group_ref[...] = jnp.dot(group, keep[0] + keep[1], preferred_element_type=jnp.float32)
 
 
 def pack_kernel(
@@ -189,25 +222,25 @@
     links_ref,
     sems,
 ):
-    pairs = [(inverse_hbm, inverse_ref), (wind_hbm, wind_ref), (links_hbm, links_ref)]
+    pairs = [(links_hbm, links_ref), (inverse_hbm, inverse_ref), (wind_hbm, wind_ref)]
     for at in chunks(state_ref):
         pairs += [(state_hbm.at[:, at], state_ref.at[:, at]), (prev_hbm.at[:, at], prev_ref.at[:, at])]
     copies = [pltpu.make_async_copy(a, b, sems.at[i]) for i, (a, b) in enumerate(pairs)]
     for copy in copies:
         copy.start()
+    copies[0].wait()
+    devices = lax.axis_size(AXES)
+    elements = links_ref.shape[2]
+    targets = edge_targets(links_ref, lax.axis_index(AXES) * elements, elements * devices)
     groups, lev = inverse_ref.shape[0], inverse_ref.shape[1]
-    copies[0].wait()
+    copies[1].wait()
     eye = lax.broadcasted_iota(jnp.int32, (lev, lev), 0) == lax.broadcasted_iota(jnp.int32, (lev, lev), 1)
     eye = eye.astype(jnp.float32)
     blank = jnp.zeros((lev, LANES - lev), jnp.float32)
     matrix = [jnp.concatenate([inverse_ref[c] - eye, blank], axis=1) for c in range(groups)]
     matrix_ref[...] = jnp.concatenate(matrix, axis=0).astype(jnp.bfloat16)
     packed_ref[...] = packed_matrices(matrix).astype(jnp.bfloat16)
-    copies[1].wait()
     copies[2].wait()
-    devices = lax.axis_size(AXES)
-    elements = links_ref.shape[2]
-    targets = edge_targets(links_ref, lax.axis_index(AXES) * elements, elements * devices)
     target_ref[...] = targets
     end = off_ref.shape[1]
     filler = jnp.zeros((8, LANES), jnp.float32)
@@ -242,14 +275,16 @@
     return [pl.ds(start, CHUNK) for start in range(0, ref.shape[1], CHUNK)]
 
 
-def in_turns(first, count, stages):
+def in_turns(first, count, stages, together=False):
     running = []
     for j in range(count):
         running.append(stages(pl.ds((first + j) * CHUNK, CHUNK), pl.ds(j * CHUNK, CHUNK), j))
     waiting, started = list(running), []
     while waiting or started:
-        if waiting:
+        while waiting:
             started.append(waiting.pop(0))
+            if not together:
+                break
         started = [one for one in started if next(one, started) is not started]
 
 
@@ -314,16 +349,21 @@
 
 
 class Physics:
-    def __init__(self, slot_ref, matrix_refs):
-        self.take(jnp.concatenate([ref[...] for ref in matrix_refs], axis=0) if matrix_refs else None)
+    def __init__(self, slot_ref):
         group = column_group(slot_ref)
+        self.here = group < 8
         self.group = jnp.concatenate([group, group], axis=1)
         self.inner = inner_lanes()
         self.chosen = sides()
 
-    def take(self, matrices):
-        if matrices is not None:
-            self.matrices = jnp.concatenate([matrices, matrices], axis=1)
+    def take_own(self, own_ref):
+        self.own = jnp.concatenate([own_ref[...], own_ref[...]], axis=1)
+
+    def take_far(self, far, keep_ref, spread_ref, far_group_ref):
+        self.far = far
+        self.keep, self.spread = keep_ref[...], spread_ref[...]
+        group = (far_group_ref[0:1, :] + 0.5).astype(jnp.int32)
+        self.far_group = jnp.concatenate([group, group], axis=1)
 
     def begin(self, wind_ref, target_ref, slope_ref):
         slots, _ = point_sets()
@@ -334,28 +374,47 @@
     def motion(self, state):
         return moved(state, self.slope, *self.blow)
 
-    def start(self, state, prev, motion):
+    def start(self, state, prev):
+        motion = self.motion(state)
+        yield
         total = jnp.dot(motion, self.sums, preferred_element_type=jnp.float32)
         return state + total + time_step * hermite(0)[0] * prev
 
-    def products(self, pairs, others=None, first=0):
+    def own_products(self, pairs):
         ahead, rows = None, []
-
-        def choose(k):
-            other = None
-            if others:
-                lev = others[k].shape[0] // 2
-                other = jnp.concatenate([others[k][:lev], others[k][lev:]], axis=1)
-            return as_rows(chosen_rows(ahead, self.group, other, first))
-
         for k, pair in enumerate(pairs):
-            product = jnp.dot(self.matrices, column_pair(pair), preferred_element_type=jnp.float32)
+            product = jnp.dot(self.own, column_pair(pair), preferred_element_type=jnp.float32)
             if k:
-                rows.append(choose(k - 1))
+                rows.append(as_rows(chosen_rows(ahead, self.group)))
             ahead = product
             yield
-        rows.append(choose(len(pairs) - 1))
+        rows.append(as_rows(chosen_rows(ahead, self.group)))
         return rows
+
+    def far_products(self, pairs):
+        high = [pair.astype(jnp.bfloat16) for pair in pairs]
+        both = [jnp.concatenate(high[k : k + 2], axis=1) for k in (0, 2)]
+        few = jnp.dot(jnp.concatenate(both, axis=0), self.keep, preferred_element_type=jnp.float32)
+        yield
+        size = pairs[0].shape[0]
+        lev = size // 2
+        blank = jnp.zeros((LANES - lev, 2 * LANES), jnp.float32)
+        products, rows = [], []
+        for k in range(2):
+            part = few[k * size : (k + 1) * size]
+            part = jnp.concatenate([part[:lev], part[lev:]], axis=1)
+            column = jnp.concatenate([part, blank], axis=0).astype(jnp.bfloat16)
+            products.append(jnp.dot(self.far, column, preferred_element_type=jnp.float32))
+            yield
+        for k in range(2):
+            rows.append(as_rows(chosen_rows(products[k], self.far_group)))
+        rows = jnp.concatenate(rows, axis=0).astype(jnp.bfloat16)
+        wide = jnp.dot(rows, self.spread, preferred_element_type=jnp.float32)
+        yield
+        return [wide[k * size : (k + 1) * size, c : c + LANES] for k in range(2) for c in (0, LANES)]
+
+    def merged(self, own, far):
+        return [jnp.where(self.here, a, b) for a, b in zip(own, far)]
 
     def finish(self, start, prev, tends, here_at, tend_ref, ahead_ref, off_ref, on_ref):
         late = time_step * hermite(0)[1]
@@ -379,22 +438,23 @@
 
 
 def own_kernel(
-    first, count, state_ref, prev_ref, wind_ref, target_ref, slope_ref, slot_ref, own_ref, part_ref, start_ref
+    first, count, state_ref, prev_ref, wind_ref, target_ref, slope_ref, slot_ref, own_ref, part_ref, start_ref, *tables
 ):
-    physics = Physics(slot_ref, [own_ref])
+    physics = Physics(slot_ref)
+    physics.take_own(own_ref)
     physics.begin(wind_ref, target_ref, slope_ref)
-    def stages(at, here_at, _):
-        state = flat(state_ref[:, at])
-        motion = physics.motion(state)
-        yield
-        start = physics.start(state, flat(prev_ref[:, at]), motion)
+
+    def stages(at, here_at, j):
+        parts, start, *_ = yield from mixed(
+            physics.own_products([state_ref[k, at] for k in range(PARTS)]),
+            physics.start(flat(state_ref[:, at]), flat(prev_ref[:, at])),
+            *([leaving_tables(slot_ref, *tables)] if j == 0 else []),
+        )
         start_ref[:, here_at] = start.reshape(PARTS, CHUNK, LANES)
-        yield
-        parts = yield from physics.products([state_ref[k, at] for k in range(PARTS)])
         for k, part in enumerate(parts):
             part_ref[k, here_at] = part
 
-    in_turns(first, count, stages)
+    in_turns(first, count, stages, True)
 
 
 def far_kernel(
@@ -404,6 +464,9 @@
     prev_ref,
     slot_ref,
     packed_ref,
+    keep_ref,
+    spread_ref,
+    far_group_ref,
     part_ref,
     start_ref,
     tend_ref,
@@ -412,20 +475,19 @@
     on_ref,
     far_ref,
 ):
-    physics = Physics(slot_ref, [])
+    physics = Physics(slot_ref)
     matrices = unpacked_matrices(packed_ref[...].astype(jnp.float32)).astype(jnp.bfloat16)
     far_ref[...] = matrices
-    physics.take(matrices)
+    physics.take_far(matrices, keep_ref, spread_ref, far_group_ref)
 
     def stages(at, here_at, _):
-        tends = yield from physics.products(
-            [state_ref[k, at] for k in range(PARTS)], [part_ref[k, here_at] for k in range(PARTS)], 8
-        )
+        far = yield from physics.far_products([state_ref[k, at] for k in range(PARTS)])
+        tends = physics.merged([part_ref[k, here_at] for k in range(PARTS)], far)
         start = [start_ref[k, here_at] for k in range(PARTS)]
         prev = [prev_ref[k, at].astype(jnp.float32) for k in range(PARTS)]
         physics.finish(start, prev, tends, here_at, tend_ref, ahead_ref, off_ref, on_ref)
 
-    in_turns(first, count, stages)
+    in_turns(first, count, stages, True)
 
 
 def physics_kernel(
@@ -439,26 +501,32 @@
     slot_ref,
     own_ref,
     far_ref,
+    keep_ref,
+    spread_ref,
+    far_group_ref,
     tend_ref,
     ahead_ref,
     off_ref,
     on_ref,
 ):
-    physics = Physics(slot_ref, [own_ref, far_ref])
+    physics = Physics(slot_ref)
+    physics.take_own(own_ref)
+    physics.take_far(far_ref[...], keep_ref, spread_ref, far_group_ref)
     physics.begin(wind_ref, target_ref, slope_ref)
 
     def stages(at, here_at, _):
-        state = flat(state_ref[:, at])
-        motion = physics.motion(state)
-        yield
-        start = physics.start(state, flat(prev_ref[:, at]), motion)
+        pairs = [state_ref[k, at] for k in range(PARTS)]
+        far, own, start = yield from mixed(
+            physics.far_products(pairs),
+            physics.own_products(pairs),
+            physics.start(flat(state_ref[:, at]), flat(prev_ref[:, at])),
+        )
         start = [start[k * CHUNK : (k + 1) * CHUNK] for k in range(PARTS)]
-        yield
-        tends = yield from physics.products([state_ref[k, at] for k in range(PARTS)])
+        tends = physics.merged(own, far)
         prev = [prev_ref[k, at].astype(jnp.float32) for k in range(PARTS)]
         physics.finish(start, prev, tends, here_at, tend_ref, ahead_ref, off_ref, on_ref)
 
-    in_turns(first, count, stages)
+    in_turns(first, count, stages, True)
 
 
 def near_kernel(
@@ -644,7 +712,7 @@
                 )
                 copies[-1].start()
 
-    in_turns(first, out_ref.shape[1] // CHUNK, stages)
+    in_turns(first, out_ref.shape[1] // CHUNK, stages, last)
     for copy in copies:
         copy.wait()
 
@@ -725,18 +793,19 @@
         size = count * CHUNK
         outs = (like(4, bf16, size), like(4, f32, size), like(4, bf16, size), like(4, bf16, size))
         if first == 0:
-            part, start = call(
+            part, start, *tables = call(
                 functools.partial(own_kernel, first, count),
                 (state, prev) + shared,
-                (like(4, f32, size), like(4, f32, size)),
+                (like(4, f32, size), like(4, f32, size))
+                + (table(bf16, 2 * LANES, LANES), table(bf16, LANES, 2 * LANES), table(f32, 8, LANES)),
                 "own",
                 3 * count,
             )
-            ins = (state, prev, slot, far_packed, part, start)
+            ins = (state, prev, slot, far_packed, *tables, part, start)
             body, name = far_kernel, "far"
             outs += (table(bf16, *matrices.shape),)
         else:
-            ins = (state, prev) + shared + (far_matrices,)
+            ins = (state, prev) + shared + (far_matrices, *tables)
             body, name = physics_kernel, "physics"
         tend, ahead, to_off, to_on, *more = call(
             functools.partial(body, first, count), ins, outs, name, 5 * count

time: 33.9 us -> 33.3 us (0.982)
  Pallas kernels: 15.2 us -> 14.4 us
    pallas_call x7, Pallas kernels: 15.2 us -> 14.4 us  [call(): pl.pallas_call(body, out_shape=outs, compiler_params=params, cost_estimat...]
  transfers between devices with their start and end apart: 7 -> 7, of which waited for: 2 -> 2; matrix products, arithmetic and copies ran while one was open for 0% -> 0% of each run, Pallas kernels for 31% -> 30%
where the time goes in v8:
time: 33.3 us; the launch traced here: 33.2 us
  starting transfers between devices  15.9 us (48%)
  Pallas kernels  14.4 us (43%)
  waiting for transfers between devices  1.99 us (6%)
  between operations  0.88 us (3%)
    pallas_call x7, Pallas kernels, call(): pl.pallas_call(body, out_shape=outs, compiler_params=params, cost_estimat...  14.4 us
    ppermute x3, starting transfers between devices, exchanged(): return (lax.ppermute(off, AXES, across), on)  11.9 us
    ppermute x1, starting transfers between devices, per_device(): lax.ppermute(packed, AXES, [(i, i ^ devices // 2) for i in range(devices)])  4.04 us
    ppermute x3, waiting for transfers between devices, exchanged(): return (lax.ppermute(off, AXES, across), on)  1.98 us
  transfers between devices with their start and end apart: 7, of which 2 were waited for; matrix products, arithmetic and copies ran while one was open for 0% of the time, Pallas kernels for 30%

profile of v8, /device:TPU:0, one launch (start us, length us, event | category | flops | bytes accessed | tf_op | source)
XLA Modules:
  0.0 33.2 jit_solution(10797308876870674971)
XLA Ops:
  0.6 0.0 copy-start.1
  0.6 0.0 copy-start
  0.7 1.9 %pack.1 = (bf16[576,128]{1,0:T(8,128)(2,1)S(1)}, bf16[368,128]{1,0:T(8,128)(2,1)S(1)}, bf16[3,784,128]{2,1,0:T(8,128)(2,1)S(1)}, bf16[3,784,128]{2,1,0:T(8,128)(...) custom-call(f32[8,72,72]{2,1,0:T(8,128)} %inverse_hbm.1, ...), custom_call_target="tpu_custom_call" | custom-call | flops 754974720 | bytes 4903424 | tf_op jit(solution)/shard_map/pack/pallas_call | solution.py:750
  2.6 4.0 %collective-permute-start.2 = (bf16[368,128]{1,0:T(8,128)(2,1)S(1)}, bf16[368,128]{1,0:T(8,128)(2,1)S(1)}, u32[]{:S(2)}, u32[]{:S(2)}) collective-permute-start(bf16[368,128]{1,0:T(8,128)(2,1)S(1)} %get-tuple-element.40), channel_id=1, source_target_pairs={{0,64},{1,65},{2,66},{3,67},{4,68},{5,69},{6,70},{7,71},{8,72},{9,... | collective-permute-start | bytes 282632 | tf_op jit(solution)/shard_map/ppermute | solution.py:787
  6.6 4.5 %collective-permute-start = (bf16[3,784,128]{2,1,0:T(8,128)(2,1)S(1)}, bf16[3,784,128]{2,1,0:T(8,128)(2,1)S(1)}, u32[]{:S(2)}, u32[]{:S(2)}) collective-permute-start(bf16[3,784,128]{2,1,0:T(8,128)(2,1)S(1)} %get-tuple-element.37), channel_id=1, source_target_pairs={{0,127},{1,2},{2,1},{3,4},{4,3},{5,6},{6,5},{7,8},{8,7},{9,10},{10... | collective-permute-start | bytes 1806344 | tf_op jit(solution)/shard_map/ppermute | solution.py:725
  11.2 0.0 collective-permute-start.1
  11.2 0.0 copy-done.1
  11.2 0.0 copy-done
  11.2 1.5 %own.1 = (f32[4,432,128]{2,1,0:T(8,128)S(1)}, f32[4,432,128]{2,1,0:T(8,128)S(1)}, bf16[256,128]{1,0:T(8,128)(2,1)S(1)}, bf16[128,256]{1,0:T(8,128)(2,1)S(1)}, f32[8,128]{1,0:T(8,128)S(1)}) custom-call(f32[4,720,128]{2,1,0:T(8,128)S(1)} %get-tuple-element.34.state_ref, bf16[4,720,128]{2,1,0:T(8,128)(2,1)S(1)} %get-tuple-element.39.prev_ref, ...), custom_call_target="tpu_custom_call" | custom-call | flops 3397386240 | bytes 5137408 | tf_op jit(solution)/shard_map/own/pallas_call | solution.py:750
  12.7 0.0 collective-permute-done.2.packed_ref
  12.7 1.2 %far.1 = (bf16[4,432,128]{2,1,0:T(8,128)(2,1)S(1)}, f32[4,432,128]{2,1,0:T(8,128)S(1)}, bf16[4,432,128]{2,1,0:T(8,128)(2,1)S(1)}, bf16[4,432,128]{2,1,0:T(8,128)(2,1)S(1)}, bf16[576,128]{1,0:T(8,128)(2,1)S(1)}) custom-call(f32[4,720,128]{2,1,0:T(8,128)S(1)} %get-tuple-element.34.state_ref, bf16[4,720,128]{2,1,0:T(8,128)(2,1)S(1)} %get-tuple-element.39.prev_ref, ...), custom_call_target="tpu_custom_call" | custom-call | flops 5662310400 | bytes 8422400 | tf_op jit(solution)/shard_map/far/pallas_call | solution.py:750
  13.9 3.2 %collective-permute-start.5 = (bf16[4,432,128]{2,1,0:T(8,128)(2,1)S(1)}, bf16[4,432,128]{2,1,0:T(8,128)(2,1)S(1)}, u32[]{:S(2)}, u32[]{:S(2)}) collective-permute-start(bf16[4,432,128]{2,1,0:T(8,128)(2,1)S(1)} %get-tuple-element.62), channel_id=1, source_target_pairs={{0,127},{1,2},{2,1},{3,4},{4,3},{5,6},{6,5},{7,8},{8,7},{9,10},{10... | collective-permute-start | bytes 1327112 | tf_op jit(solution)/shard_map/ppermute | solution.py:725
  17.1 0.0 collective-permute-start.6
  17.1 1.7 %physics.1 = (bf16[4,288,128]{2,1,0:T(8,128)(2,1)S(1)}, f32[4,288,128]{2,1,0:T(8,128)S(1)}, bf16[4,288,128]{2,1,0:T(8,128)(2,1)S(1)}, bf16[4,288,128]{2,1,0:T(8,128)(2,1)S(1)}) custom-call(f32[4,720,128]{2,1,0:T(8,128)S(1)} %get-tuple-element.34.state_ref, bf16[4,720,128]{2,1,0:T(8,128)(2,1)S(1)} %get-tuple-element.39.prev_ref, ...), custom_call_target="tpu_custom_call" | custom-call | flops 3774873600 | bytes 5702656 | tf_op jit(solution)/shard_map/physics/pallas_call | solution.py:750
  18.8 4.2 %collective-permute-start.3 = (bf16[4,288,128]{2,1,0:T(8,128)(2,1)S(1)}, bf16[4,288,128]{2,1,0:T(8,128)(2,1)S(1)}, u32[]{:S(2)}, u32[]{:S(2)}) collective-permute-start(bf16[4,288,128]{2,1,0:T(8,128)(2,1)S(1)} %get-tuple-element.57), channel_id=1, source_target_pairs={{0,127},{1,2},{2,1},{3,4},{4,3},{5,6},{6,5},{7,8},{8,7},{9,10},{10... | collective-permute-start | bytes 884744 | tf_op jit(solution)/shard_map/ppermute | solution.py:725
  23.0 0.0 collective-permute-done.off_ref
  23.0 0.0 collective-permute-start.4
  23.0 0.0 collective-permute-done.1.on_ref
  23.0 2.9 %near.1 = (f32[4,720,128]{2,1,0:T(8,128)S(1)}, f32[4,720,128]{2,1,0:T(8,128)S(1)}, f32[4,720,128]{2,1,0:T(8,128)S(1)}, f32[4,720,128]{2,1,0:T(8,128)S(1)}, f32[4...) custom-call(f32[4,720,128]{2,1,0:T(8,128)S(1)} %get-tuple-element.34, ...), custom_call_target="tpu_custom_call" | custom-call | flops 6039797760 | bytes 11673600 | tf_op jit(solution)/shard_map/near/pallas_call | solution.py:750
  26.0 1.2 %collective-permute-done.5.off_ref = bf16[4,432,128]{2,1,0:T(8,128)(2,1)S(1)} collective-permute-done((bf16[4,432,128]{2,1,0:T(8,128)(2,1)S(1)}, bf16[4,432,128]{2,1,0:T(8,128)(2,1)S(1)}, u32[]{:S(2)}, u32[]{:S(2)}) %collective-permute-start.5) | collective-permute-done | bytes 442400 | tf_op jit(solution)/shard_map/ppermute | solution.py:725
  27.2 0.0 collective-permute-done.6.on_ref
  27.2 2.5 %advance.2 = (f32[4,432,128]{2,1,0:T(8,128)S(1)}, bf16[4,720,128]{2,1,0:T(8,128)(2,1)}) custom-call(f32[4,720,128]{2,1,0:T(8,128)S(1)} %get-tuple-element.52.own_ref, f32[4,720,128]{2,1,0:T(8,128)S(1)} %get-tuple-element.53.near_ref, f32[4,720,128]{2,1,0:T(8,128)S(1)} %get-tuple-element.54.near_add_ref, f32[4,720,128]{2,1,0:T(8,128)S(1)} %get-tuple-element.55.own_force_ref, ...), custom_call_target="tpu_custom_call" | custom-call | flops 5662310400 | bytes 20152320 | tf_op jit(solution)/shard_map/advance/pallas_call | solution.py:750
  29.7 0.8 %collective-permute-done.3.off_ref = bf16[4,288,128]{2,1,0:T(8,128)(2,1)S(1)} collective-permute-done((bf16[4,288,128]{2,1,0:T(8,128)(2,1)S(1)}, bf16[4,288,128]{2,1,0:T(8,128)(2,1)S(1)}, u32[]{:S(2)}, u32[]{:S(2)}) %collective-permute-start.3) | collective-permute-done | bytes 294944 | tf_op jit(solution)/shard_map/ppermute | solution.py:725
  30.5 0.0 collective-permute-done.4.on_ref
  30.5 2.5 %advance.3 = f32[4,720,128]{2,1,0:T(8,128)} custom-call(f32[4,720,128]{2,1,0:T(8,128)S(1)} %get-tuple-element.52.own_ref, f32[4,720,128]{2,1,0:T(8,128)S(1)} %get-tuple-element.53.near_ref, f32[4,720,128]{2,1,0:T(8,128)S(1)} %get-tuple-element.54.near_add_ref, f32[4,720,128]{2,1,0:T(8,128)S(1)} %get-tuple-element.55.own_force_ref, ...), custom_call_target="tpu_custom_call" | custom-call | flops 3774873600 | bytes 20447232 | tf_op jit(solution)/shard_map/advance/pallas_call | solution.py:750
Async XLA Ops:
  0.6 10.5 %copy-start.1 = (bf16[256,256]{1,0:T(8,128)(2,1)S(1)}, bf16[256,256]{1,0:T(8,128)(2,1)}, u32[]{:S(2)}) copy-start(bf16[256,256]{1,0:T(8,128)(2,1)} %constant.2.clone.slope_ref) | copy-start | bytes 393220
  0.6 10.5 %copy-start = (s32[128]{0:T(128)S(1)}, s32[128]{0:T(128)}, u32[]{:S(2)}) copy-start(s32[128]{0:T(128)} %param.11) | copy-start | bytes 1540
  2.6 10.1 %collective-permute-start.2 = (bf16[368,128]{1,0:T(8,128)(2,1)S(1)}, bf16[368,128]{1,0:T(8,128)(2,1)S(1)}, u32[]{:S(2)}, u32[]{:S(2)}) collective-permute-start(bf16[368,128]{1,0:T(8,128)(2,1)S(1)} %get-tuple-element.40), channel_id=1, source_target_pairs={{0,64},{1,65},{2,66},{3,67},{4,68},{5,69},{6,70},{7,71},{8,72},{9,... | collective-permute-start | bytes 282632 | tf_op jit(solution)/shard_map/ppermute | solution.py:787
  6.6 16.4 %collective-permute-start = (bf16[3,784,128]{2,1,0:T(8,128)(2,1)S(1)}, bf16[3,784,128]{2,1,0:T(8,128)(2,1)S(1)}, u32[]{:S(2)}, u32[]{:S(2)}) collective-permute-start(bf16[3,784,128]{2,1,0:T(8,128)(2,1)S(1)} %get-tuple-element.37), channel_id=1, source_target_pairs={{0,127},{1,2},{2,1},{3,4},{4,3},{5,6},{6,5},{7,8},{8,7},{9,10},{10... | collective-permute-start | bytes 1806344 | tf_op jit(solution)/shard_map/ppermute | solution.py:725
  11.2 11.9 %collective-permute-start.1 = (bf16[3,784,128]{2,1,0:T(8,128)(2,1)S(1)}, bf16[3,784,128]{2,1,0:T(8,128)(2,1)S(1)}, u32[]{:S(2)}, u32[]{:S(2)}) collective-permute-start(bf16[3,784,128]{2,1,0:T(8,128)(2,1)S(1)} %get-tuple-element.38), channel_id=1, source_target_pairs={{0,1},{1,0},{2,3},{3,2},{4,5},{5,4},{6,7},{7,6},{8,9},{9,8},{10,11... | collective-permute-start | bytes 1806344 | tf_op jit(solution)/shard_map/ppermute | solution.py:724
  13.9 13.2 %collective-permute-start.5 = (bf16[4,432,128]{2,1,0:T(8,128)(2,1)S(1)}, bf16[4,432,128]{2,1,0:T(8,128)(2,1)S(1)}, u32[]{:S(2)}, u32[]{:S(2)}) collective-permute-start(bf16[4,432,128]{2,1,0:T(8,128)(2,1)S(1)} %get-tuple-element.62), channel_id=1, source_target_pairs={{0,127},{1,2},{2,1},{3,4},{4,3},{5,6},{6,5},{7,8},{8,7},{9,10},{10... | collective-permute-start | bytes 1327112 | tf_op jit(solution)/shard_map/ppermute | solution.py:725
  17.1 10.1 %collective-permute-start.6 = (bf16[4,432,128]{2,1,0:T(8,128)(2,1)S(1)}, bf16[4,432,128]{2,1,0:T(8,128)(2,1)S(1)}, u32[]{:S(2)}, u32[]{:S(2)}) collective-permute-start(bf16[4,432,128]{2,1,0:T(8,128)(2,1)S(1)} %get-tuple-element.63), channel_id=1, source_target_pairs={{0,1},{1,0},{2,3},{3,2},{4,5},{5,4},{6,7},{7,6},{8,9},{9,8},{10,11... | collective-permute-start | bytes 1327112 | tf_op jit(solution)/shard_map/ppermute | solution.py:724
  18.8 11.7 %collective-permute-start.3 = (bf16[4,288,128]{2,1,0:T(8,128)(2,1)S(1)}, bf16[4,288,128]{2,1,0:T(8,128)(2,1)S(1)}, u32[]{:S(2)}, u32[]{:S(2)}) collective-permute-start(bf16[4,288,128]{2,1,0:T(8,128)(2,1)S(1)} %get-tuple-element.57), channel_id=1, source_target_pairs={{0,127},{1,2},{2,1},{3,4},{4,3},{5,6},{6,5},{7,8},{8,7},{9,10},{10... | collective-permute-start | bytes 884744 | tf_op jit(solution)/shard_map/ppermute | solution.py:725
  23.0 7.5 %collective-permute-start.4 = (bf16[4,288,128]{2,1,0:T(8,128)(2,1)S(1)}, bf16[4,288,128]{2,1,0:T(8,128)(2,1)S(1)}, u32[]{:S(2)}, u32[]{:S(2)}) collective-permute-start(bf16[4,288,128]{2,1,0:T(8,128)(2,1)S(1)} %get-tuple-element.58), channel_id=1, source_target_pairs={{0,1},{1,0},{2,3},{3,2},{4,5},{5,4},{6,7},{7,6},{8,9},{9,8},{10,11... | collective-permute-start | bytes 884744 | tf_op jit(solution)/shard_map/ppermute | solution.py:724

commit v9 on v8

--- a/solution.py
+++ b/solution.py
@@ -159,6 +159,24 @@
                     values[i] = end.value
         yield
     return [values[i] for i in range(len(generators))]
+
+
+def packed_quarters(value, first_off, first_on):
+    quarter = lane_ids() // 32
+    to_off = to_on = jnp.zeros(value[0].shape, jnp.float32)
+    for k, turned in enumerate(value):
+        turned = pltpu.roll(turned, 32 * k, 1) if k else turned
+        to_off = jnp.where(quarter == (first_off + k) % 4, turned, to_off)
+        to_on = jnp.where(quarter == (first_on + k) % 4, turned, to_on)
+    return to_off, to_on
+
+
+def whole_quarters(off, on, chosen):
+    kept = [jnp.where(chosen, off, on)]
+    for k in range(1, PARTS):
+        turned = [pltpu.roll(side, LANES - 32 * k, 1) for side in (off, on)]
+        kept.append(jnp.where(chosen, *turned))
+    return jnp.concatenate(kept, axis=0)
 
 
 def packed_matrices(matrix):
@@ -333,6 +351,7 @@
         total = (row == lax.broadcasted_iota(jnp.int32, (LANES, LANES), 1)).astype(jnp.float32)
     place = {
         "own": row,
+        "own turned": jnp.where(row < 64, row + 64, row - 64),
         "near": jnp.where(row < 64, row + LANES, row - LANES),
         "near turned": jnp.where(row < 64, row - 64, row + 64),
         "outer": jnp.where(row < 64, row - LANES, row + LANES),
@@ -370,6 +389,19 @@
         self.sums = sum_block("own", target_ref[...].astype(jnp.int32) - 32, slots, True)
         self.blow = [-time_step * wind_ref[d] for d in range(2)]
         self.slope = slope_ref[...]
+        self.targets, self.slots = target_ref[...].astype(jnp.int32) - 32, slots
+
+    def begin_cross(self):
+        row = lax.broadcasted_iota(jnp.int32, (LANES, LANES), 0)
+        col = lax.broadcasted_iota(jnp.int32, (LANES, LANES), 1) // 32
+        blocks = []
+        for turn in (0, 64):
+            place = (row + turn) % LANES // 32
+            crossing = ((place == 1) & (col == 2)) | ((place == 2) & (col == 1))
+            block = sum_block("own turned" if turn else "own", self.targets, self.slots, False)
+            blocks.append(jnp.where(crossing, block.astype(jnp.float32), 0.0).astype(jnp.bfloat16))
+        self.cross = jnp.concatenate(blocks, axis=1)
+        self.cross_blow = [jnp.where(self.inner, w, pltpu.roll(w, 64, 1)) for w in self.blow]
 
     def motion(self, state):
         return moved(state, self.slope, *self.blow)
@@ -416,7 +448,7 @@
     def merged(self, own, far):
         return [jnp.where(self.here, a, b) for a, b in zip(own, far)]
 
-    def finish(self, start, prev, tends, here_at, tend_ref, ahead_ref, off_ref, on_ref):
+    def finish(self, start, prev, tends, here_at, tend_ref, ahead_ref, off_ref, on_ref, lean=False):
         late = time_step * hermite(0)[1]
         early_1, late_1 = (time_step * w for w in hermite(1))
         ahead, force = [], []
@@ -427,14 +459,27 @@
             ahead.append(start[k] + late * tend)
             ahead_ref[k, here_at] = ahead[k]
             force.append(jnp.where(self.inner, early_1 * prev[k] + late_1 * tend, tend))
+        middle = [jnp.where(self.inner, ahead[k], pltpu.roll(ahead[k + 2], 64, 1)) for k in range(2)]
+        if lean:
+            motion = moved(jnp.concatenate(middle, axis=0), self.slope, *self.cross_blow)
+            yield
+            cross = jnp.dot(motion, self.cross, preferred_element_type=jnp.float32)
+            yield
+            for k in range(PARTS):
+                rows = slice(k % 2 * CHUNK, (k % 2 + 1) * CHUNK)
+                force[k] = force[k] + cross[rows, k // 2 * LANES : (k // 2 + 1) * LANES]
+            to_off, to_on = packed_quarters(ahead, jnp.where(on_odd(), 2, 1), jnp.where(on_odd(), 1, 2))
+            off_ref[0, here_at] = to_off.astype(jnp.bfloat16)
+            on_ref[0, here_at] = to_on.astype(jnp.bfloat16)
+        else:
+            for k in range(2):
+                off_ref[k, here_at] = middle[k].astype(jnp.bfloat16)
+                on_ref[k, here_at] = middle[k].astype(jnp.bfloat16)
         off, on = packed_halves(force, self.chosen)
+        at = off_ref.shape[0] - 2
         for k in range(2):
-            middle = jnp.where(self.inner, ahead[k], pltpu.roll(ahead[k + 2], 64, 1))
-            middle = middle.astype(jnp.bfloat16)
-            off_ref[k, here_at] = middle
-            on_ref[k, here_at] = middle
-            off_ref[2 + k, here_at] = off[k].astype(jnp.bfloat16)
-            on_ref[2 + k, here_at] = on[k].astype(jnp.bfloat16)
+            off_ref[at + k, here_at] = off[k].astype(jnp.bfloat16)
+            on_ref[at + k, here_at] = on[k].astype(jnp.bfloat16)
 
 
 def own_kernel(
@@ -485,7 +530,7 @@
         tends = physics.merged([part_ref[k, here_at] for k in range(PARTS)], far)
         start = [start_ref[k, here_at] for k in range(PARTS)]
         prev = [prev_ref[k, at].astype(jnp.float32) for k in range(PARTS)]
-        physics.finish(start, prev, tends, here_at, tend_ref, ahead_ref, off_ref, on_ref)
+        yield from physics.finish(start, prev, tends, here_at, tend_ref, ahead_ref, off_ref, on_ref)
 
     in_turns(first, count, stages, True)
 
@@ -513,6 +558,7 @@
     physics.take_own(own_ref)
     physics.take_far(far_ref[...], keep_ref, spread_ref, far_group_ref)
     physics.begin(wind_ref, target_ref, slope_ref)
+    physics.begin_cross()
 
     def stages(at, here_at, _):
         pairs = [state_ref[k, at] for k in range(PARTS)]
@@ -524,7 +570,7 @@
         start = [start[k * CHUNK : (k + 1) * CHUNK] for k in range(PARTS)]
         tends = physics.merged(own, far)
         prev = [prev_ref[k, at].astype(jnp.float32) for k in range(PARTS)]
-        physics.finish(start, prev, tends, here_at, tend_ref, ahead_ref, off_ref, on_ref)
+        yield from physics.finish(start, prev, tends, here_at, tend_ref, ahead_ref, off_ref, on_ref, True)
 
     in_turns(first, count, stages, True)
 
@@ -568,6 +614,8 @@
     sum_ref[:LANES] = own_sums
     sum_ref[LANES:] = near_sums
     nothing = jnp.zeros((LANES, LANES), jnp.bfloat16)
+    first_sums = jnp.concatenate([nothing, own_sums[:, LANES:]], axis=1)
+    first_sums = jnp.concatenate([near_sums, first_sums], axis=0)
     for k, turn in enumerate(("", " turned")):
         edge_sum_ref[k, :LANES] = near_sums
         edge_sum_ref[k, LANES:, :LANES] = nothing
@@ -597,15 +645,10 @@
         own_move = moved(flat(state_ref[:, at]), slope, *own_blow)
         near_move = moved(near, slope, *near_blow)
         yield
-        total = jnp.dot(near_move, near_sums, preferred_element_type=jnp.float32)
-        near_total = total[:, LANES:] + jnp.dot(
-            own_move, own_sums[:, LANES:], preferred_element_type=jnp.float32
-        )
-        kept = [jnp.where(chosen, off[2], on[2])]
-        for k in range(1, PARTS):
-            turned = [pltpu.roll(side[2], LANES - 32 * k, 1) for side in (off, on)]
-            kept.append(jnp.where(chosen, *turned))
-        kept = jnp.where(inner, 0.0, jnp.concatenate(kept, axis=0))
+        total = jnp.concatenate([near_move, own_move], axis=1)
+        total = jnp.dot(total, first_sums, preferred_element_type=jnp.float32)
+        near_total = total[:, LANES:]
+        kept = jnp.where(inner, 0.0, whole_quarters(off[2], on[2], chosen))
         near = near + near_total + early * kept
         near_ref[:, at] = near.reshape(PARTS, CHUNK, LANES)
         near_force_ref[:, at] = (early_2 * kept).reshape(PARTS, CHUNK, LANES)
@@ -677,15 +720,21 @@
 
     def stages(at, here_at, j):
         off, on = off_ref[:, here_at].astype(jnp.float32), on_ref[:, here_at].astype(jnp.float32)
-        off_mid, on_mid = flat(off[:2]), flat(on[:2])
-        middle = [jnp.where(chosen, off_mid, on_mid), jnp.where(chosen, on_mid, off_mid)]
-        middle = jnp.concatenate([middle[0], pltpu.roll(middle[1], 64, 1)], axis=0)
-        outer = jnp.where(chosen == inner, on_mid, off_mid)
-        received = whole_halves(off[2:], on[2:], chosen)
+        if last:
+            middle = whole_quarters(off[0], on[0], chosen)
+        else:
+            off_mid, on_mid = flat(off[:2]), flat(on[:2])
+            middle = [jnp.where(chosen, off_mid, on_mid), jnp.where(chosen, on_mid, off_mid)]
+            middle = jnp.concatenate([middle[0], pltpu.roll(middle[1], 64, 1)], axis=0)
+            outer = jnp.where(chosen == inner, on_mid, off_mid)
+        received = whole_halves(off[-2:], on[-2:], chosen)
         near = jnp.where(inner, middle, flat(near_ref[:, at]) + lates[0] * received)
-        moves = advect(near, 1), advect(outer, 2)
-        yield
-        total = gather_shared(*moves, 0, 2 * LANES)
+        moves = [advect(near, 1)] if last else [advect(near, 1), advect(outer, 2)]
+        yield
+        if last:
+            total = jnp.dot(moves[0], sum_ref[LANES:], preferred_element_type=jnp.float32)
+        else:
+            total = gather_shared(*moves, 0, 2 * LANES)
         own = flat(own_ref[:, at]) + total[:, :LANES]
         force = received * jnp.where(inner, 1.0, lates[1])
         near = near + total[:, LANES:] + (flat(near_add_ref[:, at]) + force)
@@ -791,7 +840,8 @@
     shared = (wind, targets, slope, slot, matrices)
     for count in SPLIT:
         size = count * CHUNK
-        outs = (like(4, bf16, size), like(4, f32, size), like(4, bf16, size), like(4, bf16, size))
+        sent = like(3 if first else 4, bf16, size)
+        outs = (like(4, bf16, size), like(4, f32, size), sent, sent)
         if first == 0:
             part, start, *tables = call(
                 functools.partial(own_kernel, first, count),

time: 33.3 us -> 32.9 us (0.988)
  waiting for transfers between devices: 1.99 us -> 1.33 us
    ppermute x3, waiting for transfers between devices: 1.98 us -> 1.32 us  [exchanged(): return (lax.ppermute(off, AXES, across), on)]
  transfers between devices with their start and end apart: 7 -> 7, of which waited for: 2 -> 2; matrix products, arithmetic and copies ran while one was open for 0% -> 0% of each run, Pallas kernels for 30% -> 31%
where the time goes in v9:
time: 32.9 us; the launch traced here: 32.6 us
  starting transfers between devices  15.9 us (48%)
  Pallas kernels  14.5 us (44%)
  waiting for transfers between devices  1.33 us (4%)
  between operations  0.87 us (3%)
    pallas_call x7, Pallas kernels, call(): pl.pallas_call(body, out_shape=outs, compiler_params=params, cost_estimat...  14.5 us
    ppermute x3, starting transfers between devices, exchanged(): return (lax.ppermute(off, AXES, across), on)  11.9 us
    ppermute x1, starting transfers between devices, per_device(): lax.ppermute(packed, AXES, [(i, i ^ devices // 2) for i in range(devices)])  4.04 us
    ppermute x3, waiting for transfers between devices, exchanged(): return (lax.ppermute(off, AXES, across), on)  1.32 us
  transfers between devices with their start and end apart: 7, of which 2 were waited for; matrix products, arithmetic and copies ran while one was open for 0% of the time, Pallas kernels for 31%

profile of v9, /device:TPU:0, one launch (start us, length us, event | category | flops | bytes accessed | tf_op | source)
XLA Modules:
  0.0 32.6 jit_solution(2536573647519863274)
XLA Ops:
  0.6 0.0 copy-start.1
  0.6 0.0 copy-start
  0.7 1.9 %pack.1 = (bf16[576,128]{1,0:T(8,128)(2,1)S(1)}, bf16[368,128]{1,0:T(8,128)(2,1)S(1)}, bf16[3,784,128]{2,1,0:T(8,128)(2,1)S(1)}, bf16[3,784,128]{2,1,0:T(8,128)(...) custom-call(f32[8,72,72]{2,1,0:T(8,128)} %inverse_hbm.1, ...), custom_call_target="tpu_custom_call" | custom-call | flops 754974720 | bytes 4903424 | tf_op jit(solution)/shard_map/pack/pallas_call | solution.py:799
  2.6 4.0 %collective-permute-start.2 = (bf16[368,128]{1,0:T(8,128)(2,1)S(1)}, bf16[368,128]{1,0:T(8,128)(2,1)S(1)}, u32[]{:S(2)}, u32[]{:S(2)}) collective-permute-start(bf16[368,128]{1,0:T(8,128)(2,1)S(1)} %get-tuple-element.40), channel_id=1, source_target_pairs={{0,64},{1,65},{2,66},{3,67},{4,68},{5,69},{6,70},{7,71},{8,72},{9,... | collective-permute-start | bytes 282632 | tf_op jit(solution)/shard_map/ppermute | solution.py:836
  6.6 4.5 %collective-permute-start = (bf16[3,784,128]{2,1,0:T(8,128)(2,1)S(1)}, bf16[3,784,128]{2,1,0:T(8,128)(2,1)S(1)}, u32[]{:S(2)}, u32[]{:S(2)}) collective-permute-start(bf16[3,784,128]{2,1,0:T(8,128)(2,1)S(1)} %get-tuple-element.37), channel_id=1, source_target_pairs={{0,127},{1,2},{2,1},{3,4},{4,3},{5,6},{6,5},{7,8},{8,7},{9,10},{10... | collective-permute-start | bytes 1806344 | tf_op jit(solution)/shard_map/ppermute | solution.py:774
  11.2 0.0 collective-permute-start.1
  11.2 0.0 copy-done.1
  11.2 0.0 copy-done
  11.2 1.5 %own.1 = (f32[4,432,128]{2,1,0:T(8,128)S(1)}, f32[4,432,128]{2,1,0:T(8,128)S(1)}, bf16[256,128]{1,0:T(8,128)(2,1)S(1)}, bf16[128,256]{1,0:T(8,128)(2,1)S(1)}, f32[8,128]{1,0:T(8,128)S(1)}) custom-call(f32[4,720,128]{2,1,0:T(8,128)S(1)} %get-tuple-element.34.state_ref, bf16[4,720,128]{2,1,0:T(8,128)(2,1)S(1)} %get-tuple-element.39.prev_ref, ...), custom_call_target="tpu_custom_call" | custom-call | flops 3397386240 | bytes 5137408 | tf_op jit(solution)/shard_map/own/pallas_call | solution.py:799
  12.7 0.0 collective-permute-done.2.packed_ref
  12.7 1.2 %far.1 = (bf16[4,432,128]{2,1,0:T(8,128)(2,1)S(1)}, f32[4,432,128]{2,1,0:T(8,128)S(1)}, bf16[4,432,128]{2,1,0:T(8,128)(2,1)S(1)}, bf16[4,432,128]{2,1,0:T(8,128)(2,1)S(1)}, bf16[576,128]{1,0:T(8,128)(2,1)S(1)}) custom-call(f32[4,720,128]{2,1,0:T(8,128)S(1)} %get-tuple-element.34.state_ref, bf16[4,720,128]{2,1,0:T(8,128)(2,1)S(1)} %get-tuple-element.39.prev_ref, ...), custom_call_target="tpu_custom_call" | custom-call | flops 5662310400 | bytes 8422400 | tf_op jit(solution)/shard_map/far/pallas_call | solution.py:799
  13.9 3.2 %collective-permute-start.5 = (bf16[4,432,128]{2,1,0:T(8,128)(2,1)S(1)}, bf16[4,432,128]{2,1,0:T(8,128)(2,1)S(1)}, u32[]{:S(2)}, u32[]{:S(2)}) collective-permute-start(bf16[4,432,128]{2,1,0:T(8,128)(2,1)S(1)} %get-tuple-element.62), channel_id=1, source_target_pairs={{0,127},{1,2},{2,1},{3,4},{4,3},{5,6},{6,5},{7,8},{8,7},{9,10},{10... | collective-permute-start | bytes 1327112 | tf_op jit(solution)/shard_map/ppermute | solution.py:774
  17.1 0.0 collective-permute-start.6
  17.1 2.1 %physics.1 = (bf16[4,288,128]{2,1,0:T(8,128)(2,1)S(1)}, f32[4,288,128]{2,1,0:T(8,128)S(1)}, bf16[3,288,128]{2,1,0:T(8,128)(2,1)S(1)}, bf16[3,288,128]{2,1,0:T(8,128)(2,1)S(1)}) custom-call(f32[4,720,128]{2,1,0:T(8,128)S(1)} %get-tuple-element.34.state_ref, bf16[4,720,128]{2,1,0:T(8,128)(2,1)S(1)} %get-tuple-element.39.prev_ref, ...), custom_call_target="tpu_custom_call" | custom-call | flops 3774873600 | bytes 5702656 | tf_op jit(solution)/shard_map/physics/pallas_call | solution.py:799
  19.2 4.2 %collective-permute-start.3 = (bf16[3,288,128]{2,1,0:T(8,128)(2,1)S(1)}, bf16[3,288,128]{2,1,0:T(8,128)(2,1)S(1)}, u32[]{:S(2)}, u32[]{:S(2)}) collective-permute-start(bf16[3,288,128]{2,1,0:T(8,128)(2,1)S(1)} %get-tuple-element.57), channel_id=1, source_target_pairs={{0,127},{1,2},{2,1},{3,4},{4,3},{5,6},{6,5},{7,8},{8,7},{9,10},{10... | collective-permute-start | bytes 663560 | tf_op jit(solution)/shard_map/ppermute | solution.py:774
  23.4 0.0 collective-permute-done.off_ref
  23.4 0.0 collective-permute-start.4
  23.4 0.0 collective-permute-done.1.on_ref
  23.4 2.8 %near.1 = (f32[4,720,128]{2,1,0:T(8,128)S(1)}, f32[4,720,128]{2,1,0:T(8,128)S(1)}, f32[4,720,128]{2,1,0:T(8,128)S(1)}, f32[4,720,128]{2,1,0:T(8,128)S(1)}, f32[4...) custom-call(f32[4,720,128]{2,1,0:T(8,128)S(1)} %get-tuple-element.34, ...), custom_call_target="tpu_custom_call" | custom-call | flops 6039797760 | bytes 11673600 | tf_op jit(solution)/shard_map/near/pallas_call | solution.py:799
  26.2 1.0 %collective-permute-done.5.off_ref = bf16[4,432,128]{2,1,0:T(8,128)(2,1)S(1)} collective-permute-done((bf16[4,432,128]{2,1,0:T(8,128)(2,1)S(1)}, bf16[4,432,128]{2,1,0:T(8,128)(2,1)S(1)}, u32[]{:S(2)}, u32[]{:S(2)}) %collective-permute-start.5) | collective-permute-done | bytes 442400 | tf_op jit(solution)/shard_map/ppermute | solution.py:774
  27.2 0.0 collective-permute-done.6.on_ref
  27.2 2.5 %advance.2 = (f32[4,432,128]{2,1,0:T(8,128)S(1)}, bf16[4,720,128]{2,1,0:T(8,128)(2,1)}) custom-call(f32[4,720,128]{2,1,0:T(8,128)S(1)} %get-tuple-element.52.own_ref, f32[4,720,128]{2,1,0:T(8,128)S(1)} %get-tuple-element.53.near_ref, f32[4,720,128]{2,1,0:T(8,128)S(1)} %get-tuple-element.54.near_add_ref, f32[4,720,128]{2,1,0:T(8,128)S(1)} %get-tuple-element.55.own_force_ref, ...), custom_call_target="tpu_custom_call" | custom-call | flops 5662310400 | bytes 20152320 | tf_op jit(solution)/shard_map/advance/pallas_call | solution.py:799
  29.7 0.3 %collective-permute-done.3.off_ref = bf16[3,288,128]{2,1,0:T(8,128)(2,1)S(1)} collective-permute-done((bf16[3,288,128]{2,1,0:T(8,128)(2,1)S(1)}, bf16[3,288,128]{2,1,0:T(8,128)(2,1)S(1)}, u32[]{:S(2)}, u32[]{:S(2)}) %collective-permute-start.3) | collective-permute-done | bytes 221216 | tf_op jit(solution)/shard_map/ppermute | solution.py:774
  30.1 0.0 collective-permute-done.4.on_ref
  30.1 2.4 %advance.3 = f32[4,720,128]{2,1,0:T(8,128)} custom-call(f32[4,720,128]{2,1,0:T(8,128)S(1)} %get-tuple-element.52.own_ref, f32[4,720,128]{2,1,0:T(8,128)S(1)} %get-tuple-element.53.near_ref, f32[4,720,128]{2,1,0:T(8,128)S(1)} %get-tuple-element.54.near_add_ref, f32[4,720,128]{2,1,0:T(8,128)S(1)} %get-tuple-element.55.own_force_ref, ...), custom_call_target="tpu_custom_call" | custom-call | flops 3774873600 | bytes 20152320 | tf_op jit(solution)/shard_map/advance/pallas_call | solution.py:799
Async XLA Ops:
  0.6 10.5 %copy-start.1 = (bf16[256,256]{1,0:T(8,128)(2,1)S(1)}, bf16[256,256]{1,0:T(8,128)(2,1)}, u32[]{:S(2)}) copy-start(bf16[256,256]{1,0:T(8,128)(2,1)} %constant.2.clone.slope_ref) | copy-start | bytes 393220
  0.6 10.5 %copy-start = (s32[128]{0:T(128)S(1)}, s32[128]{0:T(128)}, u32[]{:S(2)}) copy-start(s32[128]{0:T(128)} %param.11) | copy-start | bytes 1540
  2.6 10.1 %collective-permute-start.2 = (bf16[368,128]{1,0:T(8,128)(2,1)S(1)}, bf16[368,128]{1,0:T(8,128)(2,1)S(1)}, u32[]{:S(2)}, u32[]{:S(2)}) collective-permute-start(bf16[368,128]{1,0:T(8,128)(2,1)S(1)} %get-tuple-element.40), channel_id=1, source_target_pairs={{0,64},{1,65},{2,66},{3,67},{4,68},{5,69},{6,70},{7,71},{8,72},{9,... | collective-permute-start | bytes 282632 | tf_op jit(solution)/shard_map/ppermute | solution.py:836
  6.6 16.7 %collective-permute-start = (bf16[3,784,128]{2,1,0:T(8,128)(2,1)S(1)}, bf16[3,784,128]{2,1,0:T(8,128)(2,1)S(1)}, u32[]{:S(2)}, u32[]{:S(2)}) collective-permute-start(bf16[3,784,128]{2,1,0:T(8,128)(2,1)S(1)} %get-tuple-element.37), channel_id=1, source_target_pairs={{0,127},{1,2},{2,1},{3,4},{4,3},{5,6},{6,5},{7,8},{8,7},{9,10},{10... | collective-permute-start | bytes 1806344 | tf_op jit(solution)/shard_map/ppermute | solution.py:774
  11.2 12.2 %collective-permute-start.1 = (bf16[3,784,128]{2,1,0:T(8,128)(2,1)S(1)}, bf16[3,784,128]{2,1,0:T(8,128)(2,1)S(1)}, u32[]{:S(2)}, u32[]{:S(2)}) collective-permute-start(bf16[3,784,128]{2,1,0:T(8,128)(2,1)S(1)} %get-tuple-element.38), channel_id=1, source_target_pairs={{0,1},{1,0},{2,3},{3,2},{4,5},{5,4},{6,7},{7,6},{8,9},{9,8},{10,11... | collective-permute-start | bytes 1806344 | tf_op jit(solution)/shard_map/ppermute | solution.py:773
  13.9 13.2 %collective-permute-start.5 = (bf16[4,432,128]{2,1,0:T(8,128)(2,1)S(1)}, bf16[4,432,128]{2,1,0:T(8,128)(2,1)S(1)}, u32[]{:S(2)}, u32[]{:S(2)}) collective-permute-start(bf16[4,432,128]{2,1,0:T(8,128)(2,1)S(1)} %get-tuple-element.62), channel_id=1, source_target_pairs={{0,127},{1,2},{2,1},{3,4},{4,3},{5,6},{6,5},{7,8},{8,7},{9,10},{10... | collective-permute-start | bytes 1327112 | tf_op jit(solution)/shard_map/ppermute | solution.py:774
  17.1 10.1 %collective-permute-start.6 = (bf16[4,432,128]{2,1,0:T(8,128)(2,1)S(1)}, bf16[4,432,128]{2,1,0:T(8,128)(2,1)S(1)}, u32[]{:S(2)}, u32[]{:S(2)}) collective-permute-start(bf16[4,432,128]{2,1,0:T(8,128)(2,1)S(1)} %get-tuple-element.63), channel_id=1, source_target_pairs={{0,1},{1,0},{2,3},{3,2},{4,5},{5,4},{6,7},{7,6},{8,9},{9,8},{10,11... | collective-permute-start | bytes 1327112 | tf_op jit(solution)/shard_map/ppermute | solution.py:773
  19.2 10.9 %collective-permute-start.3 = (bf16[3,288,128]{2,1,0:T(8,128)(2,1)S(1)}, bf16[3,288,128]{2,1,0:T(8,128)(2,1)S(1)}, u32[]{:S(2)}, u32[]{:S(2)}) collective-permute-start(bf16[3,288,128]{2,1,0:T(8,128)(2,1)S(1)} %get-tuple-element.57), channel_id=1, source_target_pairs={{0,127},{1,2},{2,1},{3,4},{4,3},{5,6},{6,5},{7,8},{8,7},{9,10},{10... | collective-permute-start | bytes 663560 | tf_op jit(solution)/shard_map/ppermute | solution.py:774
  23.4 6.7 %collective-permute-start.4 = (bf16[3,288,128]{2,1,0:T(8,128)(2,1)S(1)}, bf16[3,288,128]{2,1,0:T(8,128)(2,1)S(1)}, u32[]{:S(2)}, u32[]{:S(2)}) collective-permute-start(bf16[3,288,128]{2,1,0:T(8,128)(2,1)S(1)} %get-tuple-element.58), channel_id=1, source_target_pairs={{0,1},{1,0},{2,3},{3,2},{4,5},{5,4},{6,7},{7,6},{8,9},{9,8},{10,11... | collective-permute-start | bytes 663560 | tf_op jit(solution)/shard_map/ppermute | solution.py:773

commit v10 on v9

--- a/solution.py
+++ b/solution.py
@@ -585,7 +585,7 @@
     prev_ref,
     *rest,
 ):
-    parts, outs = rest[:-8], rest[-8:]
+    parts, outs = rest[:-10], rest[-9:-1]
     own_ref, near_ref, near_add_ref, own_force_ref, near_force_ref, sum_ref, edge_sum_ref, blow_ref = outs
     lev = wind_ref.shape[1]
     slots, _ = point_sets()
@@ -766,12 +766,13 @@
         copy.wait()
 
 
-def exchanged(off, on):
+def across(value):
     count = lax.axis_size(AXES)
-    across = [(i, (i + 1) % count if i % 2 else (i - 1) % count) for i in range(count)]
-    inside = [(i, i ^ 1) for i in range(count)]
-    on = lax.ppermute(on, AXES, inside)
-    return lax.ppermute(off, AXES, across), on
+    return lax.ppermute(value, AXES, [(i, (i + 1) % count if i % 2 else (i - 1) % count) for i in range(count)])
+
+
+def inside(value):
+    return lax.ppermute(value, AXES, [(i, i ^ 1) for i in range(lax.axis_size(AXES))])
 
 
 def per_device(state, prev_tendency, wind, edge_links, swap_slot, inverse):
@@ -834,7 +835,7 @@
         ],
     )
     far_packed = lax.ppermute(packed, AXES, [(i, i ^ (devices // 2)) for i in range(devices)])
-    off, on = exchanged(to_off, to_on)
+    off, on = across(to_off), inside(to_on)
     halves = []
     first = 0
     shared = (wind, targets, slope, slot, matrices)
@@ -861,12 +862,14 @@
             functools.partial(body, first, count), ins, outs, name, 5 * count
         )
         far_matrices = more[0] if more else far_matrices
-        halves.append((first, count, tend, ahead, exchanged(to_off, to_on)))
+        halves.append([first, count, tend, ahead, across(to_off), to_on if first else inside(to_on)])
         first += count
-    parts = sum(((tend, ahead) for _, _, tend, ahead, _ in halves), ())
-    own, near, near_add, own_force, near_force, sums, edge_sums, blow = call(
+    parts = sum(((tend, ahead) for _, _, tend, ahead, _, _ in halves), ())
+    passed = halves[-1][-1]
+    ins = (state, wind, targets, slope, off, on, prev) + parts + (passed,)
+    own, near, near_add, own_force, near_force, sums, edge_sums, blow, passed = call(
         near_kernel,
-        (state, wind, targets, slope, off, on, prev) + parts,
+        ins,
         (
             like(4, f32),
             like(4, f32),
@@ -876,14 +879,17 @@
             table(bf16, 2 * LANES, 2 * LANES),
             table(bf16, 4, 2 * LANES, 2 * LANES),
             table(f32, 4, 2, lev, LANES),
+            like(3, bf16, passed.shape[1]),
         ),
         "near",
         16,
+        input_output_aliases={len(ins) - 1: 8},
     )
-    tends = tuple(tend for _, _, tend, _, _ in halves)
+    halves[-1][-1] = inside(passed)
+    tends = tuple(tend for _, _, tend, _, _, _ in halves)
     out_spec = jax.ShapeDtypeStruct((PARTS, rows, LANES), f32)
     tend_spec = jax.ShapeDtypeStruct((PARTS, rows, LANES), bf16)
-    for part, (first, count, tend, _, (off, on)) in enumerate(halves):
+    for part, (first, count, tend, _, off, on) in enumerate(halves):
         ins = (own, near, near_add, own_force, near_force, off, on, slope, sums, edge_sums, blow)
         size = count * CHUNK
         if part == 0:

time: 32.9 us -> 33.2 us (level)
  no operation moved by 1% of the time
where the time goes in v10:
time: 33.2 us; the launch traced here: 32.6 us
  starting transfers between devices  16.2 us (49%)
  Pallas kernels  14.5 us (44%)
  waiting for transfers between devices  1.05 us (3%)
  between operations  0.87 us (3%)
    pallas_call x7, Pallas kernels, call(): pl.pallas_call(body, out_shape=outs, compiler_params=params, cost_estimat...  14.5 us
    ppermute x3, starting transfers between devices, across(): lax.ppermute(value, AXES, [(i, (i + 1) % count if i % 2 else (i - 1) % co...  11.9 us
    ppermute x1, starting transfers between devices, per_device(): lax.ppermute(packed, AXES, [(i, i ^ devices // 2) for i in range(devices)])  4.04 us
    ppermute x3, waiting for transfers between devices, across(): lax.ppermute(value, AXES, [(i, (i + 1) % count if i % 2 else (i - 1) % co...  1.04 us
  transfers between devices with their start and end apart: 7, of which 2 were waited for; matrix products, arithmetic and copies ran while one was open for 0% of the time, Pallas kernels for 31%

profile of v10, /device:TPU:0, one launch (start us, length us, event | category | flops | bytes accessed | tf_op | source)
XLA Modules:
  0.0 32.6 jit_solution(6008061488937738363)
XLA Ops:
  0.6 0.0 copy-start.1
  0.6 0.0 copy-start
  0.7 1.9 %pack.1 = (bf16[576,128]{1,0:T(8,128)(2,1)S(1)}, bf16[368,128]{1,0:T(8,128)(2,1)S(1)}, bf16[3,784,128]{2,1,0:T(8,128)(2,1)S(1)}, bf16[3,784,128]{2,1,0:T(8,128)(...) custom-call(f32[8,72,72]{2,1,0:T(8,128)} %inverse_hbm.1, ...), custom_call_target="tpu_custom_call" | custom-call | flops 754974720 | bytes 4903424 | tf_op jit(solution)/shard_map/pack/pallas_call | solution.py:800
  2.6 4.0 %collective-permute-start.2 = (bf16[368,128]{1,0:T(8,128)(2,1)S(1)}, bf16[368,128]{1,0:T(8,128)(2,1)S(1)}, u32[]{:S(2)}, u32[]{:S(2)}) collective-permute-start(bf16[368,128]{1,0:T(8,128)(2,1)S(1)} %get-tuple-element.41), channel_id=1, source_target_pairs={{0,64},{1,65},{2,66},{3,67},{4,68},{5,69},{6,70},{7,71},{8,72},{9,... | collective-permute-start | bytes 282632 | tf_op jit(solution)/shard_map/ppermute | solution.py:837
  6.6 4.5 %collective-permute-start = (bf16[3,784,128]{2,1,0:T(8,128)(2,1)S(1)}, bf16[3,784,128]{2,1,0:T(8,128)(2,1)S(1)}, u32[]{:S(2)}, u32[]{:S(2)}) collective-permute-start(bf16[3,784,128]{2,1,0:T(8,128)(2,1)S(1)} %get-tuple-element.38), channel_id=1, source_target_pairs={{0,127},{1,2},{2,1},{3,4},{4,3},{5,6},{6,5},{7,8},{8,7},{9,10},{10... | collective-permute-start | bytes 1806344 | tf_op jit(solution)/shard_map/ppermute | solution.py:771
  11.2 0.0 collective-permute-start.1
  11.2 0.0 copy-done.1
  11.2 0.0 copy-done
  11.2 1.5 %own.1 = (f32[4,432,128]{2,1,0:T(8,128)S(1)}, f32[4,432,128]{2,1,0:T(8,128)S(1)}, bf16[256,128]{1,0:T(8,128)(2,1)S(1)}, bf16[128,256]{1,0:T(8,128)(2,1)S(1)}, f32[8,128]{1,0:T(8,128)S(1)}) custom-call(f32[4,720,128]{2,1,0:T(8,128)S(1)} %get-tuple-element.35.state_ref, bf16[4,720,128]{2,1,0:T(8,128)(2,1)S(1)} %get-tuple-element.40.prev_ref, ...), custom_call_target="tpu_custom_call" | custom-call | flops 3397386240 | bytes 5137408 | tf_op jit(solution)/shard_map/own/pallas_call | solution.py:800
  12.7 0.0 collective-permute-done.2.packed_ref
  12.7 1.2 %far.1 = (bf16[4,432,128]{2,1,0:T(8,128)(2,1)S(1)}, f32[4,432,128]{2,1,0:T(8,128)S(1)}, bf16[4,432,128]{2,1,0:T(8,128)(2,1)S(1)}, bf16[4,432,128]{2,1,0:T(8,128)(2,1)S(1)}, bf16[576,128]{1,0:T(8,128)(2,1)S(1)}) custom-call(f32[4,720,128]{2,1,0:T(8,128)S(1)} %get-tuple-element.35.state_ref, bf16[4,720,128]{2,1,0:T(8,128)(2,1)S(1)} %get-tuple-element.40.prev_ref, ...), custom_call_target="tpu_custom_call" | custom-call | flops 5662310400 | bytes 8422400 | tf_op jit(solution)/shard_map/far/pallas_call | solution.py:800
  14.0 3.2 %collective-permute-start.5 = (bf16[4,432,128]{2,1,0:T(8,128)(2,1)S(1)}, bf16[4,432,128]{2,1,0:T(8,128)(2,1)S(1)}, u32[]{:S(2)}, u32[]{:S(2)}) collective-permute-start(bf16[4,432,128]{2,1,0:T(8,128)(2,1)S(1)} %get-tuple-element.64), channel_id=1, source_target_pairs={{0,127},{1,2},{2,1},{3,4},{4,3},{5,6},{6,5},{7,8},{8,7},{9,10},{10... | collective-permute-start | bytes 1327112 | tf_op jit(solution)/shard_map/ppermute | solution.py:771
  17.1 0.0 collective-permute-start.6
  17.1 2.1 %physics.1 = (bf16[4,288,128]{2,1,0:T(8,128)(2,1)S(1)}, f32[4,288,128]{2,1,0:T(8,128)S(1)}, bf16[3,288,128]{2,1,0:T(8,128)(2,1)S(1)}, bf16[3,288,128]{2,1,0:T(8,128)(2,1)S(1)}) custom-call(f32[4,720,128]{2,1,0:T(8,128)S(1)} %get-tuple-element.35.state_ref, bf16[4,720,128]{2,1,0:T(8,128)(2,1)S(1)} %get-tuple-element.40.prev_ref, ...), custom_call_target="tpu_custom_call" | custom-call | flops 3774873600 | bytes 5702656 | tf_op jit(solution)/shard_map/physics/pallas_call | solution.py:800
  19.2 4.2 %collective-permute-start.3 = (bf16[3,288,128]{2,1,0:T(8,128)(2,1)S(1)}, bf16[3,288,128]{2,1,0:T(8,128)(2,1)S(1)}, u32[]{:S(2)}, u32[]{:S(2)}) collective-permute-start(bf16[3,288,128]{2,1,0:T(8,128)(2,1)S(1)} %get-tuple-element.59), channel_id=1, source_target_pairs={{0,127},{1,2},{2,1},{3,4},{4,3},{5,6},{6,5},{7,8},{8,7},{9,10},{10... | collective-permute-start | bytes 663560 | tf_op jit(solution)/shard_map/ppermute | solution.py:771
  23.4 0.0 collective-permute-done.off_ref
  23.4 0.0 collective-permute-done.1.on_ref
  23.4 2.8 %near.1 = (f32[4,720,128]{2,1,0:T(8,128)S(1)}, f32[4,720,128]{2,1,0:T(8,128)S(1)}, f32[4,720,128]{2,1,0:T(8,128)S(1)}, f32[4,720,128]{2,1,0:T(8,128)S(1)}, f32[4...) custom-call(f32[4,720,128]{2,1,0:T(8,128)S(1)} %get-tuple-element.35, ...), custom_call_target="tpu_custom_call", output_to_operand_aliasing={{8}: (11, {})} | custom-call | flops 6039797760 | bytes 12115968 | tf_op jit(solution)/shard_map/near/pallas_call | solution.py:800
  26.2 0.3 collective-permute-start.4
  26.5 0.7 %collective-permute-done.5.off_ref = bf16[4,432,128]{2,1,0:T(8,128)(2,1)S(1)} collective-permute-done((bf16[4,432,128]{2,1,0:T(8,128)(2,1)S(1)}, bf16[4,432,128]{2,1,0:T(8,128)(2,1)S(1)}, u32[]{:S(2)}, u32[]{:S(2)}) %collective-permute-start.5) | collective-permute-done | bytes 442400 | tf_op jit(solution)/shard_map/ppermute | solution.py:771
  27.2 0.0 collective-permute-done.6.on_ref
  27.2 2.5 %advance.2 = (f32[4,432,128]{2,1,0:T(8,128)S(1)}, bf16[4,720,128]{2,1,0:T(8,128)(2,1)}) custom-call(f32[4,720,128]{2,1,0:T(8,128)S(1)} %get-tuple-element.54.own_ref, f32[4,720,128]{2,1,0:T(8,128)S(1)} %get-tuple-element.55.near_ref, f32[4,720,128]{2,1,0:T(8,128)S(1)} %get-tuple-element.56.near_add_ref, f32[4,720,128]{2,1,0:T(8,128)S(1)} %get-tuple-element.57.own_force_ref, ...), custom_call_target="tpu_custom_call" | custom-call | flops 5662310400 | bytes 20152320 | tf_op jit(solution)/shard_map/advance/pallas_call | solution.py:800
  29.7 0.3 %collective-permute-done.3.off_ref = bf16[3,288,128]{2,1,0:T(8,128)(2,1)S(1)} collective-permute-done((bf16[3,288,128]{2,1,0:T(8,128)(2,1)S(1)}, bf16[3,288,128]{2,1,0:T(8,128)(2,1)S(1)}, u32[]{:S(2)}, u32[]{:S(2)}) %collective-permute-start.3) | collective-permute-done | bytes 221216 | tf_op jit(solution)/shard_map/ppermute | solution.py:771
  30.1 0.0 collective-permute-done.4.on_ref
  30.1 2.4 %advance.3 = f32[4,720,128]{2,1,0:T(8,128)} custom-call(f32[4,720,128]{2,1,0:T(8,128)S(1)} %get-tuple-element.54.own_ref, f32[4,720,128]{2,1,0:T(8,128)S(1)} %get-tuple-element.55.near_ref, f32[4,720,128]{2,1,0:T(8,128)S(1)} %get-tuple-element.56.near_add_ref, f32[4,720,128]{2,1,0:T(8,128)S(1)} %get-tuple-element.57.own_force_ref, ...), custom_call_target="tpu_custom_call" | custom-call | flops 3774873600 | bytes 20152320 | tf_op jit(solution)/shard_map/advance/pallas_call | solution.py:800
Async XLA Ops:
  0.6 10.5 %copy-start.1 = (bf16[256,256]{1,0:T(8,128)(2,1)S(1)}, bf16[256,256]{1,0:T(8,128)(2,1)}, u32[]{:S(2)}) copy-start(bf16[256,256]{1,0:T(8,128)(2,1)} %constant.2.clone.slope_ref) | copy-start | bytes 393220
  0.6 10.5 %copy-start = (s32[128]{0:T(128)S(1)}, s32[128]{0:T(128)}, u32[]{:S(2)}) copy-start(s32[128]{0:T(128)} %param.11) | copy-start | bytes 1540
  2.6 10.1 %collective-permute-start.2 = (bf16[368,128]{1,0:T(8,128)(2,1)S(1)}, bf16[368,128]{1,0:T(8,128)(2,1)S(1)}, u32[]{:S(2)}, u32[]{:S(2)}) collective-permute-start(bf16[368,128]{1,0:T(8,128)(2,1)S(1)} %get-tuple-element.41), channel_id=1, source_target_pairs={{0,64},{1,65},{2,66},{3,67},{4,68},{5,69},{6,70},{7,71},{8,72},{9,... | collective-permute-start | bytes 282632 | tf_op jit(solution)/shard_map/ppermute | solution.py:837
  6.6 16.7 %collective-permute-start = (bf16[3,784,128]{2,1,0:T(8,128)(2,1)S(1)}, bf16[3,784,128]{2,1,0:T(8,128)(2,1)S(1)}, u32[]{:S(2)}, u32[]{:S(2)}) collective-permute-start(bf16[3,784,128]{2,1,0:T(8,128)(2,1)S(1)} %get-tuple-element.38), channel_id=1, source_target_pairs={{0,127},{1,2},{2,1},{3,4},{4,3},{5,6},{6,5},{7,8},{8,7},{9,10},{10... | collective-permute-start | bytes 1806344 | tf_op jit(solution)/shard_map/ppermute | solution.py:771
  11.2 12.2 %collective-permute-start.1 = (bf16[3,784,128]{2,1,0:T(8,128)(2,1)S(1)}, bf16[3,784,128]{2,1,0:T(8,128)(2,1)S(1)}, u32[]{:S(2)}, u32[]{:S(2)}) collective-permute-start(bf16[3,784,128]{2,1,0:T(8,128)(2,1)S(1)} %get-tuple-element.39), channel_id=1, source_target_pairs={{0,1},{1,0},{2,3},{3,2},{4,5},{5,4},{6,7},{7,6},{8,9},{9,8},{10,11... | collective-permute-start | bytes 1806344 | tf_op jit(solution)/shard_map/ppermute | solution.py:775
  14.0 13.2 %collective-permute-start.5 = (bf16[4,432,128]{2,1,0:T(8,128)(2,1)S(1)}, bf16[4,432,128]{2,1,0:T(8,128)(2,1)S(1)}, u32[]{:S(2)}, u32[]{:S(2)}) collective-permute-start(bf16[4,432,128]{2,1,0:T(8,128)(2,1)S(1)} %get-tuple-element.64), channel_id=1, source_target_pairs={{0,127},{1,2},{2,1},{3,4},{4,3},{5,6},{6,5},{7,8},{8,7},{9,10},{10... | collective-permute-start | bytes 1327112 | tf_op jit(solution)/shard_map/ppermute | solution.py:771
  17.1 10.1 %collective-permute-start.6 = (bf16[4,432,128]{2,1,0:T(8,128)(2,1)S(1)}, bf16[4,432,128]{2,1,0:T(8,128)(2,1)S(1)}, u32[]{:S(2)}, u32[]{:S(2)}) collective-permute-start(bf16[4,432,128]{2,1,0:T(8,128)(2,1)S(1)} %get-tuple-element.65), channel_id=1, source_target_pairs={{0,1},{1,0},{2,3},{3,2},{4,5},{5,4},{6,7},{7,6},{8,9},{9,8},{10,11... | collective-permute-start | bytes 1327112 | tf_op jit(solution)/shard_map/ppermute | solution.py:775
  19.2 10.9 %collective-permute-start.3 = (bf16[3,288,128]{2,1,0:T(8,128)(2,1)S(1)}, bf16[3,288,128]{2,1,0:T(8,128)(2,1)S(1)}, u32[]{:S(2)}, u32[]{:S(2)}) collective-permute-start(bf16[3,288,128]{2,1,0:T(8,128)(2,1)S(1)} %get-tuple-element.59), channel_id=1, source_target_pairs={{0,127},{1,2},{2,1},{3,4},{4,3},{5,6},{6,5},{7,8},{8,7},{9,10},{10... | collective-permute-start | bytes 663560 | tf_op jit(solution)/shard_map/ppermute | solution.py:771
  26.2 3.9 %collective-permute-start.4 = (bf16[3,288,128]{2,1,0:T(8,128)(2,1)S(1)}, bf16[3,288,128]{2,1,0:T(8,128)(2,1)S(1)}, u32[]{:S(2)}, u32[]{:S(2)}) collective-permute-start(bf16[3,288,128]{2,1,0:T(8,128)(2,1)S(1)} %get-tuple-element.60), channel_id=1, source_target_pairs={{0,1},{1,0},{2,3},{3,2},{4,5},{5,4},{6,7},{7,6},{8,9},{9,8},{10,11... | collective-permute-start | bytes 663560 | tf_op jit(solution)/shard_map/ppermute | solution.py:775

commit v11 on v9

--- a/solution.py
+++ b/solution.py
@@ -406,8 +406,9 @@
     def motion(self, state):
         return moved(state, self.slope, *self.blow)
 
-    def start(self, state, prev):
+    def start(self, state, prev, move_ref, at):
         motion = self.motion(state)
+        move_ref[:, at] = motion.reshape(PARTS, CHUNK, LANES)
         yield
         total = jnp.dot(motion, self.sums, preferred_element_type=jnp.float32)
         return state + total + time_step * hermite(0)[0] * prev
@@ -483,7 +484,7 @@
 
 
 def own_kernel(
-    first, count, state_ref, prev_ref, wind_ref, target_ref, slope_ref, slot_ref, own_ref, part_ref, start_ref, *tables
+    first, count, state_ref, prev_ref, wind_ref, target_ref, slope_ref, slot_ref, own_ref, part_ref, start_ref, move_ref, *tables
 ):
     physics = Physics(slot_ref)
     physics.take_own(own_ref)
@@ -492,7 +493,7 @@
     def stages(at, here_at, j):
         parts, start, *_ = yield from mixed(
             physics.own_products([state_ref[k, at] for k in range(PARTS)]),
-            physics.start(flat(state_ref[:, at]), flat(prev_ref[:, at])),
+            physics.start(flat(state_ref[:, at]), flat(prev_ref[:, at]), move_ref, here_at),
             *([leaving_tables(slot_ref, *tables)] if j == 0 else []),
         )
         start_ref[:, here_at] = start.reshape(PARTS, CHUNK, LANES)
@@ -553,6 +554,7 @@
     ahead_ref,
     off_ref,
     on_ref,
+    move_ref,
 ):
     physics = Physics(slot_ref)
     physics.take_own(own_ref)
@@ -565,7 +567,7 @@
         far, own, start = yield from mixed(
             physics.far_products(pairs),
             physics.own_products(pairs),
-            physics.start(flat(state_ref[:, at]), flat(prev_ref[:, at])),
+            physics.start(flat(state_ref[:, at]), flat(prev_ref[:, at]), move_ref, here_at),
         )
         start = [start[k * CHUNK : (k + 1) * CHUNK] for k in range(PARTS)]
         tends = physics.merged(own, far)
@@ -639,10 +641,10 @@
     own_blow = (blow_ref[0, 0], blow_ref[0, 1])
     near_blow = (blow_ref[1, 0], blow_ref[1, 1])
 
-    def stages(at, here_at, tend_ref, ahead_ref):
+    def stages(at, here_at, tend_ref, ahead_ref, move_ref):
         off, on = off_ref[:, at].astype(jnp.float32), on_ref[:, at].astype(jnp.float32)
         near = whole_halves(off[:2], on[:2], chosen)
-        own_move = moved(flat(state_ref[:, at]), slope, *own_blow)
+        own_move = move_ref[:, here_at].reshape(-1, LANES)
         near_move = moved(near, slope, *near_blow)
         yield
         total = jnp.concatenate([near_move, own_move], axis=1)
@@ -666,8 +668,8 @@
         near_add_ref[:, at] = near_add.reshape(PARTS, CHUNK, LANES)
 
     places = []
-    for tend_ref, ahead_ref in zip(parts[::2], parts[1::2]):
-        places += [(here_at, tend_ref, ahead_ref) for here_at in chunks(tend_ref)]
+    for refs in zip(parts[::3], parts[1::3], parts[2::3]):
+        places += [(here_at, *refs) for here_at in chunks(refs[0])]
     in_turns(0, len(places), lambda at, _, j: stages(at, *places[j]))
 
 
@@ -843,10 +845,10 @@
         sent = like(3 if first else 4, bf16, size)
         outs = (like(4, bf16, size), like(4, f32, size), sent, sent)
         if first == 0:
-            part, start, *tables = call(
+            part, start, move, *tables = call(
                 functools.partial(own_kernel, first, count),
                 (state, prev) + shared,
-                (like(4, f32, size), like(4, f32, size))
+                (like(4, f32, size), like(4, f32, size), like(4, bf16, size))
                 + (table(bf16, 2 * LANES, LANES), table(bf16, LANES, 2 * LANES), table(f32, 8, LANES)),
                 "own",
                 3 * count,
@@ -857,13 +859,17 @@
         else:
             ins = (state, prev) + shared + (far_matrices, *tables)
             body, name = physics_kernel, "physics"
+            outs += (like(4, bf16, size),)
         tend, ahead, to_off, to_on, *more = call(
             functools.partial(body, first, count), ins, outs, name, 5 * count
         )
-        far_matrices = more[0] if more else far_matrices
-        halves.append((first, count, tend, ahead, exchanged(to_off, to_on)))
+        if first:
+            move = more[0]
+        else:
+            far_matrices = more[0]
+        halves.append((first, count, tend, (tend, ahead, move), exchanged(to_off, to_on)))
         first += count
-    parts = sum(((tend, ahead) for _, _, tend, ahead, _ in halves), ())
+    parts = sum((part for _, _, _, part, _ in halves), ())
     own, near, near_add, own_force, near_force, sums, edge_sums, blow = call(
         near_kernel,
         (state, wind, targets, slope, off, on, prev) + parts,

time: 32.9 us -> 32.8 us (level)
  Pallas kernels: 14.5 us -> 14 us
  waiting for transfers between devices: 1.33 us -> 1.81 us
    pallas_call x7, Pallas kernels: 14.5 us -> 14 us  [call(): pl.pallas_call(body, out_shape=outs, compiler_params=params, cost_estimat...]
    ppermute x3, waiting for transfers between devices: 1.32 us -> 1.8 us  [exchanged(): return (lax.ppermute(off, AXES, across), on)]
  transfers between devices with their start and end apart: 7 -> 7, of which waited for: 2 -> 2; matrix products, arithmetic and copies ran while one was open for 0% -> 0% of each run, Pallas kernels for 31% -> 30%
where the time goes in v11:
time: 32.8 us; the launch traced here: 32.6 us
  starting transfers between devices  15.9 us (48%)
  Pallas kernels  14 us (43%)
  waiting for transfers between devices  1.81 us (6%)
  between operations  0.87 us (3%)
    pallas_call x7, Pallas kernels, call(): pl.pallas_call(body, out_shape=outs, compiler_params=params, cost_estimat...  14 us
    ppermute x3, starting transfers between devices, exchanged(): return (lax.ppermute(off, AXES, across), on)  11.8 us
    ppermute x1, starting transfers between devices, per_device(): lax.ppermute(packed, AXES, [(i, i ^ devices // 2) for i in range(devices)])  4.04 us
    ppermute x3, waiting for transfers between devices, exchanged(): return (lax.ppermute(off, AXES, across), on)  1.8 us
  transfers between devices with their start and end apart: 7, of which 2 were waited for; matrix products, arithmetic and copies ran while one was open for 0% of the time, Pallas kernels for 30%

profile of v11, /device:TPU:0, one launch (start us, length us, event | category | flops | bytes accessed | tf_op | source)
XLA Modules:
  0.0 32.6 jit_solution(13719451827124603727)
XLA Ops:
  0.6 0.0 copy-start.1
  0.6 0.0 copy-start
  0.7 1.9 %pack.1 = (bf16[576,128]{1,0:T(8,128)(2,1)S(1)}, bf16[368,128]{1,0:T(8,128)(2,1)S(1)}, bf16[3,784,128]{2,1,0:T(8,128)(2,1)S(1)}, bf16[3,784,128]{2,1,0:T(8,128)(...) custom-call(f32[8,72,72]{2,1,0:T(8,128)} %inverse_hbm.1, ...), custom_call_target="tpu_custom_call" | custom-call | flops 754974720 | bytes 4903424 | tf_op jit(solution)/shard_map/pack/pallas_call | solution.py:801
  2.6 4.0 %collective-permute-start.2 = (bf16[368,128]{1,0:T(8,128)(2,1)S(1)}, bf16[368,128]{1,0:T(8,128)(2,1)S(1)}, u32[]{:S(2)}, u32[]{:S(2)}) collective-permute-start(bf16[368,128]{1,0:T(8,128)(2,1)S(1)} %get-tuple-element.42), channel_id=1, source_target_pairs={{0,64},{1,65},{2,66},{3,67},{4,68},{5,69},{6,70},{7,71},{8,72},{9,... | collective-permute-start | bytes 282632 | tf_op jit(solution)/shard_map/ppermute | solution.py:838
  6.6 4.5 %collective-permute-start = (bf16[3,784,128]{2,1,0:T(8,128)(2,1)S(1)}, bf16[3,784,128]{2,1,0:T(8,128)(2,1)S(1)}, u32[]{:S(2)}, u32[]{:S(2)}) collective-permute-start(bf16[3,784,128]{2,1,0:T(8,128)(2,1)S(1)} %get-tuple-element.39), channel_id=1, source_target_pairs={{0,127},{1,2},{2,1},{3,4},{4,3},{5,6},{6,5},{7,8},{8,7},{9,10},{10... | collective-permute-start | bytes 1806344 | tf_op jit(solution)/shard_map/ppermute | solution.py:776
  11.2 0.0 collective-permute-start.1
  11.2 0.0 copy-done.1
  11.2 0.0 copy-done
  11.2 1.5 %own.1 = (f32[4,432,128]{2,1,0:T(8,128)S(1)}, f32[4,432,128]{2,1,0:T(8,128)S(1)}, bf16[4,432,128]{2,1,0:T(8,128)(2,1)S(1)}, bf16[256,128]{1,0:T(8,128)(2,1)S(1)}...) custom-call(f32[4,720,128]{2,1,0:T(8,128)S(1)} %get-tuple-element.36.state_ref, ...), custom_call_target="tpu_custom_call" | custom-call | flops 3397386240 | bytes 5137408 | tf_op jit(solution)/shard_map/own/pallas_call | solution.py:801
  12.7 0.0 collective-permute-done.2.packed_ref
  12.7 1.2 %far.1 = (bf16[4,432,128]{2,1,0:T(8,128)(2,1)S(1)}, f32[4,432,128]{2,1,0:T(8,128)S(1)}, bf16[4,432,128]{2,1,0:T(8,128)(2,1)S(1)}, bf16[4,432,128]{2,1,0:T(8,128)(2,1)S(1)}, bf16[576,128]{1,0:T(8,128)(2,1)S(1)}) custom-call(f32[4,720,128]{2,1,0:T(8,128)S(1)} %get-tuple-element.36.state_ref, bf16[4,720,128]{2,1,0:T(8,128)(2,1)S(1)} %get-tuple-element.41.prev_ref, ...), custom_call_target="tpu_custom_call" | custom-call | flops 5662310400 | bytes 8422400 | tf_op jit(solution)/shard_map/far/pallas_call | solution.py:801
  13.9 3.2 %collective-permute-start.5 = (bf16[4,432,128]{2,1,0:T(8,128)(2,1)S(1)}, bf16[4,432,128]{2,1,0:T(8,128)(2,1)S(1)}, u32[]{:S(2)}, u32[]{:S(2)}) collective-permute-start(bf16[4,432,128]{2,1,0:T(8,128)(2,1)S(1)} %get-tuple-element.66), channel_id=1, source_target_pairs={{0,127},{1,2},{2,1},{3,4},{4,3},{5,6},{6,5},{7,8},{8,7},{9,10},{10... | collective-permute-start | bytes 1327112 | tf_op jit(solution)/shard_map/ppermute | solution.py:776
  17.1 0.0 collective-permute-start.6
  17.1 2.1 %physics.1 = (bf16[4,288,128]{2,1,0:T(8,128)(2,1)S(1)}, f32[4,288,128]{2,1,0:T(8,128)S(1)}, bf16[3,288,128]{2,1,0:T(8,128)(2,1)S(1)}, bf16[3,288,128]{2,1,0:T(8,128)(2,1)S(1)}, bf16[4,288,128]{2,1,0:T(8,128)(2,1)S(1)}) custom-call(f32[4,720,128]{2,1,0:T(8,128)S(1)} %get-tuple-element.36.state_ref, bf16[4,720,128]{2,1,0:T(8,128)(2,1)S(1)} %get-tuple-element.41.prev_ref, ...), custom_call_target="tpu_custom_call" | custom-call | flops 3774873600 | bytes 5702656 | tf_op jit(solution)/shard_map/physics/pallas_call | solution.py:801
  19.2 4.1 %collective-permute-start.3 = (bf16[3,288,128]{2,1,0:T(8,128)(2,1)S(1)}, bf16[3,288,128]{2,1,0:T(8,128)(2,1)S(1)}, u32[]{:S(2)}, u32[]{:S(2)}) collective-permute-start(bf16[3,288,128]{2,1,0:T(8,128)(2,1)S(1)} %get-tuple-element.61), channel_id=1, source_target_pairs={{0,127},{1,2},{2,1},{3,4},{4,3},{5,6},{6,5},{7,8},{8,7},{9,10},{10... | collective-permute-start | bytes 663560 | tf_op jit(solution)/shard_map/ppermute | solution.py:776
  23.4 0.0 collective-permute-done.off_ref
  23.4 0.0 collective-permute-start.4
  23.4 0.0 collective-permute-done.1.on_ref
  23.4 2.4 %near.1 = (f32[4,720,128]{2,1,0:T(8,128)S(1)}, f32[4,720,128]{2,1,0:T(8,128)S(1)}, f32[4,720,128]{2,1,0:T(8,128)S(1)}, f32[4,720,128]{2,1,0:T(8,128)S(1)}, f32[4...) custom-call(f32[4,720,128]{2,1,0:T(8,128)S(1)} %get-tuple-element.36, ...), custom_call_target="tpu_custom_call" | custom-call | flops 6039797760 | bytes 13148160 | tf_op jit(solution)/shard_map/near/pallas_call | solution.py:801
  25.7 1.4 %collective-permute-done.5.off_ref = bf16[4,432,128]{2,1,0:T(8,128)(2,1)S(1)} collective-permute-done((bf16[4,432,128]{2,1,0:T(8,128)(2,1)S(1)}, bf16[4,432,128]{2,1,0:T(8,128)(2,1)S(1)}, u32[]{:S(2)}, u32[]{:S(2)}) %collective-permute-start.5) | collective-permute-done | bytes 442400 | tf_op jit(solution)/shard_map/ppermute | solution.py:776
  27.2 0.0 collective-permute-done.6.on_ref
  27.2 2.5 %advance.2 = (f32[4,432,128]{2,1,0:T(8,128)S(1)}, bf16[4,720,128]{2,1,0:T(8,128)(2,1)}) custom-call(f32[4,720,128]{2,1,0:T(8,128)S(1)} %get-tuple-element.56.own_ref, f32[4,720,128]{2,1,0:T(8,128)S(1)} %get-tuple-element.57.near_ref, f32[4,720,128]{2,1,0:T(8,128)S(1)} %get-tuple-element.58.near_add_ref, f32[4,720,128]{2,1,0:T(8,128)S(1)} %get-tuple-element.59.own_force_ref, ...), custom_call_target="tpu_custom_call" | custom-call | flops 5662310400 | bytes 20152320 | tf_op jit(solution)/shard_map/advance/pallas_call | solution.py:801
  29.7 0.4 %collective-permute-done.3.off_ref = bf16[3,288,128]{2,1,0:T(8,128)(2,1)S(1)} collective-permute-done((bf16[3,288,128]{2,1,0:T(8,128)(2,1)S(1)}, bf16[3,288,128]{2,1,0:T(8,128)(2,1)S(1)}, u32[]{:S(2)}, u32[]{:S(2)}) %collective-permute-start.3) | collective-permute-done | bytes 221216 | tf_op jit(solution)/shard_map/ppermute | solution.py:776
  30.1 0.0 collective-permute-done.4.on_ref
  30.1 2.4 %advance.3 = f32[4,720,128]{2,1,0:T(8,128)} custom-call(f32[4,720,128]{2,1,0:T(8,128)S(1)} %get-tuple-element.56.own_ref, f32[4,720,128]{2,1,0:T(8,128)S(1)} %get-tuple-element.57.near_ref, f32[4,720,128]{2,1,0:T(8,128)S(1)} %get-tuple-element.58.near_add_ref, f32[4,720,128]{2,1,0:T(8,128)S(1)} %get-tuple-element.59.own_force_ref, ...), custom_call_target="tpu_custom_call" | custom-call | flops 3774873600 | bytes 20152320 | tf_op jit(solution)/shard_map/advance/pallas_call | solution.py:801
Async XLA Ops:
  0.6 10.5 %copy-start.1 = (bf16[256,256]{1,0:T(8,128)(2,1)S(1)}, bf16[256,256]{1,0:T(8,128)(2,1)}, u32[]{:S(2)}) copy-start(bf16[256,256]{1,0:T(8,128)(2,1)} %constant.2.clone.slope_ref) | copy-start | bytes 393220
  0.6 10.5 %copy-start = (s32[128]{0:T(128)S(1)}, s32[128]{0:T(128)}, u32[]{:S(2)}) copy-start(s32[128]{0:T(128)} %param.11) | copy-start | bytes 1540
  2.6 10.1 %collective-permute-start.2 = (bf16[368,128]{1,0:T(8,128)(2,1)S(1)}, bf16[368,128]{1,0:T(8,128)(2,1)S(1)}, u32[]{:S(2)}, u32[]{:S(2)}) collective-permute-start(bf16[368,128]{1,0:T(8,128)(2,1)S(1)} %get-tuple-element.42), channel_id=1, source_target_pairs={{0,64},{1,65},{2,66},{3,67},{4,68},{5,69},{6,70},{7,71},{8,72},{9,... | collective-permute-start | bytes 282632 | tf_op jit(solution)/shard_map/ppermute | solution.py:838
  6.6 16.7 %collective-permute-start = (bf16[3,784,128]{2,1,0:T(8,128)(2,1)S(1)}, bf16[3,784,128]{2,1,0:T(8,128)(2,1)S(1)}, u32[]{:S(2)}, u32[]{:S(2)}) collective-permute-start(bf16[3,784,128]{2,1,0:T(8,128)(2,1)S(1)} %get-tuple-element.39), channel_id=1, source_target_pairs={{0,127},{1,2},{2,1},{3,4},{4,3},{5,6},{6,5},{7,8},{8,7},{9,10},{10... | collective-permute-start | bytes 1806344 | tf_op jit(solution)/shard_map/ppermute | solution.py:776
  11.2 12.2 %collective-permute-start.1 = (bf16[3,784,128]{2,1,0:T(8,128)(2,1)S(1)}, bf16[3,784,128]{2,1,0:T(8,128)(2,1)S(1)}, u32[]{:S(2)}, u32[]{:S(2)}) collective-permute-start(bf16[3,784,128]{2,1,0:T(8,128)(2,1)S(1)} %get-tuple-element.40), channel_id=1, source_target_pairs={{0,1},{1,0},{2,3},{3,2},{4,5},{5,4},{6,7},{7,6},{8,9},{9,8},{10,11... | collective-permute-start | bytes 1806344 | tf_op jit(solution)/shard_map/ppermute | solution.py:775
  13.9 13.2 %collective-permute-start.5 = (bf16[4,432,128]{2,1,0:T(8,128)(2,1)S(1)}, bf16[4,432,128]{2,1,0:T(8,128)(2,1)S(1)}, u32[]{:S(2)}, u32[]{:S(2)}) collective-permute-start(bf16[4,432,128]{2,1,0:T(8,128)(2,1)S(1)} %get-tuple-element.66), channel_id=1, source_target_pairs={{0,127},{1,2},{2,1},{3,4},{4,3},{5,6},{6,5},{7,8},{8,7},{9,10},{10... | collective-permute-start | bytes 1327112 | tf_op jit(solution)/shard_map/ppermute | solution.py:776
  17.1 10.1 %collective-permute-start.6 = (bf16[4,432,128]{2,1,0:T(8,128)(2,1)S(1)}, bf16[4,432,128]{2,1,0:T(8,128)(2,1)S(1)}, u32[]{:S(2)}, u32[]{:S(2)}) collective-permute-start(bf16[4,432,128]{2,1,0:T(8,128)(2,1)S(1)} %get-tuple-element.67), channel_id=1, source_target_pairs={{0,1},{1,0},{2,3},{3,2},{4,5},{5,4},{6,7},{7,6},{8,9},{9,8},{10,11... | collective-permute-start | bytes 1327112 | tf_op jit(solution)/shard_map/ppermute | solution.py:775
  19.2 10.9 %collective-permute-start.3 = (bf16[3,288,128]{2,1,0:T(8,128)(2,1)S(1)}, bf16[3,288,128]{2,1,0:T(8,128)(2,1)S(1)}, u32[]{:S(2)}, u32[]{:S(2)}) collective-permute-start(bf16[3,288,128]{2,1,0:T(8,128)(2,1)S(1)} %get-tuple-element.61), channel_id=1, source_target_pairs={{0,127},{1,2},{2,1},{3,4},{4,3},{5,6},{6,5},{7,8},{8,7},{9,10},{10... | collective-permute-start | bytes 663560 | tf_op jit(solution)/shard_map/ppermute | solution.py:776
  23.4 6.7 %collective-permute-start.4 = (bf16[3,288,128]{2,1,0:T(8,128)(2,1)S(1)}, bf16[3,288,128]{2,1,0:T(8,128)(2,1)S(1)}, u32[]{:S(2)}, u32[]{:S(2)}) collective-permute-start(bf16[3,288,128]{2,1,0:T(8,128)(2,1)S(1)} %get-tuple-element.62), channel_id=1, source_target_pairs={{0,1},{1,0},{2,3},{3,2},{4,5},{5,4},{6,7},{7,6},{8,9},{9,8},{10,11... | collective-permute-start | bytes 663560 | tf_op jit(solution)/shard_map/ppermute | solution.py:775

commit v12 on v11

--- a/solution.py
+++ b/solution.py
@@ -429,6 +429,8 @@
         both = [jnp.concatenate(high[k : k + 2], axis=1) for k in (0, 2)]
         few = jnp.dot(jnp.concatenate(both, axis=0), self.keep, preferred_element_type=jnp.float32)
         yield
+        if self.far is None:
+            self.far = self.unpack()
         size = pairs[0].shape[0]
         lev = size // 2
         blank = jnp.zeros((LANES - lev, 2 * LANES), jnp.float32)
@@ -438,9 +440,10 @@
             part = jnp.concatenate([part[:lev], part[lev:]], axis=1)
             column = jnp.concatenate([part, blank], axis=0).astype(jnp.bfloat16)
             products.append(jnp.dot(self.far, column, preferred_element_type=jnp.float32))
+            if k:
+                rows.append(as_rows(chosen_rows(products[0], self.far_group)))
             yield
-        for k in range(2):
-            rows.append(as_rows(chosen_rows(products[k], self.far_group)))
+        rows.append(as_rows(chosen_rows(products[1], self.far_group)))
         rows = jnp.concatenate(rows, axis=0).astype(jnp.bfloat16)
         wide = jnp.dot(rows, self.spread, preferred_element_type=jnp.float32)
         yield
@@ -522,9 +525,14 @@
     far_ref,
 ):
     physics = Physics(slot_ref)
-    matrices = unpacked_matrices(packed_ref[...].astype(jnp.float32)).astype(jnp.bfloat16)
-    far_ref[...] = matrices
-    physics.take_far(matrices, keep_ref, spread_ref, far_group_ref)
+    physics.take_far(None, keep_ref, spread_ref, far_group_ref)
+
+    def unpack():
+        matrices = unpacked_matrices(packed_ref[...].astype(jnp.float32)).astype(jnp.bfloat16)
+        far_ref[...] = matrices
+        return matrices
+
+    physics.unpack = unpack
 
     def stages(at, here_at, _):
         far = yield from physics.far_products([state_ref[k, at] for k in range(PARTS)])

time: 32.8 us -> 32.8 us (level)
  no operation moved by 1% of the time
where the time goes in v12:
time: 32.8 us; the launch traced here: 32.6 us
  starting transfers between devices  15.9 us (48%)
  Pallas kernels  14 us (43%)
  waiting for transfers between devices  1.81 us (6%)
  between operations  0.87 us (3%)
    pallas_call x7, Pallas kernels, call(): pl.pallas_call(body, out_shape=outs, compiler_params=params, cost_estimat...  14 us
    ppermute x3, starting transfers between devices, exchanged(): return (lax.ppermute(off, AXES, across), on)  11.8 us
    ppermute x1, starting transfers between devices, per_device(): lax.ppermute(packed, AXES, [(i, i ^ devices // 2) for i in range(devices)])  4.04 us
    ppermute x3, waiting for transfers between devices, exchanged(): return (lax.ppermute(off, AXES, across), on)  1.8 us
  transfers between devices with their start and end apart: 7, of which 2 were waited for; matrix products, arithmetic and copies ran while one was open for 0% of the time, Pallas kernels for 30%

profile of v12, /device:TPU:0, one launch (start us, length us, event | category | flops | bytes accessed | tf_op | source)
XLA Modules:
  0.0 32.6 jit_solution(13719451827124603727)
XLA Ops:
  0.6 0.0 copy-start.1
  0.6 0.0 copy-start
  0.7 1.9 %pack.1 = (bf16[576,128]{1,0:T(8,128)(2,1)S(1)}, bf16[368,128]{1,0:T(8,128)(2,1)S(1)}, bf16[3,784,128]{2,1,0:T(8,128)(2,1)S(1)}, bf16[3,784,128]{2,1,0:T(8,128)(...) custom-call(f32[8,72,72]{2,1,0:T(8,128)} %inverse_hbm.1, ...), custom_call_target="tpu_custom_call" | custom-call | flops 754974720 | bytes 4903424 | tf_op jit(solution)/shard_map/pack/pallas_call | solution.py:809
  2.6 4.0 %collective-permute-start.2 = (bf16[368,128]{1,0:T(8,128)(2,1)S(1)}, bf16[368,128]{1,0:T(8,128)(2,1)S(1)}, u32[]{:S(2)}, u32[]{:S(2)}) collective-permute-start(bf16[368,128]{1,0:T(8,128)(2,1)S(1)} %get-tuple-element.42), channel_id=1, source_target_pairs={{0,64},{1,65},{2,66},{3,67},{4,68},{5,69},{6,70},{7,71},{8,72},{9,... | collective-permute-start | bytes 282632 | tf_op jit(solution)/shard_map/ppermute | solution.py:846
  6.6 4.5 %collective-permute-start = (bf16[3,784,128]{2,1,0:T(8,128)(2,1)S(1)}, bf16[3,784,128]{2,1,0:T(8,128)(2,1)S(1)}, u32[]{:S(2)}, u32[]{:S(2)}) collective-permute-start(bf16[3,784,128]{2,1,0:T(8,128)(2,1)S(1)} %get-tuple-element.39), channel_id=1, source_target_pairs={{0,127},{1,2},{2,1},{3,4},{4,3},{5,6},{6,5},{7,8},{8,7},{9,10},{10... | collective-permute-start | bytes 1806344 | tf_op jit(solution)/shard_map/ppermute | solution.py:784
  11.2 0.0 collective-permute-start.1
  11.2 0.0 copy-done.1
  11.2 0.0 copy-done
  11.2 1.5 %own.1 = (f32[4,432,128]{2,1,0:T(8,128)S(1)}, f32[4,432,128]{2,1,0:T(8,128)S(1)}, bf16[4,432,128]{2,1,0:T(8,128)(2,1)S(1)}, bf16[256,128]{1,0:T(8,128)(2,1)S(1)}...) custom-call(f32[4,720,128]{2,1,0:T(8,128)S(1)} %get-tuple-element.36.state_ref, ...), custom_call_target="tpu_custom_call" | custom-call | flops 3397386240 | bytes 5137408 | tf_op jit(solution)/shard_map/own/pallas_call | solution.py:809
  12.7 0.0 collective-permute-done.2.packed_ref
  12.7 1.2 %far.1 = (bf16[4,432,128]{2,1,0:T(8,128)(2,1)S(1)}, f32[4,432,128]{2,1,0:T(8,128)S(1)}, bf16[4,432,128]{2,1,0:T(8,128)(2,1)S(1)}, bf16[4,432,128]{2,1,0:T(8,128)(2,1)S(1)}, bf16[576,128]{1,0:T(8,128)(2,1)S(1)}) custom-call(f32[4,720,128]{2,1,0:T(8,128)S(1)} %get-tuple-element.36.state_ref, bf16[4,720,128]{2,1,0:T(8,128)(2,1)S(1)} %get-tuple-element.41.prev_ref, ...), custom_call_target="tpu_custom_call" | custom-call | flops 5662310400 | bytes 8422400 | tf_op jit(solution)/shard_map/far/pallas_call | solution.py:809
  13.9 3.2 %collective-permute-start.5 = (bf16[4,432,128]{2,1,0:T(8,128)(2,1)S(1)}, bf16[4,432,128]{2,1,0:T(8,128)(2,1)S(1)}, u32[]{:S(2)}, u32[]{:S(2)}) collective-permute-start(bf16[4,432,128]{2,1,0:T(8,128)(2,1)S(1)} %get-tuple-element.66), channel_id=1, source_target_pairs={{0,127},{1,2},{2,1},{3,4},{4,3},{5,6},{6,5},{7,8},{8,7},{9,10},{10... | collective-permute-start | bytes 1327112 | tf_op jit(solution)/shard_map/ppermute | solution.py:784
  17.1 0.0 collective-permute-start.6
  17.1 2.1 %physics.1 = (bf16[4,288,128]{2,1,0:T(8,128)(2,1)S(1)}, f32[4,288,128]{2,1,0:T(8,128)S(1)}, bf16[3,288,128]{2,1,0:T(8,128)(2,1)S(1)}, bf16[3,288,128]{2,1,0:T(8,128)(2,1)S(1)}, bf16[4,288,128]{2,1,0:T(8,128)(2,1)S(1)}) custom-call(f32[4,720,128]{2,1,0:T(8,128)S(1)} %get-tuple-element.36.state_ref, bf16[4,720,128]{2,1,0:T(8,128)(2,1)S(1)} %get-tuple-element.41.prev_ref, ...), custom_call_target="tpu_custom_call" | custom-call | flops 3774873600 | bytes 5702656 | tf_op jit(solution)/shard_map/physics/pallas_call | solution.py:809
  19.2 4.1 %collective-permute-start.3 = (bf16[3,288,128]{2,1,0:T(8,128)(2,1)S(1)}, bf16[3,288,128]{2,1,0:T(8,128)(2,1)S(1)}, u32[]{:S(2)}, u32[]{:S(2)}) collective-permute-start(bf16[3,288,128]{2,1,0:T(8,128)(2,1)S(1)} %get-tuple-element.61), channel_id=1, source_target_pairs={{0,127},{1,2},{2,1},{3,4},{4,3},{5,6},{6,5},{7,8},{8,7},{9,10},{10... | collective-permute-start | bytes 663560 | tf_op jit(solution)/shard_map/ppermute | solution.py:784
  23.4 0.0 collective-permute-done.off_ref
  23.4 0.0 collective-permute-start.4
  23.4 0.0 collective-permute-done.1.on_ref
  23.4 2.4 %near.1 = (f32[4,720,128]{2,1,0:T(8,128)S(1)}, f32[4,720,128]{2,1,0:T(8,128)S(1)}, f32[4,720,128]{2,1,0:T(8,128)S(1)}, f32[4,720,128]{2,1,0:T(8,128)S(1)}, f32[4...) custom-call(f32[4,720,128]{2,1,0:T(8,128)S(1)} %get-tuple-element.36, ...), custom_call_target="tpu_custom_call" | custom-call | flops 6039797760 | bytes 13148160 | tf_op jit(solution)/shard_map/near/pallas_call | solution.py:809
  25.7 1.4 %collective-permute-done.5.off_ref = bf16[4,432,128]{2,1,0:T(8,128)(2,1)S(1)} collective-permute-done((bf16[4,432,128]{2,1,0:T(8,128)(2,1)S(1)}, bf16[4,432,128]{2,1,0:T(8,128)(2,1)S(1)}, u32[]{:S(2)}, u32[]{:S(2)}) %collective-permute-start.5) | collective-permute-done | bytes 442400 | tf_op jit(solution)/shard_map/ppermute | solution.py:784
  27.2 0.0 collective-permute-done.6.on_ref
  27.2 2.5 %advance.2 = (f32[4,432,128]{2,1,0:T(8,128)S(1)}, bf16[4,720,128]{2,1,0:T(8,128)(2,1)}) custom-call(f32[4,720,128]{2,1,0:T(8,128)S(1)} %get-tuple-element.56.own_ref, f32[4,720,128]{2,1,0:T(8,128)S(1)} %get-tuple-element.57.near_ref, f32[4,720,128]{2,1,0:T(8,128)S(1)} %get-tuple-element.58.near_add_ref, f32[4,720,128]{2,1,0:T(8,128)S(1)} %get-tuple-element.59.own_force_ref, ...), custom_call_target="tpu_custom_call" | custom-call | flops 5662310400 | bytes 20152320 | tf_op jit(solution)/shard_map/advance/pallas_call | solution.py:809
  29.7 0.4 %collective-permute-done.3.off_ref = bf16[3,288,128]{2,1,0:T(8,128)(2,1)S(1)} collective-permute-done((bf16[3,288,128]{2,1,0:T(8,128)(2,1)S(1)}, bf16[3,288,128]{2,1,0:T(8,128)(2,1)S(1)}, u32[]{:S(2)}, u32[]{:S(2)}) %collective-permute-start.3) | collective-permute-done | bytes 221216 | tf_op jit(solution)/shard_map/ppermute | solution.py:784
  30.1 0.0 collective-permute-done.4.on_ref
  30.1 2.4 %advance.3 = f32[4,720,128]{2,1,0:T(8,128)} custom-call(f32[4,720,128]{2,1,0:T(8,128)S(1)} %get-tuple-element.56.own_ref, f32[4,720,128]{2,1,0:T(8,128)S(1)} %get-tuple-element.57.near_ref, f32[4,720,128]{2,1,0:T(8,128)S(1)} %get-tuple-element.58.near_add_ref, f32[4,720,128]{2,1,0:T(8,128)S(1)} %get-tuple-element.59.own_force_ref, ...), custom_call_target="tpu_custom_call" | custom-call | flops 3774873600 | bytes 20152320 | tf_op jit(solution)/shard_map/advance/pallas_call | solution.py:809
Async XLA Ops:
  0.6 10.5 %copy-start.1 = (bf16[256,256]{1,0:T(8,128)(2,1)S(1)}, bf16[256,256]{1,0:T(8,128)(2,1)}, u32[]{:S(2)}) copy-start(bf16[256,256]{1,0:T(8,128)(2,1)} %constant.2.clone.slope_ref) | copy-start | bytes 393220
  0.6 10.5 %copy-start = (s32[128]{0:T(128)S(1)}, s32[128]{0:T(128)}, u32[]{:S(2)}) copy-start(s32[128]{0:T(128)} %param.11) | copy-start | bytes 1540
  2.6 10.1 %collective-permute-start.2 = (bf16[368,128]{1,0:T(8,128)(2,1)S(1)}, bf16[368,128]{1,0:T(8,128)(2,1)S(1)}, u32[]{:S(2)}, u32[]{:S(2)}) collective-permute-start(bf16[368,128]{1,0:T(8,128)(2,1)S(1)} %get-tuple-element.42), channel_id=1, source_target_pairs={{0,64},{1,65},{2,66},{3,67},{4,68},{5,69},{6,70},{7,71},{8,72},{9,... | collective-permute-start | bytes 282632 | tf_op jit(solution)/shard_map/ppermute | solution.py:846
  6.6 16.7 %collective-permute-start = (bf16[3,784,128]{2,1,0:T(8,128)(2,1)S(1)}, bf16[3,784,128]{2,1,0:T(8,128)(2,1)S(1)}, u32[]{:S(2)}, u32[]{:S(2)}) collective-permute-start(bf16[3,784,128]{2,1,0:T(8,128)(2,1)S(1)} %get-tuple-element.39), channel_id=1, source_target_pairs={{0,127},{1,2},{2,1},{3,4},{4,3},{5,6},{6,5},{7,8},{8,7},{9,10},{10... | collective-permute-start | bytes 1806344 | tf_op jit(solution)/shard_map/ppermute | solution.py:784
  11.2 12.2 %collective-permute-start.1 = (bf16[3,784,128]{2,1,0:T(8,128)(2,1)S(1)}, bf16[3,784,128]{2,1,0:T(8,128)(2,1)S(1)}, u32[]{:S(2)}, u32[]{:S(2)}) collective-permute-start(bf16[3,784,128]{2,1,0:T(8,128)(2,1)S(1)} %get-tuple-element.40), channel_id=1, source_target_pairs={{0,1},{1,0},{2,3},{3,2},{4,5},{5,4},{6,7},{7,6},{8,9},{9,8},{10,11... | collective-permute-start | bytes 1806344 | tf_op jit(solution)/shard_map/ppermute | solution.py:783
  13.9 13.2 %collective-permute-start.5 = (bf16[4,432,128]{2,1,0:T(8,128)(2,1)S(1)}, bf16[4,432,128]{2,1,0:T(8,128)(2,1)S(1)}, u32[]{:S(2)}, u32[]{:S(2)}) collective-permute-start(bf16[4,432,128]{2,1,0:T(8,128)(2,1)S(1)} %get-tuple-element.66), channel_id=1, source_target_pairs={{0,127},{1,2},{2,1},{3,4},{4,3},{5,6},{6,5},{7,8},{8,7},{9,10},{10... | collective-permute-start | bytes 1327112 | tf_op jit(solution)/shard_map/ppermute | solution.py:784
  17.1 10.1 %collective-permute-start.6 = (bf16[4,432,128]{2,1,0:T(8,128)(2,1)S(1)}, bf16[4,432,128]{2,1,0:T(8,128)(2,1)S(1)}, u32[]{:S(2)}, u32[]{:S(2)}) collective-permute-start(bf16[4,432,128]{2,1,0:T(8,128)(2,1)S(1)} %get-tuple-element.67), channel_id=1, source_target_pairs={{0,1},{1,0},{2,3},{3,2},{4,5},{5,4},{6,7},{7,6},{8,9},{9,8},{10,11... | collective-permute-start | bytes 1327112 | tf_op jit(solution)/shard_map/ppermute | solution.py:783
  19.2 10.9 %collective-permute-start.3 = (bf16[3,288,128]{2,1,0:T(8,128)(2,1)S(1)}, bf16[3,288,128]{2,1,0:T(8,128)(2,1)S(1)}, u32[]{:S(2)}, u32[]{:S(2)}) collective-permute-start(bf16[3,288,128]{2,1,0:T(8,128)(2,1)S(1)} %get-tuple-element.61), channel_id=1, source_target_pairs={{0,127},{1,2},{2,1},{3,4},{4,3},{5,6},{6,5},{7,8},{8,7},{9,10},{10... | collective-permute-start | bytes 663560 | tf_op jit(solution)/shard_map/ppermute | solution.py:784
  23.4 6.7 %collective-permute-start.4 = (bf16[3,288,128]{2,1,0:T(8,128)(2,1)S(1)}, bf16[3,288,128]{2,1,0:T(8,128)(2,1)S(1)}, u32[]{:S(2)}, u32[]{:S(2)}) collective-permute-start(bf16[3,288,128]{2,1,0:T(8,128)(2,1)S(1)} %get-tuple-element.62), channel_id=1, source_target_pairs={{0,1},{1,0},{2,3},{3,2},{4,5},{5,4},{6,7},{7,6},{8,9},{9,8},{10,11... | collective-permute-start | bytes 663560 | tf_op jit(solution)/shard_map/ppermute | solution.py:783
